TPU v7x, 32 devices: a whole 2x2x4 slice. The times are simulated.
32 devices in a mesh: fsdp: 8 (over y, x, core), tp: 4 (over z).
Axes of the slice: x: 2, y: 2, z: 4, core: 2. Of those that a mesh axis runs over, the one named last changes fastest.
Arguments:
- activations: bfloat16 [8, 2048, 1152], P('fsdp', 'tp'), may hold values from -6 to 6
- lengths: int32 [8, 3], P('fsdp'), may hold values from 100 to 1024, as said below
- cotangent: bfloat16 [8, 2048, 1152], P('fsdp', 'tp'), may hold values from -6 to 6
- ln1_gain: float32 [1, 1152], P(None, 'fsdp'), may hold values from 0.5 to 1.5
- ln1_bias: float32 [1, 1152], P(None, 'fsdp'), may hold values from -2 to 2
- query_weight: bfloat16 [1, 1152, 1152], P(None, 'fsdp', 'tp'), may hold values from -0.1875 to 0.1875
- query_bias: float32 [1, 1152], P(None, 'tp'), may hold values from -3 to 3
- key_weight: bfloat16 [1, 1152, 1152], P(None, 'fsdp', 'tp'), may hold values from -0.1875 to 0.1875
- value_weight: bfloat16 [1, 1152, 1152], P(None, 'fsdp', 'tp'), may hold values from -0.1875 to 0.1875
- value_bias: float32 [1, 1152], P(None, 'tp'), may hold values from -3 to 3
- out_weight: bfloat16 [1, 1152, 1152], P(None, 'fsdp', 'tp'), may hold values from -0.75 to 0.75
- out_bias: float32 [1, 1152], P(None, 'fsdp'), may hold values from -2 to 2
- ln2_gain: float32 [1, 1152], P(None, 'fsdp'), may hold values from 0.5 to 1.5
- ln2_bias: float32 [1, 1152], P(None, 'fsdp'), may hold values from -2 to 2
- up_weight: bfloat16 [1, 1152, 4304], P(None, 'fsdp', 'tp'), may hold values from -0.1875 to 0.1875
- up_bias: float32 [1, 4304], P(None, 'tp'), may hold values from -3 to 3
- down_weight: bfloat16 [1, 1152, 4304], P(None, 'fsdp', 'tp'), may hold values from -0.09375 to 0.09375
- down_bias: float32 [1, 1152], P(None, 'fsdp'), may hold values from -2 to 2
Outputs:
- activations_out: bfloat16 [8, 2048, 1152], P('fsdp', 'tp')
- input_grad: float32 [8, 2048, 1152], P('fsdp', 'tp')
- ln1_gain_grad: float32 [1, 1152], P(None, 'fsdp')
- ln1_bias_grad: float32 [1, 1152], P(None, 'fsdp')
- query_weight_grad: float32 [1, 1152, 1152], P(None, 'fsdp', 'tp')
- query_bias_grad: float32 [1, 1152], P(None, 'tp')
- key_weight_grad: float32 [1, 1152, 1152], P(None, 'fsdp', 'tp')
- value_weight_grad: float32 [1, 1152, 1152], P(None, 'fsdp', 'tp')
- value_bias_grad: float32 [1, 1152], P(None, 'tp')
- out_weight_grad: float32 [1, 1152, 1152], P(None, 'fsdp', 'tp')
- out_bias_grad: float32 [1, 1152], P(None, 'fsdp')
- ln2_gain_grad: float32 [1, 1152], P(None, 'fsdp')
- ln2_bias_grad: float32 [1, 1152], P(None, 'fsdp')
- up_weight_grad: float32 [1, 1152, 4304], P(None, 'fsdp', 'tp')
- up_bias_grad: float32 [1, 4304], P(None, 'tp')
- down_weight_grad: float32 [1, 1152, 4304], P(None, 'fsdp', 'tp')
- down_bias_grad: float32 [1, 1152], P(None, 'fsdp')
Inputs may be any that keep to these rules, and one draw needn't show every extreme that they name: `lengths`: each row holds 3 pictures laid end to end from slot 0, each of 100 to 1024 patches and together at most 2048; the slots after them are padding; some row has a picture of exactly 1024 patches.
All inputs are finite; a program needn't handle non-finite values.
Results may differ from a plain program's by a relative error of at most 0.033.
Values may be sent and summed in bfloat16 or wider, within the bound.
No kernel may reach another device: no remote copies, remote signals or barrier semaphores. Data moves between devices by JAX's collectives and lax.ppermute only.
A program may use at most 192 MiB of HBM per device.

v0:
```python
import jax
import jax.numpy as jnp
from jax import lax
from jax.sharding import PartitionSpec as P

HEAD_DIM = 72


def layer_norm(values, gain, shift):
    center = values - jnp.mean(values, axis=-1, keepdims=True)
    spread = jnp.mean(center * center, axis=-1, keepdims=True)
    return center * lax.rsqrt(spread + 1e-06) * gain + shift


def gelu_tanh(values):
    return jax.nn.gelu(values, approximate=True)


def product(form, left, right):
    return jnp.einsum(form, left, right, preferred_element_type=jnp.float32)


def fetch_layer(
    layer_idx,
    ln1_gain,
    ln1_bias,
    query_weight,
    key_weight,
    value_weight,
    out_weight,
    out_bias,
    ln2_gain,
    ln2_bias,
    up_weight,
    down_weight,
    down_bias,
):
    return (
        lax.all_gather(ln1_gain[layer_idx].astype(jnp.bfloat16), "fsdp", axis=0, tiled=True).astype(
            jnp.float32
        ),
        lax.all_gather(ln1_bias[layer_idx].astype(jnp.bfloat16), "fsdp", axis=0, tiled=True).astype(
            jnp.float32
        ),
        lax.all_gather(query_weight[layer_idx], "fsdp", axis=0, tiled=True),
        lax.all_gather(key_weight[layer_idx], "fsdp", axis=0, tiled=True),
        lax.all_gather(value_weight[layer_idx], "fsdp", axis=0, tiled=True),
        lax.all_gather(out_weight[layer_idx], "fsdp", axis=0, tiled=True),
        lax.all_gather(out_bias[layer_idx].astype(jnp.bfloat16), "fsdp", axis=0, tiled=True).astype(
            jnp.float32
        ),
        lax.all_gather(ln2_gain[layer_idx].astype(jnp.bfloat16), "fsdp", axis=0, tiled=True).astype(
            jnp.float32
        ),
        lax.all_gather(ln2_bias[layer_idx].astype(jnp.bfloat16), "fsdp", axis=0, tiled=True).astype(
            jnp.float32
        ),
        lax.all_gather(up_weight[layer_idx], "fsdp", axis=0, tiled=True),
        lax.all_gather(down_weight[layer_idx], "fsdp", axis=0, tiled=True),
        lax.all_gather(
            down_bias[layer_idx].astype(jnp.bfloat16), "fsdp", axis=0, tiled=True
        ).astype(jnp.float32),
    )


def block_scores(query_block, key_heads, seg_block, seg_row, scale):
    scores = product("qhe,khe->hqk", query_block, key_heads) * scale
    return jnp.where((seg_block[:, None] == seg_row[None, :])[None], scores, -1e30)


def attend_rows(queries, keys_all, values_all, segment, heads_here):
    rows_here, seq_len, columns = queries.shape
    head_dim = columns // heads_here
    block = min(512, seq_len)
    blocks = seq_len // block
    scale = head_dim ** (-0.5)

    def one_row(row_items):
        query_row, key_row, value_row, seg_row = row_items
        key_heads = key_row.reshape(seq_len, heads_here, head_dim)
        value_heads = value_row.reshape(seq_len, heads_here, head_dim)
        query_blocks = query_row.reshape(blocks, block, heads_here, head_dim)
        seg_blocks = seg_row.reshape(blocks, block)

        def one_block(block_items):
            query_block, seg_block = block_items
            scores = block_scores(query_block, key_heads, seg_block, seg_row, scale)
            top = jnp.max(scores, axis=-1, keepdims=True)
            exponent = jnp.exp(scores - top)
            total = jnp.sum(exponent, axis=-1, keepdims=True)
            probs = (exponent / total).astype(jnp.bfloat16)
            result = product("hqk,khe->qhe", probs, value_heads)
            return (result, (top + jnp.log(total))[..., 0])

        result, log_total = lax.map(one_block, (query_blocks, seg_blocks))
        return (result.reshape(seq_len, columns), log_total)

    return lax.map(one_row, (queries, keys_all, values_all, segment))


def attend_back(queries, keys_all, values_all, segment, grad_out, log_total, heads_here):
    rows_here, seq_len, columns = queries.shape
    head_dim = columns // heads_here
    block = min(512, seq_len)
    blocks = seq_len // block
    scale = head_dim ** (-0.5)

    def one_row(row_items):
        query_row, key_row, value_row, seg_row, grad_row, lse_row = row_items
        key_heads = key_row.reshape(seq_len, heads_here, head_dim)
        value_heads = value_row.reshape(seq_len, heads_here, head_dim)
        query_blocks = query_row.reshape(blocks, block, heads_here, head_dim)
        grad_blocks = grad_row.reshape(blocks, block, heads_here, head_dim)
        seg_blocks = seg_row.reshape(blocks, block)

        def one_block(carry, block_items):
            key_acc, value_acc = carry
            query_block, grad_block, lse_block, seg_block = block_items
            scores = block_scores(query_block, key_heads, seg_block, seg_row, scale)
            probs = jnp.exp(scores - lse_block[..., None])
            dprobs = product("qhe,khe->hqk", grad_block, value_heads)
            dscores = probs * (dprobs - jnp.sum(probs * dprobs, axis=-1, keepdims=True))
            dscores = dscores.astype(jnp.bfloat16)
            query_grad = product("hqk,khe->qhe", dscores, key_heads) * scale
            key_acc = key_acc + product("hqk,qhe->khe", dscores, query_block) * scale
            value_acc = value_acc + product("hqk,qhe->khe", probs.astype(jnp.bfloat16), grad_block)
            return ((key_acc, value_acc), query_grad)

        zeros = jnp.zeros((seq_len, heads_here, head_dim), jnp.float32)
        (key_acc, value_acc), query_grad = lax.scan(
            one_block, (zeros, zeros), (query_blocks, grad_blocks, lse_row, seg_blocks)
        )
        return (
            query_grad.reshape(seq_len, columns),
            key_acc.reshape(seq_len, columns),
            value_acc.reshape(seq_len, columns),
        )

    return lax.map(one_row, (queries, keys_all, values_all, segment, grad_out, log_total))


def local(
    activations,
    lengths,
    cotangent,
    ln1_gain,
    ln1_bias,
    query_weight,
    query_bias,
    key_weight,
    value_weight,
    value_bias,
    out_weight,
    out_bias,
    ln2_gain,
    ln2_bias,
    up_weight,
    up_bias,
    down_weight,
    down_bias,
):
    tp_count = lax.axis_size("tp")
    rows_here, local_len, model_width = activations.shape
    seq_len = local_len * tp_count
    heads_here = query_weight.shape[2] // HEAD_DIM
    layer_count = query_weight.shape[0]
    pic_count = lengths.shape[1]
    positions = jnp.arange(seq_len, dtype=jnp.int32)
    ends = jnp.cumsum(lengths, axis=1)
    segment = jnp.sum((positions[None, :, None] >= ends[:, None, :]).astype(jnp.int32), axis=2)
    valid_full = (segment < pic_count).astype(jnp.float32)
    valid_local = lax.dynamic_slice_in_dim(
        valid_full, lax.axis_index("tp") * local_len, local_len, 1
    )
    valid_mask = valid_full[:, :, None].astype(jnp.bfloat16)

    def fetch(layer_idx):
        return fetch_layer(
            layer_idx,
            ln1_gain,
            ln1_bias,
            query_weight,
            key_weight,
            value_weight,
            out_weight,
            out_bias,
            ln2_gain,
            ln2_bias,
            up_weight,
            down_weight,
            down_bias,
        )

    current = activations.astype(jnp.float32)
    layer_idx = 0
    fetched = fetch(layer_idx)
    (
        gain_one,
        shift_one,
        query_full,
        key_full,
        value_full,
        out_full,
        out_shift,
        gain_two,
        shift_two,
        up_full,
        down_full,
        down_shift,
    ) = fetched
    normed = layer_norm(current, gain_one, shift_one).astype(jnp.bfloat16)
    normed_all = lax.all_gather(normed, "tp", axis=1, tiled=True)
    queries = (product("rsd,dc->rsc", normed_all, query_full) + query_bias[layer_idx]).astype(
        jnp.bfloat16
    )
    keys_all = product("rsd,dc->rsc", normed_all, key_full).astype(jnp.bfloat16)
    values_all = (product("rsd,dc->rsc", normed_all, value_full) + value_bias[layer_idx]).astype(
        jnp.bfloat16
    )
    attended, log_total = attend_rows(queries, keys_all, values_all, segment, heads_here)
    attended = (attended * valid_full[:, :, None]).astype(jnp.bfloat16)
    partial_out = product("rsc,dc->rsd", attended, out_full)
    branch = (
        lax.psum_scatter(
            partial_out.astype(jnp.bfloat16), "tp", scatter_dimension=1, tiled=True
        ).astype(jnp.float32)
        + out_shift
    )
    middle = current + branch
    normed_two = layer_norm(middle, gain_two, shift_two).astype(jnp.bfloat16)
    mlp_input = lax.all_gather(normed_two, "tp", axis=1, tiled=True)
    hidden = product("rsd,df->rsf", mlp_input, up_full) + up_bias[layer_idx]
    active = gelu_tanh(hidden).astype(jnp.bfloat16)
    mixed = (
        lax.psum_scatter(
            product("rsf,df->rsd", active, down_full).astype(jnp.bfloat16),
            "tp",
            scatter_dimension=1,
            tiled=True,
        ).astype(jnp.float32)
        + down_shift
    )
    unit_weights = (up_full, down_full)
    kept_weights = None
    saved = [
        (
            current,
            middle,
            normed_all,
            queries,
            keys_all,
            values_all,
            log_total,
            attended,
            mlp_input,
            hidden,
            active,
            unit_weights,
            kept_weights,
        )
    ]
    current = (middle + mixed) * valid_local[:, :, None]
    activations_out = current.astype(jnp.bfloat16)
    grad_now = cotangent.astype(jnp.float32)
    collected = [None] * layer_count
    for layer_idx in reversed(range(layer_count)):
        (
            layer_input,
            middle,
            normed_all,
            queries,
            keys_all,
            values_all,
            log_total,
            attended,
            mlp_input,
            hidden,
            active,
            unit_weights,
            kept_weights,
        ) = saved[layer_idx]
        fetched = fetch(layer_idx)
        (
            gain_one,
            shift_one,
            query_full,
            key_full,
            value_full,
            out_full,
            out_shift,
            gain_two,
            shift_two,
            up_full,
            down_full,
            down_shift,
        ) = fetched
        grad_two = grad_now * valid_local[:, :, None]
        grad_mixed = grad_two.astype(jnp.bfloat16)
        down_bias_part = jnp.sum(grad_mixed, axis=(0, 1), dtype=jnp.float32)
        gelu_value, gelu_pull = jax.vjp(gelu_tanh, hidden)
        grad_mixed_all = lax.all_gather(grad_mixed, "tp", axis=1, tiled=True)
        grad_active = product("rsd,df->rsf", grad_mixed_all, down_full)
        grad_hidden = gelu_pull(grad_active)[0].astype(jnp.bfloat16)
        up_grad = product("rsd,rsf->df", mlp_input, grad_hidden)
        down_grad = product("rsd,rsf->df", grad_mixed_all, active)
        up_bias_part = jnp.sum(grad_hidden, axis=(0, 1), dtype=jnp.float32)
        grad_normed_two = lax.psum_scatter(
            product("rsf,df->rsd", grad_hidden, up_full).astype(jnp.bfloat16),
            "tp",
            scatter_dimension=1,
            tiled=True,
        ).astype(jnp.float32)
        norm_value, norm_two_pull = jax.vjp(layer_norm, middle, gain_two, shift_two)
        grad_middle_norm, gain_two_grad, shift_two_grad = norm_two_pull(grad_normed_two)
        grad_middle = grad_two + grad_middle_norm
        grad_branch = grad_middle.astype(jnp.bfloat16)
        out_bias_part = jnp.sum(grad_branch, axis=(0, 1), dtype=jnp.float32)
        grad_branch_all = lax.all_gather(grad_branch, "tp", axis=1, tiled=True)
        out_grad = product("rsd,rsc->dc", grad_branch_all, attended)
        grad_attended = (
            product("rsd,dc->rsc", grad_branch_all, out_full).astype(jnp.bfloat16) * valid_mask
        )
        query_grad, key_grad, value_grad = attend_back(
            queries, keys_all, values_all, segment, grad_attended, log_total, heads_here
        )
        query_grad = query_grad.astype(jnp.bfloat16)
        key_grad = key_grad.astype(jnp.bfloat16)
        value_grad = value_grad.astype(jnp.bfloat16)
        query_weight_grad = product("rsd,rsc->dc", normed_all, query_grad)
        key_weight_grad = product("rsd,rsc->dc", normed_all, key_grad)
        value_weight_grad = product("rsd,rsc->dc", normed_all, value_grad)
        query_bias_part = jnp.sum(query_grad, axis=(0, 1), dtype=jnp.float32)
        value_bias_part = jnp.sum(value_grad, axis=(0, 1), dtype=jnp.float32)
        grad_normed_part = (
            product("rsc,dc->rsd", query_grad, query_full)
            + product("rsc,dc->rsd", key_grad, key_full)
            + product("rsc,dc->rsd", value_grad, value_full)
        )
        grad_normed = lax.psum_scatter(
            grad_normed_part.astype(jnp.bfloat16), "tp", scatter_dimension=1, tiled=True
        ).astype(jnp.float32)
        norm_value, norm_one_pull = jax.vjp(layer_norm, layer_input, gain_one, shift_one)
        grad_input_norm, gain_one_grad, shift_one_grad = norm_one_pull(grad_normed)
        grad_now = grad_middle + grad_input_norm
        vector_sums = lax.psum(
            (
                gain_one_grad,
                shift_one_grad,
                out_bias_part,
                gain_two_grad,
                shift_two_grad,
                down_bias_part,
            ),
            "tp",
        )
        sharded = (
            lax.psum_scatter(
                vector_sums[0].astype(jnp.bfloat16), "fsdp", scatter_dimension=0, tiled=True
            ).astype(jnp.float32),
            lax.psum_scatter(
                vector_sums[1].astype(jnp.bfloat16), "fsdp", scatter_dimension=0, tiled=True
            ).astype(jnp.float32),
            lax.psum_scatter(
                query_weight_grad.astype(jnp.bfloat16), "fsdp", scatter_dimension=0, tiled=True
            ).astype(jnp.float32),
            lax.psum_scatter(
                key_weight_grad.astype(jnp.bfloat16), "fsdp", scatter_dimension=0, tiled=True
            ).astype(jnp.float32),
            lax.psum_scatter(
                value_weight_grad.astype(jnp.bfloat16), "fsdp", scatter_dimension=0, tiled=True
            ).astype(jnp.float32),
            lax.psum_scatter(
                out_grad.astype(jnp.bfloat16), "fsdp", scatter_dimension=0, tiled=True
            ).astype(jnp.float32),
            lax.psum_scatter(
                vector_sums[2].astype(jnp.bfloat16), "fsdp", scatter_dimension=0, tiled=True
            ).astype(jnp.float32),
            lax.psum_scatter(
                vector_sums[3].astype(jnp.bfloat16), "fsdp", scatter_dimension=0, tiled=True
            ).astype(jnp.float32),
            lax.psum_scatter(
                vector_sums[4].astype(jnp.bfloat16), "fsdp", scatter_dimension=0, tiled=True
            ).astype(jnp.float32),
            lax.psum_scatter(
                up_grad.astype(jnp.bfloat16), "fsdp", scatter_dimension=0, tiled=True
            ).astype(jnp.float32),
            lax.psum_scatter(
                down_grad.astype(jnp.bfloat16), "fsdp", scatter_dimension=0, tiled=True
            ).astype(jnp.float32),
            lax.psum_scatter(
                vector_sums[5].astype(jnp.bfloat16), "fsdp", scatter_dimension=0, tiled=True
            ).astype(jnp.float32),
        )
        head_sums = lax.psum((query_bias_part, value_bias_part, up_bias_part), "fsdp")
        collected[layer_idx] = (sharded, head_sums)

    def stacked(group, member):
        return jnp.stack([collected[0][group][member]])

    return (
        activations_out,
        grad_now,
        stacked(0, 0),
        stacked(0, 1),
        stacked(0, 2),
        stacked(1, 0),
        stacked(0, 3),
        stacked(0, 4),
        stacked(1, 1),
        stacked(0, 5),
        stacked(0, 6),
        stacked(0, 7),
        stacked(0, 8),
        stacked(0, 9),
        stacked(1, 2),
        stacked(0, 10),
        stacked(0, 11),
    )


def solution(mesh):
    in_specs = (
        P("fsdp", "tp", None),
        P("fsdp", None),
        P("fsdp", "tp", None),
        P(None, "fsdp"),
        P(None, "fsdp"),
        P(None, "fsdp", "tp"),
        P(None, "tp"),
        P(None, "fsdp", "tp"),
        P(None, "fsdp", "tp"),
        P(None, "tp"),
        P(None, "fsdp", "tp"),
        P(None, "fsdp"),
        P(None, "fsdp"),
        P(None, "fsdp"),
        P(None, "fsdp", "tp"),
        P(None, "tp"),
        P(None, "fsdp", "tp"),
        P(None, "fsdp"),
    )
    out_specs = (
        P("fsdp", "tp", None),
        P("fsdp", "tp", None),
        P(None, "fsdp"),
        P(None, "fsdp"),
        P(None, "fsdp", "tp"),
        P(None, "tp"),
        P(None, "fsdp", "tp"),
        P(None, "fsdp", "tp"),
        P(None, "tp"),
        P(None, "fsdp", "tp"),
        P(None, "fsdp"),
        P(None, "fsdp"),
        P(None, "fsdp"),
        P(None, "fsdp", "tp"),
        P(None, "tp"),
        P(None, "fsdp", "tp"),
        P(None, "fsdp"),
    )
    return jax.shard_map(local, mesh=mesh, in_specs=in_specs, out_specs=out_specs, check_vma=False)
```

profile of v0, /device:TPU:0, one launch (start us, length us, event | category | flops | bytes accessed | tf_op | source)
XLA Modules:
  0.0 1254.9 jit_solution(4234695958085850078)
XLA Ops:
  17.5 26.1 %all-reduce.15 = (bf16[1152]{0:T(1024)(128)(2,1)}, bf16[1152]{0:T(1024)(128)(2,1)}, bf16[1152]{0:T(1024)(128)(2,1)S(1)}, bf16[1152]{0:T(1024)(128)(2,1)S(1)}, bf16[1152]{0:T(1024)(128)(2,1)}) all-reduce(bf16[1152]{0:T(1024)(128)(2,1)S(1)} %dynamic-update-slice.4, ...), channel_id=10, replica_groups=mesh['fsdp'=8,'tp'=4] {'fsdp'}, use_global_device_ids=true, to_apply=%add.4 | all-reduce | flops 5760 | bytes 23040
  46.2 9.7 all-gather.2
  55.8 11.7 all-gather.3
  67.5 11.4 all-gather.4
  78.9 11.5 all-gather.5
  91.0 43.7 %all-gather.19.cloned.1.call-done = bf16[1,2048,1152]{2,1,0:T(8,128)(2,1)} async-done(((bf16[1,512,1152]{2,1,0:T(8,128)(2,1)}), bf16[1,2048,1152]{2,1,0:T(8,128)(2,1)}) %all-gather.19.cloned.1.call-update) | async-done | bytes 4718608 | tf_op jit(solution)/shard_map/all_gather | solution.py:212
  147.5 62.6 %while.49 = (s32[]{:T(128)}, f32[4,512,4,72]{1,3,2,0:T(8,128)}, f32[4,4,512]{2,1,0:T(4,128)S(1)}, s32[4,512]{1,0:T(4,128)S(1)}, s32[2048]{0:T(1024)S(1)}, /*inde...) while((s32[]{:T(128)}, f32[4,512,4,72]{1,3,2,0:T(8,128)}, ...), condition=%wide.region_7.8_spmd.clone, body=%wide.region_4.7_spmd.sunk.clone | while | flops 1259337728 | bytes 57849964 | solution.py:95
  173.2 5.5 fusion.207
  220.1 83.2 %reduce-scatter.11.cloned.1.call-done = bf16[1,512,1152]{2,1,0:T(8,128)(2,1)} async-done(((bf16[1,2048,1152]{2,1,0:T(8,128)(2,1)}), bf16[1,512,1152]{2,1,0:T(8,128)(2,1)}) %reduce-scatter.11.cloned.1.call-update) | async-done | bytes 1179664 | tf_op jit(solution)/shard_map/reduce_scatter | solution.py:224
  311.6 85.8 %all-gather.21.cloned.1.call-done = bf16[1,2048,1152]{2,1,0:T(8,128)(2,1)} async-done(((bf16[1,512,1152]{2,1,0:T(8,128)(2,1)}), bf16[1,2048,1152]{2,1,0:T(8,128)(2,1)}) %all-gather.21.cloned.1.call-update) | async-done | bytes 4718608 | tf_op jit(solution)/shard_map/all_gather | solution.py:231
  397.4 11.1 convolution_add_fusion.2
  408.5 19.2 %all-gather.29.cloned.1.call-done = bf16[1,1152,1076]{2,1,0:T(8,128)(2,1)} async-done(((bf16[1,144,1076]{2,1,0:T(8,128)(2,1)}), bf16[1,1152,1076]{2,1,0:T(8,128)(2,1)}) %all-gather.29.cloned.1.call-update) | async-done | bytes 2479120 | tf_op jit(solution)/shard_map/all_gather | solution.py:59
  427.7 91.4 %all-gather.23.cloned.1.call-done = bf16[1,2048,1152]{2,1,0:T(8,128)(2,1)} async-done(((bf16[1,512,1152]{2,1,0:T(8,128)(2,1)}), bf16[1,2048,1152]{2,1,0:T(8,128)(2,1)}) %all-gather.23.cloned.1.call-update) | async-done | bytes 4718608 | tf_op jit(solution)/shard_map/all_gather | solution.py:301
  519.2 17.1 %convert_reduce_fusion = (f32[1076]{0:T(1024)}, bf16[2048,1076]{0,1:T(8,128)(2,1)S(1)}) fusion(f32[2048,1076]{0,1:T(8,128)} %convolution_add_fusion.2, bf16[1,1152,1076]{2,1,0:T(8,128)(2,1)} %all-gather.29.cloned.1.call-done, bf16[1,2048,1152]{2,1,0:T(8,128)(2,1)} %all-gather.23.cloned.1.call-done), kind=kOutput, calls=%fused_computation.62 | convolution fusion | flops 5125684224 | bytes 20423888 | tf_op jit(solution)/shard_map/rsd,df->rsf/dot_general | solution.py:20
  538.3 9.0 fusion.51
  547.3 83.8 %reduce-scatter.15.cloned.1.call-done = bf16[1,512,1152]{2,1,0:T(8,128)(2,1)} async-done(((bf16[1,2048,1152]{2,1,0:T(8,128)(2,1)}), bf16[1,512,1152]{2,1,0:T(8,128)(2,1)}) %reduce-scatter.15.cloned.1.call-update) | async-done | bytes 1179664 | tf_op jit(solution)/shard_map/reduce_scatter | solution.py:307
  639.7 12.9 %convolution_convert_fusion = bf16[1152,1076]{1,0:T(8,128)(2,1)} fusion(bf16[1,2048,1152]{2,1,0:T(8,128)(2,1)} %all-gather.23.cloned.1.call-done, f32[2048,1076]{0,1:T(8,128)} %convolution_add_fusion.2), kind=kOutput, calls=%fused_computation.65 | convolution fusion | flops 5098277376 | bytes 16012288 | tf_op jit(solution)/shard_map/rsd,rsf->df/dot_general | solution.py:20
  652.9 11.6 convolution_convert_fusion.1
  670.4 58.9 %all-gather.25.cloned.1.call-done = bf16[1,2048,1152]{2,1,0:T(8,128)(2,1)} async-done(((bf16[1,512,1152]{2,1,0:T(8,128)(2,1)}), bf16[1,2048,1152]{2,1,0:T(8,128)(2,1)}) %all-gather.25.cloned.1.call-update) | async-done | bytes 4718608 | tf_op jit(solution)/shard_map/all_gather | solution.py:318
  739.2 6.3 fusion.92
  745.5 202.7 %while.50 = (s32[]{:T(128)}, f32[2048,4,72]{0,2,1:T(8,128)}, f32[2048,4,72]{0,2,1:T(8,128)}, bf16[4,512,4,72]{1,3,2,0:T(8,128)(2,1)}, bf16[4,512,4,72]{1,3,2,0:T...) while((s32[]{:T(128)}, f32[2048,4,72]{0,2,1:T(8,128)}, ...), condition=%wide.region_17.18_spmd.clone.clone, body=%wide.region_15.17_spmd.clone.sunk.clone | while | flops 3086956544 | bytes 221386992 | solution.py:130
  749.7 6.0 copy-done
  755.7 7.3 fusion.219
  763.0 12.8 %multiply_reduce_fusion.4 = (f32[4,512]{1,0:T(4,128)S(1)}, f32[4,512,2048]{2,1,0:T(8,128)}) fusion(f32[4,512,2048]{2,1,0:T(8,128)} %copy-done, f32[4,512]{1,0:T(4,128)S(1)} %dynamic-slice_bitcast_fusion.3, pred[512,2048]{1,0:T(8,128)(4,1)S(1)} %broadcast_compare_fusion.7, bf16[2048,4,72]{0,2,1:T(8,128)(2,1)} %get-tuple-element.606, ...), kind=kOutput, calls=%fused_computation.18.clone.1.clone | convolution fusion | flops 624949248 | bytes 36093956 | tf_op jit(solution)/shard_map/while/body/eval_jaxpr/while/body/eval_jaxpr/qhe,khe->hqk/dot_general | solution.py:20
  775.8 12.7 %multiply_convert_fusion.10 = bf16[4,512,2048]{2,1,0:T(8,128)(2,1)S(1)} fusion(f32[4,512,2048]{2,1,0:T(8,128)} %get-tuple-element.535, f32[4,512,2048]{2,1,0:T(8,128)} %copy-done, f32[4,512]{1,0:T(4,128)S(1)} %get-tuple-element.536, f32[4,512]{1,0:T(4,128)S(1)} %dynamic-slice_bitcast_fusion.3, pred[512,2048]{1,0:T(8,128)(4,1)S(1)} %broadcast_compare_fusion.7), kind=kLoop, calls=%fused_computation.17.clone.1.clone | loop fusion | flops 25165824 | bytes 43008000 | tf_op jit(solution)/shard_map/while/body/eval_jaxpr/while/body/eval_jaxpr/convert_element_type | solution.py:123
  799.6 5.7 copy-done
  805.3 7.8 fusion.219
  813.1 13.1 %multiply_reduce_fusion.4 = (f32[4,512]{1,0:T(4,128)S(1)}, f32[4,512,2048]{2,1,0:T(8,128)}) fusion(f32[4,512,2048]{2,1,0:T(8,128)} %copy-done, f32[4,512]{1,0:T(4,128)S(1)} %dynamic-slice_bitcast_fusion.3, pred[512,2048]{1,0:T(8,128)(4,1)S(1)} %broadcast_compare_fusion.7, bf16[2048,4,72]{0,2,1:T(8,128)(2,1)} %get-tuple-element.606, ...), kind=kOutput, calls=%fused_computation.18.clone.1.clone | convolution fusion | flops 624949248 | bytes 36093956 | tf_op jit(solution)/shard_map/while/body/eval_jaxpr/while/body/eval_jaxpr/qhe,khe->hqk/dot_general | solution.py:20
  826.2 12.7 %multiply_convert_fusion.10 = bf16[4,512,2048]{2,1,0:T(8,128)(2,1)S(1)} fusion(f32[4,512,2048]{2,1,0:T(8,128)} %get-tuple-element.535, f32[4,512,2048]{2,1,0:T(8,128)} %copy-done, f32[4,512]{1,0:T(4,128)S(1)} %get-tuple-element.536, f32[4,512]{1,0:T(4,128)S(1)} %dynamic-slice_bitcast_fusion.3, pred[512,2048]{1,0:T(8,128)(4,1)S(1)} %broadcast_compare_fusion.7), kind=kLoop, calls=%fused_computation.17.clone.1.clone | loop fusion | flops 25165824 | bytes 43008000 | tf_op jit(solution)/shard_map/while/body/eval_jaxpr/while/body/eval_jaxpr/convert_element_type | solution.py:123
  850.9 5.7 copy-done
  856.6 7.7 fusion.219
  864.4 12.9 %multiply_reduce_fusion.4 = (f32[4,512]{1,0:T(4,128)S(1)}, f32[4,512,2048]{2,1,0:T(8,128)}) fusion(f32[4,512,2048]{2,1,0:T(8,128)} %copy-done, f32[4,512]{1,0:T(4,128)S(1)} %dynamic-slice_bitcast_fusion.3, pred[512,2048]{1,0:T(8,128)(4,1)S(1)} %broadcast_compare_fusion.7, bf16[2048,4,72]{0,2,1:T(8,128)(2,1)} %get-tuple-element.606, ...), kind=kOutput, calls=%fused_computation.18.clone.1.clone | convolution fusion | flops 624949248 | bytes 36093956 | tf_op jit(solution)/shard_map/while/body/eval_jaxpr/while/body/eval_jaxpr/qhe,khe->hqk/dot_general | solution.py:20
  877.2 12.2 multiply_convert_fusion.10
  901.5 5.7 copy-done
  907.2 7.7 fusion.219
  914.9 12.9 %multiply_reduce_fusion.4 = (f32[4,512]{1,0:T(4,128)S(1)}, f32[4,512,2048]{2,1,0:T(8,128)}) fusion(f32[4,512,2048]{2,1,0:T(8,128)} %copy-done, f32[4,512]{1,0:T(4,128)S(1)} %dynamic-slice_bitcast_fusion.3, pred[512,2048]{1,0:T(8,128)(4,1)S(1)} %broadcast_compare_fusion.7, bf16[2048,4,72]{0,2,1:T(8,128)(2,1)} %get-tuple-element.606, ...), kind=kOutput, calls=%fused_computation.18.clone.1.clone | convolution fusion | flops 624949248 | bytes 36093956 | tf_op jit(solution)/shard_map/while/body/eval_jaxpr/while/body/eval_jaxpr/qhe,khe->hqk/dot_general | solution.py:20
  927.8 12.2 multiply_convert_fusion.10
  958.3 6.0 fusion.86
  964.4 6.5 fusion.140
  970.9 6.1 fusion.89
  977.0 6.0 convolution_add_fusion.1
  989.4 12.2 fusion.50
  1007.5 14.2 %all-reduce.12 = (f32[1,288]{1,0:T(1,128)}, f32[1,288]{1,0:T(1,128)}, f32[1,1076]{1,0:T(1,128)}) all-reduce(f32[1,288]{1,0:T(1,128)S(1)} %stack.87, f32[1,288]{1,0:T(1,128)S(1)} %stack.92, f32[1,1076]{1,0:T(1,128)S(1)} %stack.103), channel_id=1, replica_groups=mesh['fsdp'=8,'tp'=4] {'fsdp'}, use_global_device_ids=true, to_apply=%region_29.30 | all-reduce | flops 1652 | bytes 13216 | tf_op jit(solution)/shard_map/psum | solution.py:394
  1028.5 36.9 %reduce-scatter.23.cloned.1.call-done = bf16[144,288]{1,0:T(8,128)(2,1)} async-done(((bf16[1152,288]{1,0:T(8,128)(2,1)}), bf16[144,288]{1,0:T(8,128)(2,1)}) %reduce-scatter.23.cloned.1.call-update) | async-done | bytes 82960 | tf_op jit(solution)/shard_map/reduce_scatter | solution.py:369
  1067.0 85.9 %reduce-scatter.17.cloned.1.call-done = bf16[1,512,1152]{2,1,0:T(8,128)(2,1)} async-done(((bf16[1,2048,1152]{2,1,0:T(8,128)(2,1)}), bf16[1,512,1152]{2,1,0:T(8,128)(2,1)}) %reduce-scatter.17.cloned.1.call-update) | async-done | bytes 1179664 | tf_op jit(solution)/shard_map/reduce_scatter | solution.py:339
  1159.3 21.3 %all-reduce.13 = (bf16[1152]{0:T(1024)(128)(2,1)}, bf16[1152]{0:T(1024)(128)(2,1)}, bf16[1152]{0:T(1024)(128)(2,1)}, bf16[1152]{0:T(1024)(128)(2,1)}, bf16[1152]{0:T(1024)(128)(2,1)}, /*index=5*/bf16[1152]{0:T(1024)(128)(2,1)}) all-reduce(f32[1152]{0:T(1024)} %get-tuple-element.289, ...), channel_id=1, replica_groups=mesh['fsdp'=8,'tp'=4] {'tp'}, use_global_device_ids=true, to_apply=%region_22.23 | all-reduce | flops 6912 | bytes 41472 | tf_op jit(solution)/shard_map/psum | solution.py:345
  1180.6 24.7 %all-reduce.14 = (bf16[1152]{0:T(1024)(128)(2,1)}, bf16[1152]{0:T(1024)(128)(2,1)}, bf16[1152]{0:T(1024)(128)(2,1)}, bf16[1152]{0:T(1024)(128)(2,1)}, bf16[1152]...) all-reduce(bf16[1152]{0:T(1024)(128)(2,1)} %copy-done.35, ...), channel_id=13, replica_groups=mesh['fsdp'=8,'tp'=4] {'fsdp'}, use_global_device_ids=true, to_apply=%add.5 | all-reduce | flops 8064 | bytes 32256
  1211.9 30.5 %reduce-scatter.13.cloned.1.call-done = bf16[1,512,1152]{2,1,0:T(8,128)(2,1)} async-done(((bf16[1,2048,1152]{2,1,0:T(8,128)(2,1)}), bf16[1,512,1152]{2,1,0:T(8,128)(2,1)}) %reduce-scatter.13.cloned.1.call-update) | async-done | bytes 1179664 | tf_op jit(solution)/shard_map/reduce_scatter | solution.py:235
  (301 shorter events, 220.8 us)
Async XLA Ops:
  8.0 7.0 copy-start.43
  8.0 36.1 %copy-start.1 = (bf16[1,512,1152]{2,1,0:T(8,128)(2,1)S(1)}, bf16[1,512,1152]{2,1,0:T(8,128)(2,1)}, u32[]{:S(2)}) copy-start(bf16[1,512,1152]{2,1,0:T(8,128)(2,1)} %param.22) | copy-start | bytes 3538948
  8.0 126.6 %all-gather.19.cloned.1.call-start = ((), (), s32[]{:S(2)}) async-start(), calls=%async_computation.10 | async-start | bytes 5898240 | tf_op jit(solution)/shard_map/all_gather | solution.py:212
  13.2 32.5 %copy-start.29 = (f32[512]{0:T(512)}, f32[512]{0:T(512)S(1)}, u32[]{:S(2)}) copy-start(f32[512]{0:T(512)S(1)} %broadcast_multiply_fusion.1) | copy-start | bytes 6148
  13.2 32.6 %copy-start.50 = (s32[1,3]{1,0:T(1,128)S(1)}, s32[1,3]{1,0:T(1,128)}, u32[]{:S(2)}) copy-start(s32[1,3]{1,0:T(1,128)} %param.23) | copy-start | bytes 40
  13.2 32.8 %copy-start.44 = (f32[1,288]{1,0:T(1,128)S(1)}, f32[1,288]{1,0:T(1,128)}, u32[]{:S(2)}) copy-start(f32[1,288]{1,0:T(1,128)} %param.28) | copy-start | bytes 3460
  13.2 32.8 %copy-start.45 = (f32[1,288]{1,0:T(1,128)S(1)}, f32[1,288]{1,0:T(1,128)}, u32[]{:S(2)}) copy-start(f32[1,288]{1,0:T(1,128)} %param.31) | copy-start | bytes 3460
  13.2 32.9 %copy-start.25 = (bf16[1,144,288]{2,1,0:T(8,128)(2,1)S(1)}, bf16[1,144,288]{2,1,0:T(8,128)(2,1)}, u32[]{:S(2)}) copy-start(bf16[1,144,288]{2,1,0:T(8,128)(2,1)} %param.27) | copy-start | bytes 248836
  15.0 28.6 %copy-start.32 = (f32[512]{0:T(512)}, f32[512]{0:T(512)S(1)}, u32[]{:S(2)}) copy-start(f32[512]{0:T(512)S(1)} %fusion.124) | copy-start | bytes 6148
  15.0 40.8 %copy-start.26 = (bf16[1,144,288]{2,1,0:T(8,128)(2,1)S(1)}, bf16[1,144,288]{2,1,0:T(8,128)(2,1)}, u32[]{:S(2)}) copy-start(bf16[1,144,288]{2,1,0:T(8,128)(2,1)} %param.29) | copy-start | bytes 248836
  15.0 52.5 %copy-start.30 = (f32[512]{0:T(512)}, f32[512]{0:T(512)S(1)}, u32[]{:S(2)}) copy-start(f32[512]{0:T(512)S(1)} %fusion.144) | copy-start | bytes 6148
  44.2 23.4 %copy-start.27 = (bf16[1,144,288]{2,1,0:T(8,128)(2,1)S(1)}, bf16[1,144,288]{2,1,0:T(8,128)(2,1)}, u32[]{:S(2)}) copy-start(bf16[1,144,288]{2,1,0:T(8,128)(2,1)} %param.30) | copy-start | bytes 248836
  45.7 33.2 %copy-start.28 = (bf16[1,144,288]{2,1,0:T(8,128)(2,1)S(1)}, bf16[1,144,288]{2,1,0:T(8,128)(2,1)}, u32[]{:S(2)}) copy-start(bf16[1,144,288]{2,1,0:T(8,128)(2,1)} %param.32) | copy-start | bytes 248836
  45.7 257.6 %reduce-scatter.11.cloned.1.call-start = ((), (), s32[]{:S(2)}) async-start(), calls=%async_computation.11 | async-start | bytes 5898240 | tf_op jit(solution)/shard_map/reduce_scatter | solution.py:224
  55.8 78.8 %copy-start.14 = (bf16[1,1152,288]{2,1,0:T(8,128)(2,1)}, bf16[1,1152,288]{2,1,0:T(8,128)(2,1)S(1)}, u32[]{:S(2)}) copy-start(bf16[1,1152,288]{2,1,0:T(8,128)(2,1)S(1)} %all-gather.2) | copy-start | bytes 1990660
  139.7 6.0 slice-start
  219.4 83.9 %copy-start.2 = (bf16[1,512,1152]{2,1,0:T(8,128)(2,1)S(1)}, bf16[1,512,1152]{2,1,0:T(8,128)(2,1)}, u32[]{:S(2)}) copy-start(bf16[1,512,1152]{2,1,0:T(8,128)(2,1)} %param.22) | copy-start | bytes 3538948
  219.4 92.1 %all-gather.27.cloned.1.call-start = ((), (), s32[]{:S(2)}) async-start(), calls=%async_computation.24 | async-start | bytes 2985984 | tf_op jit(solution)/shard_map/all_gather | solution.py:58
  220.0 177.4 %all-gather.21.cloned.1.call-start = ((), (), s32[]{:S(2)}) async-start(), calls=%async_computation.12 | async-start | bytes 5898240 | tf_op jit(solution)/shard_map/all_gather | solution.py:231
  220.1 414.5 %copy-start.21 = (f32[1152]{0:T(1024)}, f32[1152]{0:T(1024)S(1)}, u32[]{:S(2)}) copy-start(f32[1152]{0:T(1024)S(1)} %convert_element_type.390) | copy-start | bytes 13828
  307.5 120.2 %all-gather.29.cloned.1.call-start = ((), (), s32[]{:S(2)}) async-start(), calls=%async_computation.25 | async-start | bytes 2985984 | tf_op jit(solution)/shard_map/all_gather | solution.py:59
  308.1 211.1 %all-gather.23.cloned.1.call-start = ((), (), s32[]{:S(2)}) async-start(), calls=%async_computation.14 | async-start | bytes 5898240 | tf_op jit(solution)/shard_map/all_gather | solution.py:301
  308.2 328.8 %copy-start.31 = (f32[512]{0:T(512)}, f32[512]{0:T(512)S(1)}, u32[]{:S(2)}) copy-start(f32[512]{0:T(512)S(1)} %dynamic-slice.4) | copy-start | bytes 6148
  311.5 319.7 %reduce-scatter.15.cloned.1.call-start = ((), (), s32[]{:S(2)}) async-start(), calls=%async_computation.15 | async-start | bytes 5898240 | tf_op jit(solution)/shard_map/reduce_scatter | solution.py:307
  519.2 19.1 %copy-start.48 = (bf16[1,1152,1076]{2,1,0:T(8,128)(2,1)S(1)}, bf16[1,1152,1076]{2,1,0:T(8,128)(2,1)}, u32[]{:S(2)}) copy-start(bf16[1,1152,1076]{2,1,0:T(8,128)(2,1)} %all-gather.27.cloned.1.call-done) | copy-start | bytes 7437316
  547.3 182.1 %all-gather.25.cloned.1.call-start = ((), (), s32[]{:S(2)}) async-start(), calls=%async_computation.16 | async-start | bytes 5898240 | tf_op jit(solution)/shard_map/all_gather | solution.py:318
  639.4 363.9 %reduce-scatter.29.cloned.1.call-start = ((), (), s32[]{:S(2)}) async-start(), calls=%async_computation.23 | async-start | bytes 2985984 | tf_op jit(solution)/shard_map/reduce_scatter | solution.py:387
  652.6 352.6 %reduce-scatter.27.cloned.1.call-start = ((), (), s32[]{:S(2)}) async-start(), calls=%async_computation.22 | async-start | bytes 2985984 | tf_op jit(solution)/shard_map/reduce_scatter | solution.py:384
  664.5 357.2 %reduce-scatter.25.cloned.1.call-start = ((), (), s32[]{:S(2)}) async-start(), calls=%async_computation.21 | async-start | bytes 995328 | tf_op jit(solution)/shard_map/reduce_scatter | solution.py:372
  668.2 61.1 %copy-start.20 = (bf16[1,1152,288]{2,1,0:T(8,128)(2,1)S(1)}, bf16[1,1152,288]{2,1,0:T(8,128)(2,1)}, u32[]{:S(2)}) copy-start(bf16[1,1152,288]{2,1,0:T(8,128)(2,1)} %all-gather.5) | copy-start | bytes 1990660
  668.2 61.1 %copy-start.39 = (bf16[2048]{0:T(1024)(128)(2,1)S(1)}, bf16[2048]{0:T(1024)(128)(2,1)}, u32[]{:S(2)}) copy-start(bf16[2048]{0:T(1024)(128)(2,1)} %get-tuple-element.367) | copy-start | bytes 12292
  745.4 277.9 %reduce-scatter.19.cloned.1.call-start = ((), (), s32[]{:S(2)}) async-start(), calls=%async_computation.18 | async-start | bytes 995328 | tf_op jit(solution)/shard_map/reduce_scatter | solution.py:363
  749.7 6.0 copy-start
  775.8 12.7 %copy-start.8 = (bf16[4,512,4,72]{1,3,2,0:T(8,128)(2,1)S(1)}, bf16[4,512,4,72]{1,3,2,0:T(8,128)(2,1)}, u32[]{:S(2)}) copy-start(bf16[4,512,4,72]{1,3,2,0:T(8,128)(2,1)} %get-tuple-element.588) | copy-start | bytes 3538948 | tf_op jit(solution)/shard_map/while/body/eval_jaxpr/while
  799.6 5.7 copy-start
  826.2 12.7 %copy-start.8 = (bf16[4,512,4,72]{1,3,2,0:T(8,128)(2,1)S(1)}, bf16[4,512,4,72]{1,3,2,0:T(8,128)(2,1)}, u32[]{:S(2)}) copy-start(bf16[4,512,4,72]{1,3,2,0:T(8,128)(2,1)} %get-tuple-element.588) | copy-start | bytes 3538948 | tf_op jit(solution)/shard_map/while/body/eval_jaxpr/while
  850.9 5.7 copy-start
  877.2 12.2 copy-start.8
  927.8 12.2 copy-start.8
  954.5 72.4 %reduce-scatter.21.cloned.1.call-start = ((), (), s32[]{:S(2)}) async-start(), calls=%async_computation.19 | async-start | bytes 995328 | tf_op jit(solution)/shard_map/reduce_scatter | solution.py:366
  964.3 101.0 %reduce-scatter.23.cloned.1.call-start = ((), (), s32[]{:S(2)}) async-start(), calls=%async_computation.20 | async-start | bytes 995328 | tf_op jit(solution)/shard_map/reduce_scatter | solution.py:369
  976.9 6.1 copy-start.16
  976.9 175.9 %reduce-scatter.17.cloned.1.call-start = ((), (), s32[]{:S(2)}) async-start(), calls=%async_computation.17 | async-start | bytes 5898240 | tf_op jit(solution)/shard_map/reduce_scatter | solution.py:339
  987.7 254.6 %reduce-scatter.13.cloned.1.call-start = ((), (), s32[]{:S(2)}) async-start(), calls=%async_computation.13 | async-start | bytes 5898240 | tf_op jit(solution)/shard_map/reduce_scatter | solution.py:235
  1001.7 151.2 %copy-start.3 = (bf16[1,512,1152]{2,1,0:T(8,128)(2,1)S(1)}, bf16[1,512,1152]{2,1,0:T(8,128)(2,1)}, u32[]{:S(2)}) copy-start(bf16[1,512,1152]{2,1,0:T(8,128)(2,1)} %param.22) | copy-start | bytes 3538948
  1001.7 151.2 %copy-start.24 = (f32[1152]{0:T(1024)S(1)}, f32[1152]{0:T(1024)}, u32[]{:S(2)}) copy-start(f32[1152]{0:T(1024)} %copy-done.23) | copy-start | bytes 13828
  1067.0 175.4 %copy-start.5 = (bf16[1,512,1152]{2,1,0:T(8,128)(2,1)S(1)}, bf16[1,512,1152]{2,1,0:T(8,128)(2,1)}, u32[]{:S(2)}) copy-start(bf16[1,512,1152]{2,1,0:T(8,128)(2,1)} %reduce-scatter.11.cloned.1.call-done) | copy-start | bytes 3538948
  1067.0 175.4 %copy-start.22 = (f32[1152]{0:T(1024)S(1)}, f32[1152]{0:T(1024)}, u32[]{:S(2)}) copy-start(f32[1152]{0:T(1024)} %copy-done.21) | copy-start | bytes 13828
  (31 other events, 83.4 us)
Sparse Core Ops, SparseCore 0:
  45.8 88.7 all-gather.18
  219.6 83.6 reduce-scatter.10
  547.4 83.6 reduce-scatter.14
Sparse Core Ops, SparseCore 1:
  221.8 28.5 all-gather.26
  307.6 89.8 all-gather.20
  399.2 28.5 all-gather.28
  429.9 89.2 all-gather.22
  639.5 89.7 all-gather.24
  732.8 42.1 reduce-scatter.28
  778.7 43.6 reduce-scatter.26
  825.5 34.9 reduce-scatter.24
  954.6 33.3 reduce-scatter.18
  991.7 35.1 reduce-scatter.20
  1030.4 35.0 reduce-scatter.22
  1067.7 85.1 reduce-scatter.16
  1155.0 87.2 reduce-scatter.12
where the time goes:
time: 1260 us; the launch traced here: 1250 us
  waiting for transfers between devices  623 us (49%)
  matrix products  302 us (24%)
  other arithmetic  132 us (10%)
  blocking collectives  131 us (10%)
  local copies, waits for them, and re-layouts  47.6 us (4%)
  between operations  18.2 us (1%)
    dot_general x46, matrix products, product(): return jnp.einsum(form, left, right, preferred_element_type=jnp.float32)  302 us
    all_gather x1, waiting for transfers between devices, local(): grad_mixed_all = lax.all_gather(grad_mixed, 'tp', axis=1, tiled=True)  91.4 us
    reduce_scatter x1, waiting for transfers between devices, local(): lax.psum_scatter(grad_normed_part.astype(jnp.bfloat16), 'tp', scatter_dim...  85.9 us
    all_gather x1, waiting for transfers between devices, local(): mlp_input = lax.all_gather(normed_two, 'tp', axis=1, tiled=True)  85.8 us
    reduce_scatter x1, waiting for transfers between devices, local(): lax.psum_scatter(product('rsf,df->rsd', grad_hidden, up_full).astype(jnp....  83.8 us
    reduce_scatter x1, waiting for transfers between devices, local(): lax.psum_scatter(partial_out.astype(jnp.bfloat16), 'tp', scatter_dimensio...  83.2 us
    all_gather x1, waiting for transfers between devices, local(): grad_branch_all = lax.all_gather(grad_branch, 'tp', axis=1, tiled=True)  58.9 us
    unnamed x2, blocking collectives  50.8 us
  transfers between devices with their start and end apart: 16, of which 11 were waited for; matrix products, arithmetic and copies ran while one was open for 25% of the time, Pallas kernels for 0%

commit v1 on v0

v1 whole, which is shorter than its diff:
```python
import functools
import math

import jax
import jax.numpy as jnp
from jax import lax
from jax.experimental import pallas as pl
from jax.experimental.pallas import tpu as pltpu
from jax.sharding import PartitionSpec as P

HEAD_DIM = 72
AUG = 8
PIC_MAX = 1024
MASKED = -1e30
BF = jnp.bfloat16
F32 = jnp.float32


def xhat_of(values):
    center = values - jnp.mean(values, axis=-1, keepdims=True)
    rstd = lax.rsqrt(jnp.mean(center * center, axis=-1, keepdims=True) + 1e-06)
    return center * rstd, rstd


def norm_back(dy, xhat, rstd, gain):
    dxhat = dy * gain
    grad = dxhat - jnp.mean(dxhat, axis=-1, keepdims=True)
    grad = (grad - xhat * jnp.mean(dxhat * xhat, axis=-1, keepdims=True)) * rstd
    return grad, jnp.sum(dy * xhat, axis=0), jnp.sum(dy, axis=0)


def gelu_tanh(values):
    return jax.nn.gelu(values, approximate=True)


def product(form, left, right):
    return jnp.einsum(form, left, right, preferred_element_type=F32)


def split3(values):
    high = lax.reduce_precision(values, 8, 7)
    rest = values - high
    mid = lax.reduce_precision(rest, 8, 7)
    return jnp.stack([high, mid, rest - mid], axis=0)


def ring_gather(piece, count):
    ring = [(i, (i + 1) % count) for i in range(count)]
    slots = [piece]
    for _ in range(count - 1):
        slots.append(lax.ppermute(slots[-1], "tp", ring))
    return slots


def ring_reduce(slots):
    count = len(slots)
    ring = [(i, (i - 1) % count) for i in range(count)]
    total = slots[-1].astype(BF)
    for s in reversed(range(count - 1)):
        total = lax.ppermute(total, "tp", ring)
        total = total.astype(F32) + slots[s].astype(F32)
        if s:
            total = total.astype(BF)
    return total


def attend_kernel(count_ref, index_ref, q_ref, k_ref, v_ref, valid_ref, o_ref, lse_ref, *, q_block, k_block):
    heads, rows, q_len = q_ref.shape
    chunks = k_ref.shape[2] // k_block
    dim = rows - AUG
    for b in range(q_len // q_block):
        cols = slice(b * q_block, (b + 1) * q_block)
        q_parts = [q_ref[h, :, cols] for h in range(heads)]

        def step(t, carry):
            start = pl.multiple_of(index_ref[b * chunks + t] * k_block, k_block)
            out = []
            for h in range(heads):
                top, acc = carry[h]
                k_part = k_ref[h, :, pl.ds(start, k_block)]
                scores = lax.dot_general(
                    k_part, q_parts[h], (((0,), (0,)), ((), ())), preferred_element_type=F32
                )
                higher = jnp.maximum(top, jnp.max(scores, axis=0, keepdims=True))
                weights = jnp.exp2(scores - higher).astype(BF)
                v_part = v_ref[h, :, pl.ds(start, k_block)]
                acc = acc * jnp.exp2(top - higher) + jnp.dot(
                    v_part, weights, preferred_element_type=F32
                )
                out.append((higher, acc))
            return tuple(out)

        first = tuple(
            (jnp.full((1, q_block), MASKED, F32), jnp.zeros((rows, q_block), F32))
            for _ in range(heads)
        )
        final = lax.fori_loop(0, count_ref[b], step, first)
        live = valid_ref[:, cols] > 0
        for h in range(heads):
            top, acc = final[h]
            total = jnp.where(live, acc[dim : dim + 1], 1.0)
            o_ref[h, :, cols] = jnp.where(live, acc[:dim] / total, 0.0).astype(BF)
            lse_ref[h, :, cols] = jnp.where(live, top + jnp.log2(total), 0.0)


def attend(q_aug, k_aug, v_aug, valid, counts, indices, q_block, k_block, group):
    heads, rows, q_len = q_aug.shape
    k_len = k_aug.shape[2]
    dim = rows - AUG
    spec = lambda r, n: pl.BlockSpec((group, r, n), lambda g, *_: (g, 0, 0))
    return pl.pallas_call(
        functools.partial(attend_kernel, q_block=q_block, k_block=k_block),
        grid_spec=pltpu.PrefetchScalarGridSpec(
            num_scalar_prefetch=2,
            grid=(heads // group,),
            in_specs=[
                spec(rows, q_len),
                spec(rows, k_len),
                spec(rows, k_len),
                pl.BlockSpec((1, q_len), lambda g, *_: (0, 0)),
            ],
            out_specs=[spec(dim, q_len), spec(1, q_len)],
        ),
        out_shape=[
            jax.ShapeDtypeStruct((heads, dim, q_len), BF),
            jax.ShapeDtypeStruct((heads, 1, q_len), F32),
        ],
        compiler_params=pltpu.CompilerParams(vmem_limit_bytes=40 << 20),
        cost_estimate=pl.CostEstimate(
            flops=4 * heads * rows * q_len * k_len,
            bytes_accessed=4 * heads * rows * (q_len + k_len),
            transcendentals=heads * q_len * k_len // 2,
        ),
        name="attend",
    )(counts, indices, q_aug, k_aug, v_aug, valid)


def attend_back_kernel(
    count_ref, index_ref, q_ref, k_ref, v_ref, g_ref, dq_ref, dk_ref, dv_ref, dk_acc, dv_acc, *, q_block, k_block
):
    heads, rows, q_len = q_ref.shape
    chunks = k_ref.shape[2] // k_block
    dim = rows - AUG
    dk_acc[...] = jnp.zeros_like(dk_acc)
    dv_acc[...] = jnp.zeros_like(dv_acc)
    for b in range(q_len // q_block):
        cols = slice(b * q_block, (b + 1) * q_block)
        q_parts = [q_ref[h, :, cols] for h in range(heads)]
        g_parts = [g_ref[h, :, cols] for h in range(heads)]

        def step(t, carry):
            start = pl.multiple_of(index_ref[b * chunks + t] * k_block, k_block)
            here = pl.ds(start, k_block)
            out = []
            for h in range(heads):
                k_part = k_ref[h, :, here]
                scores = lax.dot_general(
                    k_part, q_parts[h], (((0,), (0,)), ((), ())), preferred_element_type=F32
                )
                probs = jnp.exp2(scores)
                dprobs = lax.dot_general(
                    v_ref[h, :, here],
                    g_parts[h],
                    (((0,), (0,)), ((), ())),
                    preferred_element_type=F32,
                )
                dscores = (probs * dprobs).astype(BF)
                out.append(carry[h] + jnp.dot(k_part, dscores, preferred_element_type=F32))
                dk_acc[h, :, here] += lax.dot_general(
                    q_parts[h], dscores, (((1,), (1,)), ((), ())), preferred_element_type=F32
                )
                dv_acc[h, :, here] += lax.dot_general(
                    g_parts[h],
                    probs.astype(BF),
                    (((1,), (1,)), ((), ())),
                    preferred_element_type=F32,
                )
            return tuple(out)

        first = tuple(jnp.zeros((rows, q_block), F32) for _ in range(heads))
        final = lax.fori_loop(0, count_ref[b], step, first)
        for h in range(heads):
            dq_ref[h, :, cols] = (final[h][:dim] * dim**-0.5).astype(BF)
    for h in range(heads):
        dk_ref[h] = (dk_acc[h, :dim, :] * math.log(2.0)).astype(BF)
        dv_ref[h] = dv_acc[h, :dim, :].astype(BF)


def attend_back(q_aug, k_aug, v_aug, g_aug, counts, indices, q_block, k_block, group):
    heads, rows, q_len = q_aug.shape
    k_len = k_aug.shape[2]
    dim = rows - AUG
    spec = lambda r, n: pl.BlockSpec((group, r, n), lambda g, *_: (g, 0, 0))
    return pl.pallas_call(
        functools.partial(attend_back_kernel, q_block=q_block, k_block=k_block),
        grid_spec=pltpu.PrefetchScalarGridSpec(
            num_scalar_prefetch=2,
            grid=(heads // group,),
            in_specs=[spec(rows, q_len), spec(rows, k_len), spec(rows, k_len), spec(rows, q_len)],
            out_specs=[spec(dim, q_len), spec(dim, k_len), spec(dim, k_len)],
            scratch_shapes=[
                pltpu.VMEM((group, rows, k_len), F32),
                pltpu.VMEM((group, rows, k_len), F32),
            ],
        ),
        out_shape=[
            jax.ShapeDtypeStruct((heads, dim, q_len), BF),
            jax.ShapeDtypeStruct((heads, dim, k_len), BF),
            jax.ShapeDtypeStruct((heads, dim, k_len), BF),
        ],
        compiler_params=pltpu.CompilerParams(vmem_limit_bytes=40 << 20),
        cost_estimate=pl.CostEstimate(
            flops=10 * heads * rows * q_len * k_len,
            bytes_accessed=8 * heads * rows * (q_len + k_len),
            transcendentals=heads * q_len * k_len // 2,
        ),
        name="attend_back",
    )(counts, indices, q_aug, k_aug, v_aug, g_aug)


def local(
    activations,
    lengths,
    cotangent,
    ln1_gain,
    ln1_bias,
    query_weight,
    query_bias,
    key_weight,
    value_weight,
    value_bias,
    out_weight,
    out_bias,
    ln2_gain,
    ln2_bias,
    up_weight,
    up_bias,
    down_weight,
    down_bias,
):
    n = lax.axis_size("tp")
    me = lax.axis_index("tp")
    _, here, width = activations.shape
    total_len = here * n
    pics = lengths.shape[1]
    cols = query_weight.shape[2]
    units = up_weight.shape[2]
    heads = cols * n // HEAD_DIM
    hh = cols * n
    reach = min(n - 1, -(-(PIC_MAX - 1) // here))
    scale = HEAD_DIM**-0.5

    x_own = activations[0]
    to_left = [(i, i - 1) for i in range(1, n)]
    to_right = [(i, i + 1) for i in range(n - 1)]
    after, before = [x_own], [x_own]
    for _ in range(reach):
        after.append(lax.ppermute(after[-1], "tp", to_left))
        before.append(lax.ppermute(before[-1], "tp", to_right))
    slots = []
    token_slots = [x_own]
    for j in range(1, n):
        use_after, use_before = j <= reach, n - j <= reach
        if not (use_after or use_before):
            continue
        slots.append((j, use_after, use_before))
        if use_after and use_before:
            token_slots.append(jnp.where(me + j < n, after[j], before[n - j]))
        else:
            token_slots.append(after[j] if use_after else before[n - j])

    ends = jnp.cumsum(lengths[0])
    positions = jnp.arange(total_len, dtype=jnp.int32)
    segment = jnp.sum((positions[:, None] >= ends[None, :]).astype(jnp.int32), axis=1)
    own_seg = lax.dynamic_slice_in_dim(segment, me * here, here, 0)
    key_segs = [own_seg]
    for j, use_after, use_before in slots:
        seg = lax.dynamic_slice_in_dim(segment, ((me + j) % n) * here, here, 0)
        there = jnp.where(me + j < n, use_after, use_before)
        key_segs.append(jnp.where(there, seg, pics))
    key_seg = jnp.concatenate(key_segs)
    k_len = key_seg.shape[0]
    valid = (own_seg < pics).astype(F32)
    valid_col = valid[:, None]
    q_block = min(256, here)
    k_block = min(256, here)
    picture = jnp.arange(pics, dtype=jnp.int32)
    q_has = jnp.any(own_seg.reshape(-1, q_block, 1) == picture, axis=1)
    k_has = jnp.any(key_seg.reshape(-1, k_block, 1) == picture, axis=1)
    active = jnp.any(q_has[:, None, :] & k_has[None, :, :], axis=2)
    counts = jnp.sum(active.astype(jnp.int32), axis=1)
    place = jnp.cumsum(active.astype(jnp.int32), axis=1) - 1
    chunk_ids = jnp.arange(active.shape[1], dtype=jnp.int32)
    hit = active[:, :, None] & (place[:, :, None] == chunk_ids[None, None, :])
    indices = jnp.sum(jnp.where(hit, chunk_ids[None, :, None], 0), axis=1).reshape(-1)

    q_mask = jnp.concatenate(
        [
            jnp.where(own_seg[None, :] == picture[:, None], 0.0, MASKED),
            jnp.full((1, here), MASKED, F32),
        ],
        axis=0,
    )
    k_mask = jnp.concatenate(
        [(key_seg[None, :] == picture[:, None]), (key_seg >= pics)[None, :]], axis=0
    ).astype(BF)
    spare = AUG - (pics + 1) - 3
    k_added = jnp.concatenate(
        [k_mask, jnp.ones((3, k_len), BF), jnp.zeros((spare, k_len), BF)], axis=0
    )
    v_added = jnp.concatenate([jnp.ones((3, k_len), BF), jnp.zeros((AUG - 3, k_len), BF)], axis=0)

    def widen(body, added):
        body = body.reshape(heads, HEAD_DIM, body.shape[-1])
        added = jnp.broadcast_to(added, (heads, AUG, body.shape[-1]))
        return jnp.concatenate([body, added.astype(BF)], axis=1)

    attn_piece = jnp.concatenate(
        [query_weight[0], key_weight[0], value_weight[0], out_weight[0]], axis=1
    )
    attn_slots = ring_gather(attn_piece, n)
    vectors = jnp.stack(
        [ln1_gain[0], ln1_bias[0], out_bias[0], ln2_gain[0], ln2_bias[0], down_bias[0]], axis=1
    ).astype(BF)
    attn_shard = jnp.concatenate(
        [s[:, t * cols : (t + 1) * cols] for t in range(4) for s in attn_slots] + [vectors], axis=1
    )
    attn_full = lax.all_gather(attn_shard, "fsdp", axis=0, tiled=True)
    up_slots = ring_gather(up_weight[0], n)
    up_full = lax.all_gather(jnp.concatenate(up_slots, axis=1), "fsdp", axis=0, tiled=True)
    down_slots = ring_gather(down_weight[0], n)
    down_full = lax.all_gather(jnp.concatenate(down_slots, axis=1), "fsdp", axis=0, tiled=True)
    bias_slots = ring_gather(
        jnp.concatenate([query_bias[0], value_bias[0], up_bias[0]]), n
    )
    query_shift = jnp.concatenate([b[:cols] for b in bias_slots])
    value_shift = jnp.concatenate([b[cols : 2 * cols] for b in bias_slots])
    up_shift = jnp.concatenate([b[2 * cols :] for b in bias_slots])

    query_full = attn_full[:, :hh]
    kv_full = attn_full[:, hh : 3 * hh]
    out_full = attn_full[:, 3 * hh : 4 * hh]
    rows = attn_full[:, 4 * hh :].astype(F32).T
    gain_one, shift_one, out_shift, gain_two, shift_two, down_shift = rows

    x = x_own.astype(F32)
    tokens = jnp.concatenate(token_slots, axis=0).astype(F32)
    all_hat, _ = xhat_of(tokens)
    normed_all = (all_hat * gain_one + shift_one).astype(BF)
    normed = normed_all[:here]
    queries = (
        (product("td,dc->ct", normed, query_full) + query_shift[:, None])
        * (scale * math.log2(math.e))
    ).astype(BF)
    kv_shift = jnp.concatenate([jnp.zeros((hh,), F32), value_shift])
    keys_values = (product("td,dc->ct", normed_all, kv_full) + kv_shift[:, None]).astype(BF)
    k_aug = widen(keys_values[:hh], k_added)
    v_aug = widen(keys_values[hh:], v_added)
    q_rest = jnp.zeros((AUG - (pics + 1), here), F32)
    q_aug = widen(queries, jnp.concatenate([q_mask, q_rest], axis=0))
    group = 4 if heads % 4 == 0 else 1
    attended, log_total = attend(
        q_aug, k_aug, v_aug, valid[None, :], counts, indices, q_block, k_block, group
    )
    flat = attended.reshape(hh, here)
    middle = x + (product("ct,dc->td", flat, out_full) + out_shift)

    two_hat, two_rstd = xhat_of(middle)
    normed_two = (two_hat * gain_two + shift_two).astype(BF)
    hidden = product("td,df->tf", normed_two, up_full) + up_shift
    active_units, gelu_pull = jax.vjp(gelu_tanh, hidden)
    active_units = active_units.astype(BF)
    mixed = product("tf,df->td", active_units, down_full) + down_shift
    activations_out = ((middle + mixed) * valid_col).astype(BF)

    grad_two = cotangent[0].astype(F32) * valid_col
    grad_mixed = grad_two.astype(BF)
    down_bias_part = jnp.sum(grad_mixed, axis=0, dtype=F32)
    down_grad = product("td,tf->df", grad_mixed, active_units).astype(BF)
    down_scattered = lax.psum_scatter(down_grad, "fsdp", scatter_dimension=0, tiled=True)
    grad_hidden = gelu_pull(product("td,df->tf", grad_mixed, down_full))[0].astype(BF)
    up_bias_part = jnp.sum(grad_hidden, axis=0, dtype=F32)
    up_grad = product("td,tf->df", normed_two, grad_hidden).astype(BF)
    grad_normed_two = product("tf,df->td", grad_hidden, up_full)
    grad_middle, gain_two_part, shift_two_part = norm_back(
        grad_normed_two, two_hat, two_rstd, gain_two
    )
    grad_middle = grad_two + grad_middle
    grad_branch = grad_middle.astype(BF)
    out_bias_part = jnp.sum(grad_branch, axis=0, dtype=F32)
    out_grad = product("td,ct->dc", grad_branch, flat).astype(BF)
    early = jnp.stack([out_bias_part, gain_two_part, shift_two_part, down_bias_part], axis=1)
    up_scattered = lax.psum_scatter(
        jnp.concatenate([up_grad, out_grad, early.astype(BF)], axis=1),
        "fsdp",
        scatter_dimension=0,
        tiled=True,
    )

    grad_attended = product("td,dc->ct", grad_branch, out_full).astype(BF)
    grad_attended = grad_attended * valid.astype(BF)
    grad_heads = grad_attended.reshape(heads, HEAD_DIM, here)
    delta = jnp.sum(grad_heads.astype(F32) * attended.astype(F32), axis=1)
    g_added = jnp.concatenate(
        [
            jnp.moveaxis(split3(-delta), 0, 1),
            jnp.zeros((heads, AUG - 3, here), F32),
        ],
        axis=1,
    )
    g_aug = widen(grad_attended, g_added)
    q_added = jnp.concatenate(
        [
            jnp.broadcast_to(q_mask, (heads, pics + 1, here)),
            jnp.moveaxis(split3(-log_total[:, 0]), 0, 1),
            jnp.zeros((heads, spare, here), F32),
        ],
        axis=1,
    )
    q_aug_back = widen(queries, q_added)
    dq, dk, dv = attend_back(
        q_aug_back, k_aug, v_aug, g_aug, counts, indices, q_block, k_block, group
    )
    dq = dq.reshape(hh, here)
    dkv = jnp.concatenate([dk.reshape(hh, k_len), dv.reshape(hh, k_len)], axis=0)
    query_grad = product("td,ct->dc", normed, dq).astype(BF)
    kv_grad = product("td,ct->dc", normed_all, dkv).astype(BF)
    qkv_scattered = lax.psum_scatter(
        jnp.concatenate([query_grad, kv_grad], axis=1), "fsdp", scatter_dimension=0, tiled=True
    )
    query_bias_part = jnp.sum(dq, axis=1, dtype=F32)
    value_bias_part = jnp.sum(dv.reshape(hh, k_len), axis=1, dtype=F32)

    grad_slots = product("ct,dc->td", dkv, kv_full)
    own_share = grad_slots[:here] + product("ct,dc->td", dq, query_full)
    to_after = [None] * (reach + 1)
    to_before = [None] * (reach + 1)
    for position, (j, use_after, use_before) in enumerate(slots):
        share = grad_slots[(position + 1) * here : (position + 2) * here].astype(BF)
        zero = jnp.zeros_like(share)
        if use_after:
            to_after[j] = jnp.where(me + j < n, share, zero)
        if use_before:
            to_before[n - j] = jnp.where(me + j >= n, share, zero)
    moving_right = to_after[reach]
    moving_left = to_before[reach]
    for distance in reversed(range(1, reach + 1)):
        moving_right = lax.ppermute(moving_right, "tp", to_right).astype(F32)
        moving_left = lax.ppermute(moving_left, "tp", to_left).astype(F32)
        if distance > 1:
            moving_right = (moving_right + to_after[distance - 1].astype(F32)).astype(BF)
            moving_left = (moving_left + to_before[distance - 1].astype(F32)).astype(BF)
    grad_normed = own_share + moving_right + moving_left
    one_hat, one_rstd = xhat_of(x)
    grad_x, gain_one_part, shift_one_part = norm_back(grad_normed, one_hat, one_rstd, gain_one)
    input_grad = grad_middle + grad_x

    def owned(scattered, start, size):
        return ring_reduce(
            [scattered[:, start + s * size : start + (s + 1) * size] for s in range(n)]
        )

    down_weight_grad = owned(down_scattered, 0, units)
    up_slots_grad = [
        jnp.concatenate(
            [
                up_scattered[:, s * units : (s + 1) * units],
                up_scattered[:, n * units + s * cols : n * units + (s + 1) * cols],
            ],
            axis=1,
        )
        for s in range(n)
    ]
    up_out = ring_reduce(up_slots_grad)
    up_weight_grad, out_weight_grad = up_out[:, :units], up_out[:, units:]
    qkv_slots_grad = [
        jnp.concatenate(
            [
                qkv_scattered[:, t * hh + s * cols : t * hh + (s + 1) * cols]
                for t in range(3)
            ],
            axis=1,
        )
        for s in range(n)
    ]
    qkv_out = ring_reduce(qkv_slots_grad)
    early_sums = sum(
        s.astype(F32) for s in ring_gather(up_scattered[:, n * units + hh :].astype(F32), n)
    )

    vector_part = jnp.concatenate([gain_one_part, shift_one_part])
    bias_parts = [
        jnp.concatenate(
            [
                query_bias_part[s * cols : (s + 1) * cols],
                value_bias_part[s * cols : (s + 1) * cols],
                up_bias_part[s * units : (s + 1) * units],
            ]
        )
        for s in range(n)
    ]
    ring = [(i, (i - 1) % n) for i in range(n)]
    carried, vector_sum, passing = bias_parts[-1], vector_part, vector_part
    for s in reversed(range(n - 1)):
        moved = lax.ppermute(jnp.concatenate([carried, passing]), "tp", ring)
        carried = moved[: carried.shape[0]] + bias_parts[s]
        passing = moved[carried.shape[0] :]
        vector_sum = vector_sum + passing
    small = lax.psum(jnp.concatenate([carried, vector_sum]), "fsdp")
    bias_size = carried.shape[0]
    share = width // lax.axis_size("fsdp")
    f = lax.axis_index("fsdp")
    ln1_gain_grad = lax.dynamic_slice_in_dim(small, bias_size + f * share, share, 0)
    ln1_bias_grad = lax.dynamic_slice_in_dim(small, bias_size + width + f * share, share, 0)
    return (
        activations_out[None],
        input_grad[None],
        ln1_gain_grad[None],
        ln1_bias_grad[None],
        qkv_out[None, :, :cols],
        small[None, :cols],
        qkv_out[None, :, cols : 2 * cols],
        qkv_out[None, :, 2 * cols :],
        small[None, cols : 2 * cols],
        out_weight_grad[None],
        early_sums[None, :, 0],
        early_sums[None, :, 1],
        early_sums[None, :, 2],
        up_weight_grad[None],
        small[None, 2 * cols : bias_size],
        down_weight_grad[None],
        early_sums[None, :, 3],
    )


def solution(mesh):
    token = P("fsdp", "tp", None)
    vector, shift, matrix = P(None, "fsdp"), P(None, "tp"), P(None, "fsdp", "tp")
    in_specs = (
        token,
        P("fsdp", None),
        token,
        vector,
        vector,
        matrix,
        shift,
        matrix,
        matrix,
        shift,
        matrix,
        vector,
        vector,
        vector,
        matrix,
        shift,
        matrix,
        vector,
    )
    out_specs = (
        token,
        token,
        vector,
        vector,
        matrix,
        shift,
        matrix,
        matrix,
        shift,
        matrix,
        vector,
        vector,
        vector,
        matrix,
        shift,
        matrix,
        vector,
    )
    return jax.shard_map(local, mesh=mesh, in_specs=in_specs, out_specs=out_specs, check_vma=False)
```

time: 1260 us -> 764 us (0.61)
  the two profiles are of different devices: /device:TPU:0 before, /device:TPU:30 now
where the time goes in v1:
time: 764 us; the launch traced here: 750 us
  local copies, waits for them, and re-layouts  164 us (21%)
  matrix products  164 us (21%)
  starting transfers between devices  145 us (19%)
  waiting for transfers between devices  115 us (15%)
  other arithmetic  74.5 us (10%)
  Pallas kernels  38.3 us (5%)
  blocking collectives  33.3 us (4%)
  between operations  15.7 us (2%)
    dot_general x15, matrix products, product(): return jnp.einsum(form, left, right, preferred_element_type=F32)  164 us
    ppermute x2, starting transfers between devices, local(): moving_left = lax.ppermute(moving_left, 'tp', to_left).astype(F32)  70.6 us
    ppermute x15, waiting for transfers between devices, ring_gather(): slots.append(lax.ppermute(slots[-1], 'tp', ring))  59 us
    concatenate x1, local copies, waits for them, and re-layouts, local(): jnp.concatenate([up_grad, out_grad, early.astype(BF)], axis=1)  54.2 us
    ppermute x15, starting transfers between devices, ring_gather(): slots.append(lax.ppermute(slots[-1], 'tp', ring))  45.2 us
    ppermute x9, waiting for transfers between devices, ring_reduce(): total = lax.ppermute(total, 'tp', ring)  45 us
    psum x1, blocking collectives, local(): small = lax.psum(jnp.concatenate([carried, vector_sum]), 'fsdp')  33.3 us
    unnamed x166, local copies, waits for them, and re-layouts  31.8 us
  transfers between devices with their start and end apart: 41, of which 22 were waited for; matrix products, arithmetic and copies ran while one was open for 42% of the time, Pallas kernels for 2%

profile of v1, /device:TPU:30, one launch (start us, length us, event | category | flops | bytes accessed | tf_op | source)
XLA Modules:
  0.0 750.5 jit_solution(1322337299055591031)
XLA Ops:
  11.7 6.6 collective-permute-done
  22.6 4.4 collective-permute-done.1
  31.2 5.0 collective-permute-done.2
  36.4 4.7 concatenate.159
  41.3 4.3 collective-permute-start.10
  45.6 4.6 collective-permute-done.10
  54.5 5.3 collective-permute-done.11
  64.1 4.6 collective-permute-done.12
  75.3 7.6 %collective-permute-done.13 = bf16[144,1076]{1,0:T(8,128)(2,1)S(1)} collective-permute-done((bf16[144,1076]{1,0:T(8,128)(2,1)S(1)}, bf16[144,1076]{1,0:T(8,128)(2,1)S(1)}, u32[]{:S(2)}, u32[]{:S(2)}) %collective-permute-start.13) | collective-permute-done | bytes 309920 | tf_op jit(solution)/shard_map/ppermute | solution.py:51
  87.2 7.6 %collective-permute-done.14 = bf16[144,1076]{1,0:T(8,128)(2,1)S(1)} collective-permute-done((bf16[144,1076]{1,0:T(8,128)(2,1)S(1)}, bf16[144,1076]{1,0:T(8,128)(2,1)S(1)}, u32[]{:S(2)}, u32[]{:S(2)}) %collective-permute-start.14) | collective-permute-done | bytes 309920 | tf_op jit(solution)/shard_map/ppermute | solution.py:51
  99.1 6.1 collective-permute-done.15
  108.6 4.6 collective-permute-start.3
  137.0 5.6 collective-permute-start.4
  148.7 7.1 collective-permute-done.8
  155.8 4.4 collective-permute-start.9
  178.8 6.3 fusion.5
  185.2 5.2 multiply_convert_fusion.1
  191.2 17.6 %add_convert_fusion = bf16[2304,2048]{1,0:T(8,128)(2,1)} fusion(bf16[2048,1152]{1,0:T(8,128)(2,1)S(1)} %fusion.5, f32[2304]{0:T(1024)S(1)} %copy-done.64, bf16[1152,4614]{1,0:T(8,128)(2,1)} %all-gather.4.cloned.1.call-done), kind=kOutput, calls=%fused_computation.2 | convolution fusion | flops 10881073152 | bytes 19473408 | tf_op jit(solution)/shard_map/td,dc->ct/dot_general | solution.py:37
  208.8 7.5 fusion.71
  220.1 16.6 %attend.1 = (bf16[16,72,512]{2,1,0:T(8,128)(2,1)S(1)}, f32[16,1,512]{2,1,0:T(1,128)S(1)}) custom-call(s32[2]{0:T(128)S(1)} %convert_reduce_fusion.6.count_ref, s32[16]{0:T(128)S(1)} %reshape.294.index_ref, bf16[16,80,512]{2,1,0:T(8,128)(2,1)S(1)} %pad_maximum_fusion.7.q_ref, bf16[16,80,2048]{2,1,0:T(8,128)(2,1)S(1)} %get-tuple-element.215.k_ref, ...), custom_call_target="tpu_custom_call" | custom-call | flops 5368709120 | bytes 13107200 | tf_op jit(solution)/shard_map/attend/pallas_call | solution.py:111
  243.6 12.2 %convolution_add_fusion = f32[512,4304]{0,1:T(8,128)} fusion(bf16[1152,4304]{1,0:T(8,128)(2,1)} %all-gather.6.cloned.1.call-done, f32[4304]{0:T(1024)} %concatenate.177, f32[512,1152]{1,0:T(8,128)} %copy-done.9, f32[1152]{0:T(1024)} %get-tuple-element.122, f32[1152]{0:T(1024)} %get-tuple-element.120, f32[512]{0:T(512)} %add_rsqrt_fusion.2, ...), kind=kOutput, calls=%fused_computation.26 | convolution fusion | flops 5082357760 | bytes 21120832 | tf_op jit(solution)/shard_map/td,df->tf/dot_general | solution.py:37
  255.8 18.4 %convert_reduce_fusion.2 = (f32[4304]{0:T(1024)}, bf16[512,4304]{0,1:T(8,128)(2,1)}) fusion(f32[512,4304]{0,1:T(8,128)} %convolution_add_fusion, bf16[1152,4304]{1,0:T(8,128)(2,1)} %all-gather.8.cloned.1.call-done, bf16[1,512,1152]{2,1,0:T(8,128)(2,1)S(1)} %copy-done.19, f32[512]{0:T(512)S(1)} %compare_convert_fusion), kind=kOutput, calls=%fused_computation.23 | convolution fusion | flops 5127450624 | bytes 24337216 | tf_op jit(solution)/shard_map/td,df->tf/dot_general | solution.py:37
  274.3 12.6 %multiply_reduce_fusion = (bf16[1152]{0:T(1024)(128)(2,1)}, f32[512]{0:T(512)S(1)}, f32[512]{0:T(512)S(1)}, bf16[1152]{0:T(1024)(128)(2,1)}, f32[512,1152]{1,0:T(8,128)S(1)}) fusion(f32[512,1152]{1,0:T(8,128)} %copy-done.9, f32[512]{0:T(512)} %add_rsqrt_fusion.2, f32[512]{0:T(512)S(1)} %broadcast_multiply_fusion.6, f32[1152]{0:T(1024)} %get-tuple-element.120, ...), kind=kOutput, calls=%fused_computation.66 | convolution fusion | flops 5082510336 | bytes 19059712 | tf_op jit(solution)/shard_map/tf,df->td/dot_general | solution.py:37
  289.0 4.4 fusion.19
  295.1 21.7 %attend_back.1 = (bf16[16,72,512]{2,1,0:T(8,128)(2,1)S(1)}, bf16[16,72,2048]{2,1,0:T(8,128)(2,1)S(1)}, bf16[16,72,2048]{2,1,0:T(8,128)(2,1)S(1)}) custom-call(s32[2]{0:T(128)S(1)} %convert_reduce_fusion.6.count_ref, s32[16]{0:T(128)S(1)} %reshape.294.index_ref, bf16[16,80,512]{2,1,0:T(8,128)(2,1)S(1)} %maximum_maximum_fusion.q_ref, ...), custom_call_target="tpu_custom_call" | custom-call | flops 13421772800 | bytes 26214400 | tf_op jit(solution)/shard_map/attend_back/pallas_call | solution.py:194
  321.2 4.5 convolution_convert_fusion.4
  325.7 5.2 copy.83
  331.0 16.7 %convolution_convert_fusion.2 = bf16[1152,2304]{1,0:T(8,128)(2,1)} fusion(bf16[2048,1152]{1,0:T(8,128)(2,1)} %copy-done.15, bf16[1152,2048]{1,0:T(8,128)(2,1)} %bitcast.110, bf16[1152,2048]{1,0:T(8,128)(2,1)} %bitcast.119), kind=kOutput, calls=%fused_computation.7 | convolution fusion | flops 10893164544 | bytes 19464192 | tf_op jit(solution)/shard_map/td,ct->dc/dot_general | solution.py:37
  347.6 7.1 pad_maximum_fusion.1
  354.8 11.6 %convolution_convert_fusion.1 = bf16[1152,4304]{1,0:T(8,128)(2,1)} fusion(bf16[1,512,1152]{2,1,0:T(8,128)(2,1)} %param.20, f32[512]{0:T(512)S(1)} %compare_convert_fusion, f32[512,4304]{0,1:T(8,128)} %convolution_add_fusion), kind=kOutput, calls=%fused_computation.1 | convolution fusion | flops 5103765504 | bytes 19912704 | tf_op jit(solution)/shard_map/td,tf->df/dot_general | solution.py:37
  370.2 5.1 convolution_convert_fusion.3
  375.4 12.1 %convolution_convert_fusion = bf16[1152,4304]{0,1:T(8,128)(2,1)} fusion(bf16[512,4304]{0,1:T(8,128)(2,1)} %get-tuple-element.211, f32[512,1152]{1,0:T(8,128)S(1)} %copy-done.11, f32[1152]{0:T(1024)S(1)} %copy-done.66, f32[1152]{0:T(1024)S(1)} %copy-done.50, f32[512]{0:T(512)S(1)} %copy-done.71, f32[512]{0:T(512)S(1)} %broadcast_multiply_fusion.6), kind=kOutput, calls=%fused_computation | convolution fusion | flops 5085112320 | bytes 16696320 | tf_op jit(solution)/shard_map/td,tf->df/dot_general | solution.py:37
  387.5 54.2 %concatenate.197 = bf16[1152,5460]{0,1:T(8,128)(2,1)} concatenate(bf16[1152,4304]{0,1:T(8,128)(2,1)} %convolution_convert_fusion, bf16[1152,1152]{0,1:T(8,128)(2,1)} %convolution_convert_fusion.3, bf16[1152,1]{0,1:T(2,128)(2,1)S(1)} %copy-done.52, bf16[1152,1]{0,1:T(2,128)(2,1)S(1)} %copy-done.51, bf16[1152,1]{0,1:T(2,128)(2,1)S(1)} %copy-done.54, bf16[1152,1]{0,1:T(2,128)(2,1)S(1)} %copy-done.53), dimensions={1} | concatenate | bytes 25159680 | tf_op jit(solution)/shard_map/concatenate | solution.py:394
  441.7 18.5 %copy.92 = bf16[1152,5460]{1,0:T(8,128)(2,1)} copy(bf16[1152,5460]{0,1:T(8,128)(2,1)} %concatenate.197) | data formatting | bytes 25159680
  462.1 20.3 %fusion.87 = (bf16[2048,1152]{1,0:T(8,128)(2,1)}, f32[2048,1152]{1,0:T(8,128)}) fusion(bf16[1152,4614]{1,0:T(8,128)(2,1)} %all-gather.4.cloned.1.call-done, bf16[1152,2048]{1,0:T(8,128)(2,1)} %bitcast.111, bf16[1152,2048]{1,0:T(8,128)(2,1)} %bitcast.120), kind=kOutput, calls=%fused_computation.209 | convolution fusion | flops 10892869632 | bytes 28901376 | tf_op jit(solution)/shard_map/ct,dc->td/dot_general | solution.py:37
  486.3 43.5 %collective-permute-start.18 = (bf16[512,1152]{1,0:T(8,128)(2,1)S(1)}, bf16[512,1152]{1,0:T(8,128)(2,1)}, u32[]{:S(2)}, u32[]{:S(2)}) collective-permute-start(bf16[512,1152]{1,0:T(8,128)(2,1)S(1)} %get-tuple-element.135), channel_id=1, source_target_pairs={{1,0},{2,1},{3,2},{5,4},{6,5},{7,6},{9,8},{10,9},{11,10},{13,12},{... | collective-permute-start | bytes 3538952 | tf_op jit(solution)/shard_map/ppermute | solution.py:449
  548.2 27.1 %collective-permute-start.19 = (bf16[512,1152]{1,0:T(8,128)(2,1)S(1)}, bf16[512,1152]{1,0:T(8,128)(2,1)S(1)}, u32[]{:S(2)}, u32[]{:S(2)}) collective-permute-start(bf16[512,1152]{1,0:T(8,128)(2,1)S(1)} %get-tuple-element.133), channel_id=1, source_target_pairs={{1,0},{2,1},{3,2},{5,4},{6,5},{7,6},{9,8},{10,9},{11,10},{13,12},{... | collective-permute-start | bytes 3538952 | tf_op jit(solution)/shard_map/ppermute | solution.py:449
  575.4 13.0 %fusion.25 = bf16[1,512,1152]{2,1,0:T(8,128)(2,1)} fusion(f32[512,1152]{1,0:T(8,128)S(1)} %copy-done.12, bf16[1152,4304]{1,0:T(8,128)(2,1)} %all-gather.8.cloned.1.call-done, f32[512]{0:T(512)S(1)} %compare_convert_fusion, f32[1152]{0:T(1024)S(1)} %copy-done.65, f32[512,4304]{0,1:T(8,128)} %convolution_add_fusion), kind=kOutput, calls=%fused_computation.50 | convolution fusion | flops 5099397120 | bytes 22276608 | tf_op jit(solution)/shard_map/tf,df->td/dot_general | solution.py:37
  588.8 6.8 fusion.32
  597.2 10.0 %collective-permute-start.20 = (f32[3956]{0:T(1024)}, f32[3956]{0:T(1024)S(1)}, u32[]{:S(2)}, u32[]{:S(2)}) collective-permute-start(f32[3956]{0:T(1024)} %concatenate.184), channel_id=1, source_target_pairs={{0,3},{1,0},{2,1},{3,2},{4,7},{5,4},{6,5},{7,6},{8,11},{9,8},{10,9... | collective-permute-start | bytes 47480 | tf_op jit(solution)/shard_map/ppermute | solution.py:505
  608.4 6.0 collective-permute-done.20
  635.7 33.3 %psum.7 = f32[3956]{0:T(1024)S(1)} all-reduce(f32[3956]{0:T(1024)S(1)} %pad_maximum_fusion.12), channel_id=1, replica_groups=mesh['fsdp'=8,'tp'=4] {'fsdp'}, use_global_device_ids=true, to_apply=%region_24.25 | all-reduce | flops 3956 | bytes 31648 | tf_op jit(solution)/shard_map/psum | solution.py:509
  677.2 4.5 collective-permute-done.25
  682.9 6.0 collective-permute-done.32
  706.8 8.1 %collective-permute-done.26 = bf16[144,1364]{1,0:T(8,128)(2,1)S(1)} collective-permute-done((bf16[144,1364]{1,0:T(8,128)(2,1)}, bf16[144,1364]{1,0:T(8,128)(2,1)S(1)}, u32[]{:S(2)}, u32[]{:S(2)}) %collective-permute-start.26) | collective-permute-done | bytes 392864 | tf_op jit(solution)/shard_map/ppermute | solution.py:60
  716.8 5.2 collective-permute-done.34
  723.3 6.0 collective-permute-done.27
  730.2 10.7 %collective-permute-done.28 = bf16[144,1364]{1,0:T(8,128)(2,1)S(1)} collective-permute-done((bf16[144,1364]{1,0:T(8,128)(2,1)S(1)}, bf16[144,1364]{1,0:T(8,128)(2,1)S(1)}, u32[]{:S(2)}, u32[]{:S(2)}) %collective-permute-start.28) | collective-permute-done | bytes 392864 | tf_op jit(solution)/shard_map/ppermute | solution.py:60
  (395 shorter events, 194.1 us)
Async XLA Ops:
  7.2 168.6 %all-gather.4.cloned.1.call-start = ((), (), s32[]{:S(2)}) async-start(), calls=%async_computation.3 | async-start | bytes 12275712 | tf_op jit(solution)/shard_map/all_gather | solution.py:328
  8.7 9.6 %collective-permute-start = (bf16[144,1152]{1,0:T(8,128)(2,1)S(1)}, bf16[144,1152]{1,0:T(8,128)(2,1)S(1)}, u32[]{:S(2)}, u32[]{:S(2)}) collective-permute-start(bf16[144,1152]{1,0:T(8,128)(2,1)S(1)} %concatenate.158), channel_id=1, source_target_pairs={{0,1},{1,2},{2,3},{3,0},{4,5},{5,6},{6,7},{7,4},{8,9},{9,10},{10,1... | collective-permute-start | bytes 995336 | tf_op jit(solution)/shard_map/ppermute | solution.py:51
  18.3 8.7 %collective-permute-start.1 = (bf16[144,1152]{1,0:T(8,128)(2,1)S(1)}, bf16[144,1152]{1,0:T(8,128)(2,1)S(1)}, u32[]{:S(2)}, u32[]{:S(2)}) collective-permute-start(bf16[144,1152]{1,0:T(8,128)(2,1)S(1)} %collective-permute-done), channel_id=1, source_target_pairs={{0,1},{1,2},{2,3},{3,0},{4,5},{5,6},{6,7},{7,4},{8,9},{9,10},{10,1... | collective-permute-start | bytes 995336 | tf_op jit(solution)/shard_map/ppermute | solution.py:51
  26.9 9.3 %collective-permute-start.2 = (bf16[144,1152]{1,0:T(8,128)(2,1)S(1)}, bf16[144,1152]{1,0:T(8,128)(2,1)S(1)}, u32[]{:S(2)}, u32[]{:S(2)}) collective-permute-start(bf16[144,1152]{1,0:T(8,128)(2,1)S(1)} %collective-permute-done.1), channel_id=1, source_target_pairs={{0,1},{1,2},{2,3},{3,0},{4,5},{5,6},{6,7},{7,4},{8,9},{9,10},{10,1... | collective-permute-start | bytes 995336 | tf_op jit(solution)/shard_map/ppermute | solution.py:51
  41.2 202.4 %all-gather.6.cloned.1.call-start = ((), (), s32[]{:S(2)}) async-start(), calls=%async_computation.4 | async-start | bytes 11280384 | tf_op jit(solution)/shard_map/all_gather | solution.py:330
  41.3 9.0 %collective-permute-start.10 = (bf16[144,1076]{1,0:T(8,128)(2,1)S(1)}, bf16[144,1076]{1,0:T(8,128)(2,1)S(1)}, u32[]{:S(2)}, u32[]{:S(2)}) collective-permute-start(bf16[144,1076]{1,0:T(8,128)(2,1)S(1)} %bitcast.140), channel_id=1, source_target_pairs={{0,1},{1,2},{2,3},{3,0},{4,5},{5,6},{6,7},{7,4},{8,9},{9,10},{10,1... | collective-permute-start | bytes 929672 | tf_op jit(solution)/shard_map/ppermute | solution.py:51
  50.2 9.6 %collective-permute-start.11 = (bf16[144,1076]{1,0:T(8,128)(2,1)S(1)}, bf16[144,1076]{1,0:T(8,128)(2,1)S(1)}, u32[]{:S(2)}, u32[]{:S(2)}) collective-permute-start(bf16[144,1076]{1,0:T(8,128)(2,1)S(1)} %collective-permute-done.10), channel_id=1, source_target_pairs={{0,1},{1,2},{2,3},{3,0},{4,5},{5,6},{6,7},{7,4},{8,9},{9,10},{10,1... | collective-permute-start | bytes 929672 | tf_op jit(solution)/shard_map/ppermute | solution.py:51
  59.8 8.9 %collective-permute-start.12 = (bf16[144,1076]{1,0:T(8,128)(2,1)S(1)}, bf16[144,1076]{1,0:T(8,128)(2,1)S(1)}, u32[]{:S(2)}, u32[]{:S(2)}) collective-permute-start(bf16[144,1076]{1,0:T(8,128)(2,1)S(1)} %collective-permute-done.11), channel_id=1, source_target_pairs={{0,1},{1,2},{2,3},{3,0},{4,5},{5,6},{6,7},{7,4},{8,9},{9,10},{10,1... | collective-permute-start | bytes 929672 | tf_op jit(solution)/shard_map/ppermute | solution.py:51
  70.9 36.5 %copy-start.4 = (bf16[1,512,1152]{2,1,0:T(8,128)(2,1)S(1)}, bf16[1,512,1152]{2,1,0:T(8,128)(2,1)}, u32[]{:S(2)}) copy-start(bf16[1,512,1152]{2,1,0:T(8,128)(2,1)} %param.18) | copy-start | bytes 3538948
  70.9 184.9 %all-gather.8.cloned.1.call-start = ((), (), s32[]{:S(2)}) async-start(), calls=%async_computation.5 | async-start | bytes 11280384 | tf_op jit(solution)/shard_map/all_gather | solution.py:332
  71.0 12.0 %collective-permute-start.13 = (bf16[144,1076]{1,0:T(8,128)(2,1)S(1)}, bf16[144,1076]{1,0:T(8,128)(2,1)S(1)}, u32[]{:S(2)}, u32[]{:S(2)}) collective-permute-start(bf16[144,1076]{1,0:T(8,128)(2,1)S(1)} %bitcast.142), channel_id=1, source_target_pairs={{0,1},{1,2},{2,3},{3,0},{4,5},{5,6},{6,7},{7,4},{8,9},{9,10},{10,1... | collective-permute-start | bytes 929672 | tf_op jit(solution)/shard_map/ppermute | solution.py:51
  82.9 11.9 %collective-permute-start.14 = (bf16[144,1076]{1,0:T(8,128)(2,1)S(1)}, bf16[144,1076]{1,0:T(8,128)(2,1)S(1)}, u32[]{:S(2)}, u32[]{:S(2)}) collective-permute-start(bf16[144,1076]{1,0:T(8,128)(2,1)S(1)} %collective-permute-done.13), channel_id=1, source_target_pairs={{0,1},{1,2},{2,3},{3,0},{4,5},{5,6},{6,7},{7,4},{8,9},{9,10},{10,1... | collective-permute-start | bytes 929672 | tf_op jit(solution)/shard_map/ppermute | solution.py:51
  94.8 10.3 %collective-permute-start.15 = (bf16[144,1076]{1,0:T(8,128)(2,1)S(1)}, bf16[144,1076]{1,0:T(8,128)(2,1)S(1)}, u32[]{:S(2)}, u32[]{:S(2)}) collective-permute-start(bf16[144,1076]{1,0:T(8,128)(2,1)S(1)} %collective-permute-done.14), channel_id=1, source_target_pairs={{0,1},{1,2},{2,3},{3,0},{4,5},{5,6},{6,7},{7,4},{8,9},{9,10},{10,1... | collective-permute-start | bytes 929672 | tf_op jit(solution)/shard_map/ppermute | solution.py:51
  107.3 516.0 %reduce-scatter.6.cloned.1.call-start = ((), (), s32[]{:S(2)}) async-start(), calls=%async_computation.6 | async-start | bytes 8957952 | tf_op jit(solution)/shard_map/reduce_scatter | solution.py:428
  107.3 28.3 %collective-permute-start.5 = (bf16[512,1152]{1,0:T(8,128)(2,1)S(1)}, bf16[512,1152]{1,0:T(8,128)(2,1)S(1)}, u32[]{:S(2)}, u32[]{:S(2)}) collective-permute-start(bf16[512,1152]{1,0:T(8,128)(2,1)S(1)} %bitcast.121), channel_id=1, source_target_pairs={{0,1},{1,2},{2,3},{4,5},{5,6},{6,7},{8,9},{9,10},{10,11},{12,13},{... | collective-permute-start | bytes 3538952 | tf_op jit(solution)/shard_map/ppermute | solution.py:259
  108.6 28.3 %collective-permute-start.3 = (bf16[512,1152]{1,0:T(8,128)(2,1)S(1)}, bf16[512,1152]{1,0:T(8,128)(2,1)S(1)}, u32[]{:S(2)}, u32[]{:S(2)}) collective-permute-start(bf16[512,1152]{1,0:T(8,128)(2,1)S(1)} %bitcast.122), channel_id=1, source_target_pairs={{1,0},{2,1},{3,2},{5,4},{6,5},{7,6},{9,8},{10,9},{11,10},{13,12},{... | collective-permute-start | bytes 3538952 | tf_op jit(solution)/shard_map/ppermute | solution.py:258
  116.1 30.0 %collective-permute-start.7 = (f32[1652]{0:T(1024)}, f32[1652]{0:T(1024)}, u32[]{:S(2)}, u32[]{:S(2)}) collective-permute-start(f32[1652]{0:T(1024)} %concatenate.161), channel_id=1, source_target_pairs={{0,1},{1,2},{2,3},{3,0},{4,5},{5,6},{6,7},{7,4},{8,9},{9,10},{10,1... | collective-permute-start | bytes 19832 | tf_op jit(solution)/shard_map/ppermute | solution.py:51
  135.6 36.3 %copy-start.5 = (bf16[512,1152]{1,0:T(8,128)(2,1)}, bf16[512,1152]{1,0:T(8,128)(2,1)S(1)}, u32[]{:S(2)}) copy-start(bf16[512,1152]{1,0:T(8,128)(2,1)S(1)} %collective-permute-done.5) | copy-start | bytes 3538948
  135.6 33.4 %collective-permute-start.6 = (bf16[512,1152]{1,0:T(8,128)(2,1)S(1)}, bf16[512,1152]{1,0:T(8,128)(2,1)}, u32[]{:S(2)}, u32[]{:S(2)}) collective-permute-start(bf16[512,1152]{1,0:T(8,128)(2,1)S(1)} %collective-permute-done.5), channel_id=1, source_target_pairs={{0,1},{1,2},{2,3},{4,5},{5,6},{6,7},{8,9},{9,10},{10,11},{12,13},{... | collective-permute-start | bytes 3538952 | tf_op jit(solution)/shard_map/ppermute | solution.py:259
  137.0 32.1 %collective-permute-start.4 = (bf16[512,1152]{1,0:T(8,128)(2,1)S(1)}, bf16[512,1152]{1,0:T(8,128)(2,1)}, u32[]{:S(2)}, u32[]{:S(2)}) collective-permute-start(bf16[512,1152]{1,0:T(8,128)(2,1)S(1)} %collective-permute-done.3), channel_id=1, source_target_pairs={{1,0},{2,1},{3,2},{5,4},{6,5},{7,6},{9,8},{10,9},{11,10},{13,12},{... | collective-permute-start | bytes 3538952 | tf_op jit(solution)/shard_map/ppermute | solution.py:258
  146.0 9.8 %collective-permute-start.8 = (f32[1652]{0:T(1024)}, f32[1652]{0:T(1024)S(1)}, u32[]{:S(2)}, u32[]{:S(2)}) collective-permute-start(f32[1652]{0:T(1024)} %collective-permute-done.7), channel_id=1, source_target_pairs={{0,1},{1,2},{2,3},{3,0},{4,5},{5,6},{6,7},{7,4},{8,9},{9,10},{10,1... | collective-permute-start | bytes 19832 | tf_op jit(solution)/shard_map/ppermute | solution.py:51
  155.8 5.8 collective-permute-start.9
  354.7 320.2 %reduce-scatter.8.cloned.1.call-start = ((), (), s32[]{:S(2)}) async-start(), calls=%async_computation.7 | async-start | bytes 11280384 | tf_op jit(solution)/shard_map/reduce_scatter | solution.py:380
  366.4 323.5 %reduce-scatter.10.cloned.1.call-start = ((), (), s32[]{:S(2)}) async-start(), calls=%async_computation.8 | async-start | bytes 14266368 | tf_op jit(solution)/shard_map/reduce_scatter | solution.py:393
  461.5 68.3 %slice-start = ((s8[4718592]{0:T(1024)(128)(4,1)}), s8[4194304]{0:T(1024)(128)(4,1)S(1)}, s32[]{:S(2)}) async-start(s8[4718592]{0:T(1024)(128)(4,1)} %bitcast.112), calls=%async_computation.9 | async-start | bytes 8388608
  462.1 67.7 %slice-start.1 = ((s8[4718592]{0:T(1024)(128)(4,1)}), s8[524288]{0:T(1024)(128)(4,1)S(1)}, s32[]{:S(2)}) async-start(s8[4718592]{0:T(1024)(128)(4,1)} %bitcast.112), calls=%async_computation.10 | async-start | bytes 1048576
  485.0 58.7 %collective-permute-start.16 = (bf16[512,1152]{1,0:T(8,128)(2,1)}, bf16[512,1152]{1,0:T(8,128)(2,1)}, u32[]{:S(2)}, u32[]{:S(2)}) collective-permute-start(bf16[512,1152]{1,0:T(8,128)(2,1)} %get-tuple-element.134), channel_id=1, source_target_pairs={{0,1},{1,2},{2,3},{4,5},{5,6},{6,7},{8,9},{9,10},{10,11},{12,13},{... | collective-permute-start | bytes 3538952 | tf_op jit(solution)/shard_map/ppermute | solution.py:448
  486.3 57.5 %collective-permute-start.18 = (bf16[512,1152]{1,0:T(8,128)(2,1)S(1)}, bf16[512,1152]{1,0:T(8,128)(2,1)}, u32[]{:S(2)}, u32[]{:S(2)}) collective-permute-start(bf16[512,1152]{1,0:T(8,128)(2,1)S(1)} %get-tuple-element.135), channel_id=1, source_target_pairs={{1,0},{2,1},{3,2},{5,4},{6,5},{7,6},{9,8},{10,9},{11,10},{13,12},{... | collective-permute-start | bytes 3538952 | tf_op jit(solution)/shard_map/ppermute | solution.py:449
  546.9 41.5 %collective-permute-start.17 = (bf16[512,1152]{1,0:T(8,128)(2,1)S(1)}, bf16[512,1152]{1,0:T(8,128)(2,1)S(1)}, u32[]{:S(2)}, u32[]{:S(2)}) collective-permute-start(bf16[512,1152]{1,0:T(8,128)(2,1)S(1)} %get-tuple-element.132), channel_id=1, source_target_pairs={{0,1},{1,2},{2,3},{4,5},{5,6},{6,7},{8,9},{9,10},{10,11},{12,13},{... | collective-permute-start | bytes 3538952 | tf_op jit(solution)/shard_map/ppermute | solution.py:448
  548.2 40.6 %collective-permute-start.19 = (bf16[512,1152]{1,0:T(8,128)(2,1)S(1)}, bf16[512,1152]{1,0:T(8,128)(2,1)S(1)}, u32[]{:S(2)}, u32[]{:S(2)}) collective-permute-start(bf16[512,1152]{1,0:T(8,128)(2,1)S(1)} %get-tuple-element.133), channel_id=1, source_target_pairs={{1,0},{2,1},{3,2},{5,4},{6,5},{7,6},{9,8},{10,9},{11,10},{13,12},{... | collective-permute-start | bytes 3538952 | tf_op jit(solution)/shard_map/ppermute | solution.py:449
  597.2 17.2 %collective-permute-start.20 = (f32[3956]{0:T(1024)}, f32[3956]{0:T(1024)S(1)}, u32[]{:S(2)}, u32[]{:S(2)}) collective-permute-start(f32[3956]{0:T(1024)} %concatenate.184), channel_id=1, source_target_pairs={{0,3},{1,0},{2,1},{3,2},{4,7},{5,4},{6,5},{7,6},{8,11},{9,8},{10,9... | collective-permute-start | bytes 47480 | tf_op jit(solution)/shard_map/ppermute | solution.py:505
  615.8 5.5 collective-permute-start.21
  623.3 7.2 collective-permute-start.22
  626.5 8.2 %collective-permute-start.23 = (bf16[144,864]{1,0:T(8,128)(2,1)S(1)}, bf16[144,864]{1,0:T(8,128)(2,1)S(1)}, u32[]{:S(2)}, u32[]{:S(2)}) collective-permute-start(bf16[144,864]{1,0:T(8,128)(2,1)S(1)} %pad_maximum_fusion.9), channel_id=1, source_target_pairs={{0,3},{1,0},{2,1},{3,2},{4,7},{5,4},{6,5},{7,6},{8,11},{9,8},{10,9... | collective-permute-start | bytes 746504 | tf_op jit(solution)/shard_map/ppermute | solution.py:60
  630.5 51.3 %copy-start.25 = (bf16[144,288]{1,0:T(8,128)(2,1)S(1)}, bf16[144,288]{1,0:T(8,128)(2,1)}, u32[]{:S(2)}) copy-start(bf16[144,288]{1,0:T(8,128)(2,1)} %get-tuple-element.145) | copy-start | bytes 248836
  630.5 51.3 %copy-start.26 = (bf16[144,288]{1,0:T(8,128)(2,1)S(1)}, bf16[144,288]{1,0:T(8,128)(2,1)}, u32[]{:S(2)}) copy-start(bf16[144,288]{1,0:T(8,128)(2,1)} %get-tuple-element.146) | copy-start | bytes 248836
  630.5 51.3 %copy-start.27 = (bf16[144,288]{1,0:T(8,128)(2,1)S(1)}, bf16[144,288]{1,0:T(8,128)(2,1)}, u32[]{:S(2)}) copy-start(bf16[144,288]{1,0:T(8,128)(2,1)} %get-tuple-element.147) | copy-start | bytes 248836
  634.8 34.8 %collective-permute-start.24 = (bf16[144,864]{1,0:T(8,128)(2,1)S(1)}, bf16[144,864]{1,0:T(8,128)(2,1)S(1)}, u32[]{:S(2)}, u32[]{:S(2)}) collective-permute-start(bf16[144,864]{1,0:T(8,128)(2,1)S(1)} %add_convert_fusion.9), channel_id=1, source_target_pairs={{0,3},{1,0},{2,1},{3,2},{4,7},{5,4},{6,5},{7,6},{8,11},{9,8},{10,9... | collective-permute-start | bytes 746504 | tf_op jit(solution)/shard_map/ppermute | solution.py:60
  670.7 11.0 %collective-permute-start.25 = (bf16[144,864]{1,0:T(8,128)(2,1)S(1)}, bf16[144,864]{1,0:T(8,128)(2,1)S(1)}, u32[]{:S(2)}, u32[]{:S(2)}) collective-permute-start(bf16[144,864]{1,0:T(8,128)(2,1)S(1)} %add_convert_fusion.8), channel_id=1, source_target_pairs={{0,3},{1,0},{2,1},{3,2},{4,7},{5,4},{6,5},{7,6},{8,11},{9,8},{10,9... | collective-permute-start | bytes 746504 | tf_op jit(solution)/shard_map/ppermute | solution.py:60
  676.2 12.7 %collective-permute-start.32 = (bf16[144,1076]{1,0:T(8,128)(2,1)S(1)}, bf16[144,1076]{1,0:T(8,128)(2,1)S(1)}, u32[]{:S(2)}, u32[]{:S(2)}) collective-permute-start(bf16[144,1076]{1,0:T(8,128)(2,1)S(1)} %slice.465), channel_id=1, source_target_pairs={{0,3},{1,0},{2,1},{3,2},{4,7},{5,4},{6,5},{7,6},{8,11},{9,8},{10,9... | collective-permute-start | bytes 929672 | tf_op jit(solution)/shard_map/ppermute | solution.py:60
  689.8 12.0 %collective-permute-start.33 = (bf16[144,1076]{1,0:T(8,128)(2,1)}, bf16[144,1076]{1,0:T(8,128)(2,1)}, u32[]{:S(2)}, u32[]{:S(2)}) collective-permute-start(bf16[144,1076]{1,0:T(8,128)(2,1)} %add_convert_fusion.7), channel_id=1, source_target_pairs={{0,3},{1,0},{2,1},{3,2},{4,7},{5,4},{6,5},{7,6},{8,11},{9,8},{10,9... | collective-permute-start | bytes 929672 | tf_op jit(solution)/shard_map/ppermute | solution.py:60
  690.8 12.2 %collective-permute-start.29 = (f32[144,4]{0,1:T(4,128)S(1)}, f32[144,4]{0,1:T(4,128)S(1)}, u32[]{:S(2)}, u32[]{:S(2)}) collective-permute-start(f32[144,4]{0,1:T(4,128)S(1)} %convert_element_type.263), channel_id=1, source_target_pairs={{0,1},{1,2},{2,3},{3,0},{4,5},{5,6},{6,7},{7,4},{8,9},{9,10},{10,1... | collective-permute-start | bytes 6920 | tf_op jit(solution)/shard_map/ppermute | solution.py:51
  700.5 14.4 %collective-permute-start.26 = (bf16[144,1364]{1,0:T(8,128)(2,1)}, bf16[144,1364]{1,0:T(8,128)(2,1)S(1)}, u32[]{:S(2)}, u32[]{:S(2)}) collective-permute-start(bf16[144,1364]{1,0:T(8,128)(2,1)} %copy.84), channel_id=1, source_target_pairs={{0,3},{1,0},{2,1},{3,2},{4,7},{5,4},{6,5},{7,6},{8,11},{9,8},{10,9... | collective-permute-start | bytes 1178504 | tf_op jit(solution)/shard_map/ppermute | solution.py:60
  702.9 19.1 %collective-permute-start.34 = (bf16[144,1076]{1,0:T(8,128)(2,1)S(1)}, bf16[144,1076]{1,0:T(8,128)(2,1)S(1)}, u32[]{:S(2)}, u32[]{:S(2)}) collective-permute-start(bf16[144,1076]{1,0:T(8,128)(2,1)S(1)} %add_convert_fusion.6), channel_id=1, source_target_pairs={{0,3},{1,0},{2,1},{3,2},{4,7},{5,4},{6,5},{7,6},{8,11},{9,8},{10,9... | collective-permute-start | bytes 929672 | tf_op jit(solution)/shard_map/ppermute | solution.py:60
  703.0 20.3 %collective-permute-start.30 = (f32[144,4]{0,1:T(4,128)S(1)}, f32[144,4]{0,1:T(4,128)S(1)}, u32[]{:S(2)}, u32[]{:S(2)}) collective-permute-start(f32[144,4]{0,1:T(4,128)S(1)} %collective-permute-done.29), channel_id=1, source_target_pairs={{0,1},{1,2},{2,3},{3,0},{4,5},{5,6},{6,7},{7,4},{8,9},{9,10},{10,1... | collective-permute-start | bytes 6920 | tf_op jit(solution)/shard_map/ppermute | solution.py:51
  716.7 12.6 %collective-permute-start.27 = (bf16[144,1364]{1,0:T(8,128)(2,1)}, bf16[144,1364]{1,0:T(8,128)(2,1)S(1)}, u32[]{:S(2)}, u32[]{:S(2)}) collective-permute-start(bf16[144,1364]{1,0:T(8,128)(2,1)} %add_convert_fusion.5), channel_id=1, source_target_pairs={{0,3},{1,0},{2,1},{3,2},{4,7},{5,4},{6,5},{7,6},{8,11},{9,8},{10,9... | collective-permute-start | bytes 1178504 | tf_op jit(solution)/shard_map/ppermute | solution.py:60
  723.3 6.3 collective-permute-start.31
  729.5 11.3 %collective-permute-start.28 = (bf16[144,1364]{1,0:T(8,128)(2,1)S(1)}, bf16[144,1364]{1,0:T(8,128)(2,1)S(1)}, u32[]{:S(2)}, u32[]{:S(2)}) collective-permute-start(bf16[144,1364]{1,0:T(8,128)(2,1)S(1)} %add_convert_fusion.4), channel_id=1, source_target_pairs={{0,3},{1,0},{2,1},{3,2},{4,7},{5,4},{6,5},{7,6},{8,11},{9,8},{10,9... | collective-permute-start | bytes 1178504 | tf_op jit(solution)/shard_map/ppermute | solution.py:60
  (72 other events, 665.2 us)
Sparse Core Ops, SparseCore 0:
  41.3 66.0 all-gather.3
  109.3 61.3 all-gather.5
  172.6 61.3 all-gather.7
  354.9 151.4 reduce-scatter.5
  510.3 79.1 reduce-scatter.7
  592.9 94.0 reduce-scatter.9

commit v2 on v1

v2 whole, which is shorter than its diff:
```python
import functools
import math

import jax
import jax.numpy as jnp
from jax import lax
from jax.experimental import pallas as pl
from jax.experimental.pallas import tpu as pltpu
from jax.sharding import PartitionSpec as P

HEAD_DIM = 72
AUG = 8
PIC_MAX = 1024
MASKED = -1e30
BF = jnp.bfloat16
F32 = jnp.float32


def xhat_of(values):
    center = values - jnp.mean(values, axis=-1, keepdims=True)
    rstd = lax.rsqrt(jnp.mean(center * center, axis=-1, keepdims=True) + 1e-06)
    return center * rstd, rstd


def norm_back(dy, xhat, rstd, gain):
    dxhat = dy * gain
    grad = dxhat - jnp.mean(dxhat, axis=-1, keepdims=True)
    grad = (grad - xhat * jnp.mean(dxhat * xhat, axis=-1, keepdims=True)) * rstd
    return grad, jnp.sum(dy * xhat, axis=0), jnp.sum(dy, axis=0)


def gelu_tanh(values):
    return jax.nn.gelu(values, approximate=True)


def product(form, left, right):
    return jnp.einsum(form, left, right, preferred_element_type=F32)


def split3(values):
    high = lax.reduce_precision(values, 8, 7)
    rest = values - high
    mid = lax.reduce_precision(rest, 8, 7)
    return jnp.stack([high, mid, rest - mid], axis=0)


def after(value, *earlier):
    def kernel(*refs):
        pass

    return pl.pallas_call(
        kernel,
        in_specs=[pl.BlockSpec(memory_space=pl.ANY)] * (1 + len(earlier)),
        out_specs=pl.BlockSpec(memory_space=pl.ANY),
        out_shape=jax.ShapeDtypeStruct(value.shape, value.dtype),
        input_output_aliases={0: 0},
        name="after",
    )(value, *earlier)


def copy_after(value, *earlier):
    def kernel(value_ref, *refs):
        refs[-1][...] = value_ref[...]

    vmem = pl.BlockSpec(memory_space=pltpu.VMEM)
    return pl.pallas_call(
        kernel,
        in_specs=[vmem] + [pl.BlockSpec(memory_space=pl.ANY)] * len(earlier),
        out_specs=vmem,
        out_shape=jax.ShapeDtypeStruct(value.shape, value.dtype),
        name="copy_after",
    )(value, *earlier)


def slots_along_tp(piece, count, *earlier):
    slots = [piece]
    for distance in range(1, count):
        moved = lax.ppermute(piece, "tp", [(i, (i + distance) % count) for i in range(count)])
        slots.append(after(moved, *earlier) if earlier else moved)
    return slots


def by_owner(value, owners, kinds):
    rows, columns = value.shape
    size = columns // (owners * kinds)

    def kernel(value_ref, out_ref):
        for o in range(owners):
            pieces = [
                value_ref[:, (t * owners + o) * size : (t * owners + o + 1) * size]
                for t in range(kinds)
            ]
            out_ref[o] = jnp.concatenate(pieces, axis=1)

    vmem = pl.BlockSpec(memory_space=pltpu.VMEM)
    return pl.pallas_call(
        kernel,
        in_specs=[vmem],
        out_specs=vmem,
        out_shape=jax.ShapeDtypeStruct((owners, rows, kinds * size), value.dtype),
        name="by_owner",
    )(value).reshape(owners * rows, kinds * size)


def norm_kernel(*refs):
    x_refs, gain_ref, shift_ref, out_ref = refs[:-3], refs[-3], refs[-2], refs[-1]
    here, width = x_refs[0].shape
    block = math.gcd(here, 64)
    gain, shift = gain_ref[...], shift_ref[...]
    for position, x_ref in enumerate(x_refs):

        def step(i, carry):
            start = pl.multiple_of(i * block, block)
            values = x_ref[pl.ds(start, block), :].astype(F32)
            center = values - jnp.mean(values, axis=1, keepdims=True)
            spread = jnp.mean(center * center, axis=1, keepdims=True)
            result = center * lax.rsqrt(spread + 1e-06) * gain + shift
            target = pl.multiple_of(position * here + i * block, block)
            out_ref[pl.ds(target, block), :] = result.astype(BF)
            return carry

        lax.fori_loop(0, here // block, step, 0)


def norm_tokens(tokens, gain, shift):
    here, width = tokens[0].shape
    rows = here * len(tokens)
    vmem = pl.BlockSpec(memory_space=pltpu.VMEM)
    return pl.pallas_call(
        norm_kernel,
        in_specs=[vmem] * (len(tokens) + 2),
        out_specs=vmem,
        out_shape=jax.ShapeDtypeStruct((rows, width), BF),
        compiler_params=pltpu.CompilerParams(vmem_limit_bytes=32 << 20),
        cost_estimate=pl.CostEstimate(
            flops=10 * rows * width, bytes_accessed=4 * rows * width, transcendentals=rows
        ),
        name="norm_tokens",
    )(*tokens, gain[None], shift[None])


def attend_kernel(
    count_ref, index_ref, q_ref, k_ref, v_ref, valid_ref, *rest, q_block, k_block, pair
):
    o_ref, lse_ref = rest[-2:]
    heads, rows, q_len = q_ref.shape
    chunks = k_ref.shape[2] // k_block
    dim = rows - AUG
    blocks = q_len // q_block
    jobs = [(b, h) for b in range(blocks) for h in range(heads)]

    def step(t, carry):
        out = []
        for (b, h), (top, acc) in zip(jobs, carry):
            q_part = q_ref[h, :, b * q_block : (b + 1) * q_block]
            starts = [index_ref[b * chunks + t * pair + u] * k_block for u in range(pair)]
            heres = [pl.ds(pl.multiple_of(start, k_block), k_block) for start in starts]
            k_part = jnp.concatenate([k_ref[h, :, here] for here in heres], axis=1)
            v_part = jnp.concatenate([v_ref[h, :, here] for here in heres], axis=1)
            scores = lax.dot_general(
                k_part, q_part, (((0,), (0,)), ((), ())), preferred_element_type=F32
            )
            higher = jnp.maximum(top, jnp.max(scores, axis=0, keepdims=True))
            weights = jnp.exp2(scores - higher).astype(BF)
            acc = acc * jnp.exp2(top - higher) + jnp.dot(
                v_part, weights, preferred_element_type=F32
            )
            out.append((higher, acc))
        return tuple(out)

    first = tuple(
        (jnp.full((1, q_block), MASKED, F32), jnp.zeros((rows, q_block), F32)) for _ in jobs
    )
    final = lax.fori_loop(0, count_ref[0], step, first)
    for (b, h), (top, acc) in zip(jobs, final):
        cols = slice(b * q_block, (b + 1) * q_block)
        live = valid_ref[:, cols] > 0
        total = jnp.where(live, acc[dim : dim + 1], 1.0)
        o_ref[h, :, cols] = jnp.where(live, acc[:dim] / total, 0.0).astype(BF)
        lse_ref[h, :, cols] = jnp.where(live, top + jnp.log2(total), 0.0)


def attend(
    q_aug, k_aug, v_aug, valid, counts, indices, q_block, k_block, pair, group, part, parts, *earlier
):
    heads, rows, q_len = q_aug.shape
    heads = heads // parts
    base = part * (heads // group)
    k_len = k_aug.shape[2]
    dim = rows - AUG
    spec = lambda r, n: pl.BlockSpec((group, r, n), lambda g, *_: (g + base, 0, 0))
    out = lambda r, n: pl.BlockSpec((group, r, n), lambda g, *_: (g, 0, 0))
    return pl.pallas_call(
        functools.partial(attend_kernel, q_block=q_block, k_block=k_block, pair=pair),
        grid_spec=pltpu.PrefetchScalarGridSpec(
            num_scalar_prefetch=2,
            grid=(heads // group,),
            in_specs=[
                spec(rows, q_len),
                spec(rows, k_len),
                spec(rows, k_len),
                pl.BlockSpec((1, q_len), lambda g, *_: (0, 0)),
            ]
            + [pl.BlockSpec(memory_space=pl.ANY)] * len(earlier),
            out_specs=[out(dim, q_len), out(1, q_len)],
        ),
        out_shape=[
            jax.ShapeDtypeStruct((heads, dim, q_len), BF),
            jax.ShapeDtypeStruct((heads, 1, q_len), F32),
        ],
        compiler_params=pltpu.CompilerParams(vmem_limit_bytes=56 << 20),
        cost_estimate=pl.CostEstimate(
            flops=4 * heads * rows * q_len * k_len,
            bytes_accessed=4 * heads * rows * (q_len + k_len),
            transcendentals=heads * q_len * k_len // 2,
        ),
        name="attend",
    )(counts, indices, q_aug, k_aug, v_aug, valid, *earlier)


def attend_back_kernel(
    count_ref, index_ref, q_ref, k_ref, v_ref, g_ref, *rest, q_block, k_block, pair
):
    dq_ref, dkv_ref, dk_acc, dv_acc = rest[-4:]
    heads, rows, q_len = q_ref.shape
    chunks = k_ref.shape[2] // k_block
    dim = rows - AUG
    blocks = q_len // q_block
    jobs = [(b, h) for b in range(blocks) for h in range(heads)]
    dk_acc[...] = jnp.zeros_like(dk_acc)
    dv_acc[...] = jnp.zeros_like(dv_acc)

    def step(t, carry):
        out, sums = [], []
        for (b, h), dq in zip(jobs, carry):
            cols = slice(b * q_block, (b + 1) * q_block)
            q_part, g_part = q_ref[h, :, cols], g_ref[h, :, cols]
            starts = [index_ref[b * chunks + t * pair + u] * k_block for u in range(pair)]
            heres = [pl.ds(pl.multiple_of(start, k_block), k_block) for start in starts]
            k_part = jnp.concatenate([k_ref[h, :, here] for here in heres], axis=1)
            v_part = jnp.concatenate([v_ref[h, :, here] for here in heres], axis=1)
            scores = lax.dot_general(
                k_part, q_part, (((0,), (0,)), ((), ())), preferred_element_type=F32
            )
            probs = jnp.exp2(scores)
            dprobs = lax.dot_general(
                v_part, g_part, (((0,), (0,)), ((), ())), preferred_element_type=F32
            )
            dscores = (probs * dprobs).astype(BF)
            dq += jnp.dot(k_part, dscores, preferred_element_type=F32)
            dk = lax.dot_general(
                q_part, dscores, (((1,), (1,)), ((), ())), preferred_element_type=F32
            )
            dv = lax.dot_general(
                g_part, probs.astype(BF), (((1,), (1,)), ((), ())), preferred_element_type=F32
            )
            sums.append((h, heres, dk, dv))
            out.append(dq)
        for h, heres, dk, dv in sums:
            for u, here in enumerate(heres):
                dk_acc[h, :, here] += dk[:, u * k_block : (u + 1) * k_block]
                dv_acc[h, :, here] += dv[:, u * k_block : (u + 1) * k_block]
        return tuple(out)

    first = tuple(jnp.zeros((rows, q_block), F32) for _ in jobs)
    final = lax.fori_loop(0, count_ref[0], step, first)
    for (b, h), dq in zip(jobs, final):
        cols = slice(b * q_block, (b + 1) * q_block)
        dq_ref[h, :, cols] = (dq[:dim] * dim**-0.5).astype(BF)
    for h in range(heads):
        dkv_ref[0, h] = (dk_acc[h, :dim, :] * math.log(2.0)).astype(BF)
        dkv_ref[1, h] = dv_acc[h, :dim, :].astype(BF)


def attend_back(
    q_aug, k_aug, v_aug, g_aug, counts, indices, q_block, k_block, pair, group, part, parts, before, *earlier
):
    heads, rows, q_len = q_aug.shape
    k_len = k_aug.shape[2]
    dim = rows - AUG
    base = part * (heads // parts // group)
    spec = lambda r, n: pl.BlockSpec((group, r, n), lambda g, *_: (g + base, 0, 0))
    earlier = (*before, *earlier)
    return pl.pallas_call(
        functools.partial(attend_back_kernel, q_block=q_block, k_block=k_block, pair=pair),
        grid_spec=pltpu.PrefetchScalarGridSpec(
            num_scalar_prefetch=2,
            grid=(heads // parts // group,),
            in_specs=[spec(rows, q_len), spec(rows, k_len), spec(rows, k_len), spec(rows, q_len)]
            + [pl.BlockSpec(memory_space=pl.ANY)] * len(earlier),
            out_specs=[
                spec(dim, q_len),
                pl.BlockSpec((2, group, dim, k_len), lambda g, *_: (0, g + base, 0, 0)),
            ],
            scratch_shapes=[
                pltpu.VMEM((group, rows, k_len), F32),
                pltpu.VMEM((group, rows, k_len), F32),
            ],
        ),
        out_shape=[
            jax.ShapeDtypeStruct((heads, dim, q_len), BF),
            jax.ShapeDtypeStruct((2, heads, dim, k_len), BF),
        ],
        compiler_params=pltpu.CompilerParams(vmem_limit_bytes=56 << 20),
        cost_estimate=pl.CostEstimate(
            flops=10 * heads * rows * q_len * k_len,
            bytes_accessed=8 * heads * rows * (q_len + k_len),
            transcendentals=heads * q_len * k_len // 2,
        ),
        input_output_aliases={6 + i: i for i in range(len(before))},
        name="attend_back",
    )(counts, indices, q_aug, k_aug, v_aug, g_aug, *earlier)


def local(
    activations,
    lengths,
    cotangent,
    ln1_gain,
    ln1_bias,
    query_weight,
    query_bias,
    key_weight,
    value_weight,
    value_bias,
    out_weight,
    out_bias,
    ln2_gain,
    ln2_bias,
    up_weight,
    up_bias,
    down_weight,
    down_bias,
):
    n = lax.axis_size("tp")
    me = lax.axis_index("tp")
    _, here, width = activations.shape
    total_len = here * n
    pics = lengths.shape[1]
    cols = query_weight.shape[2]
    units = up_weight.shape[2]
    heads = cols * n // HEAD_DIM
    hh = cols * n
    reach = min(n - 1, -(-(PIC_MAX - 1) // here))
    scale = HEAD_DIM**-0.5

    x_own = activations[0]
    to_left = [(i, i - 1) for i in range(1, n)]
    to_right = [(i, i + 1) for i in range(n - 1)]
    ends = jnp.cumsum(lengths[0])
    positions = jnp.arange(total_len, dtype=jnp.int32)
    segment = jnp.sum((positions[:, None] >= ends[None, :]).astype(jnp.int32), axis=1)
    own_seg = lax.dynamic_slice_in_dim(segment, me * here, here, 0)
    bias_piece = jnp.concatenate([query_bias[0], value_bias[0], up_bias[0]])
    bias_terms = split3(bias_piece).astype(BF).reshape(-1)
    bias_rows = -(-bias_terms.shape[0] // (4 * cols * 8)) * 8
    bias_terms = jnp.pad(bias_terms, (0, bias_rows * 4 * cols - bias_terms.shape[0]))
    attn_piece = jnp.concatenate(
        [query_weight[0], key_weight[0], value_weight[0], out_weight[0]], axis=1
    )
    attn_piece = jnp.concatenate([attn_piece, bias_terms.reshape(bias_rows, 4 * cols)], axis=0)
    attn_parts = lax.all_gather(attn_piece, "tp", axis=0)
    vectors = jnp.concatenate([ln1_gain, ln1_bias, out_bias, ln2_gain, ln2_bias, down_bias], axis=0)
    vectors = lax.all_gather(vectors, "fsdp", axis=1, tiled=True)
    gain_one, shift_one, out_shift, gain_two, shift_two, down_shift = vectors
    slots = []
    for j in range(1, n):
        use_later, use_prior = j <= reach, n - j <= reach
        if use_later or use_prior:
            slots.append((j, use_later, use_prior))
    slots.sort(key=lambda slot: min(slot[0], n - slot[0]))
    near = 1 + sum(min(j, n - j) == 1 for j, _, _ in slots)

    key_segs = [own_seg]
    for j, use_later, use_prior in slots:
        seg = lax.dynamic_slice_in_dim(segment, ((me + j) % n) * here, here, 0)
        there = jnp.where(me + j < n, use_later, use_prior)
        key_segs.append(jnp.where(there, seg, pics))
    key_seg = jnp.concatenate(key_segs)
    k_len = key_seg.shape[0]
    valid = (own_seg < pics).astype(F32)
    valid_col = valid[:, None]
    q_block = min(512, here)
    k_block = min(256, here)
    pair = 2 if k_len % (2 * k_block) == 0 else 1
    picture = jnp.arange(pics, dtype=jnp.int32)
    q_has = jnp.any(own_seg.reshape(-1, q_block, 1) == picture, axis=1)
    k_has = jnp.any(key_seg.reshape(-1, k_block, 1) == picture, axis=1)
    active = jnp.any(q_has[:, None, :] & k_has[None, :, :], axis=2)
    used = jnp.sum(active.astype(jnp.int32), axis=1, keepdims=True)
    counts = -(-jnp.max(used, axis=0) // pair)
    place = jnp.where(
        active,
        jnp.cumsum(active.astype(jnp.int32), axis=1) - 1,
        used + jnp.cumsum(1 - active.astype(jnp.int32), axis=1) - 1,
    )
    chunk_ids = jnp.arange(active.shape[1], dtype=jnp.int32)
    hit = place[:, :, None] == chunk_ids[None, None, :]
    indices = jnp.sum(jnp.where(hit, chunk_ids[None, :, None], 0), axis=1).reshape(-1)

    q_mask = jnp.concatenate(
        [
            jnp.where(own_seg[None, :] == picture[:, None], 0.0, MASKED),
            jnp.full((1, here), MASKED, F32),
        ],
        axis=0,
    )
    k_mask = jnp.concatenate(
        [(key_seg[None, :] == picture[:, None]), (key_seg >= pics)[None, :]], axis=0
    ).astype(BF)
    spare = AUG - (pics + 1) - 3
    k_added = jnp.concatenate(
        [k_mask, jnp.ones((3, k_len), BF), jnp.zeros((spare, k_len), BF)], axis=0
    )
    v_added = jnp.concatenate([jnp.ones((3, k_len), BF), jnp.zeros((AUG - 3, k_len), BF)], axis=0)

    grad_two = cotangent[0].astype(F32) * valid_col
    grad_mixed = grad_two.astype(BF)
    down_bias_part = jnp.sum(grad_mixed, axis=0, dtype=F32)
    attn_parts = after(
        attn_parts, vectors, counts, indices, k_added, q_mask, down_bias_part, grad_mixed
    )
    share = query_weight.shape[1]
    all_biases = jnp.sum(
        attn_parts[:, share:]
        .reshape(n, -1)[:, : 3 * bias_piece.shape[0]]
        .reshape(n, 3, -1)
        .astype(F32),
        axis=1,
    )
    first = copy_after(x_own, attn_parts)
    later, prior = [first], [first]
    later.append(lax.ppermute(first, "tp", to_left))
    prior.append(lax.ppermute(first, "tp", to_right))
    query_shift = all_biases[:, :cols].reshape(-1)
    value_shift = all_biases[:, cols : 2 * cols].reshape(-1)
    ring_order = (me - jnp.arange(n)) % n
    up_shift = jnp.take(all_biases[:, 2 * cols :], ring_order, axis=0).reshape(-1)

    first_up = copy_after(
        up_weight[0], later[1], prior[1], up_shift, query_shift, value_shift
    )
    up_slots = slots_along_tp(first_up, n)
    far_later, far_prior = [later[1]], [prior[1]]
    if reach > 1:
        far_later = [after(later[1], up_slots[-1])]
        far_prior = [after(prior[1], up_slots[-1])]
    for _ in range(reach - 1):
        far_later.append(lax.ppermute(far_later[-1], "tp", to_left))
        far_prior.append(lax.ppermute(far_prior[-1], "tp", to_right))
    later, prior = [x_own] + far_later, [x_own] + far_prior

    def tokens_of(slot, *gates):
        j, use_later, use_prior = slot
        from_later = after(later[j], *gates) if use_later and gates else later[j] if use_later else None
        from_prior = after(prior[n - j], *gates) if use_prior and gates else prior[n - j] if use_prior else None
        if use_later and use_prior:
            return jnp.where(me + j < n, from_later, from_prior)
        return from_later if use_later else from_prior

    def widen(parts, added):
        parts = [part.reshape(heads, HEAD_DIM, part.shape[-1]) for part in parts]
        body = jnp.concatenate(parts, axis=2) if len(parts) > 1 else parts[0]
        added = jnp.broadcast_to(added, (heads, AUG, body.shape[-1]))
        return jnp.concatenate([body, added.astype(BF)], axis=1)

    attn_shard = jnp.concatenate(
        [attn_parts[o, :share, t * cols : (t + 1) * cols] for t in range(4) for o in range(n)],
        axis=1,
    )
    attn_full = lax.all_gather(attn_shard, "fsdp", axis=0, tiled=True)
    up_full = lax.all_gather(jnp.concatenate(up_slots, axis=1), "fsdp", axis=0, tiled=True)

    query_full = attn_full[:, :hh]
    key_full = attn_full[:, hh : 2 * hh]
    value_full = attn_full[:, 2 * hh : 3 * hh]
    kv_full = attn_full[:, hh : 3 * hh]
    out_full = attn_full[:, 3 * hh : 4 * hh]

    x = x_own.astype(F32)
    normed_near = norm_tokens(
        [x_own] + [tokens_of(slot) for slot in slots[: near - 1]], gain_one, shift_one
    )
    normed = normed_near[:here]
    queries = (
        (product("td,dc->ct", normed, query_full) + query_shift[:, None])
        * (scale * math.log2(math.e))
    ).astype(BF)
    q_rest = jnp.zeros((AUG - (pics + 1), here), F32)
    q_aug = widen([queries], jnp.concatenate([q_mask, q_rest], axis=0))

    def keys_values(tokens):
        keys = product("td,dc->ct", tokens, key_full).astype(BF)
        values = product("td,dc->ct", tokens, value_full) + value_shift[:, None]
        return keys, values.astype(BF)

    pieces = [keys_values(normed_near)]
    gates = (pieces[0][0], pieces[0][1], q_aug)
    down_first = far_later[-1], far_prior[-1]
    if slots[near - 1 :]:
        far_tokens = [tokens_of(slot, *gates) for slot in slots[near - 1 :]]
        normed_far = norm_tokens(far_tokens, gain_one, shift_one)
        pieces.append(keys_values(normed_far))
        down_first = far_tokens
    normed_all = jnp.concatenate([normed_near] + [normed_far] * (len(pieces) - 1), axis=0)
    k_aug = after(widen([piece[0] for piece in pieces], k_added))
    v_aug = after(widen([piece[1] for piece in pieces], v_added))
    group = 4 if heads % 8 == 0 else 1
    down_slots = slots_along_tp(copy_after(down_weight[0], *down_first), n, k_aug, v_aug)
    down_shard = jnp.concatenate(down_slots, axis=1)
    down_full = lax.all_gather(down_shard, "fsdp", axis=0, tiled=True)
    attended, log_total = attend(
        q_aug,
        k_aug,
        v_aug,
        valid[None, :],
        counts,
        indices,
        q_block,
        k_block,
        pair,
        group,
        0,
        1,
        down_shard,
    )
    flat = attended.reshape(hh, here)
    middle = x + (product("ct,dc->td", flat, out_full) + out_shift)

    two_hat, two_rstd = xhat_of(middle)
    normed_two = (two_hat * gain_two + shift_two).astype(BF)
    hidden = product("td,df->tf", normed_two, up_full) + up_shift
    active_units, gelu_pull = jax.vjp(gelu_tanh, hidden)
    active_units = active_units.astype(BF)

    down_grad = product("td,tf->df", grad_mixed, active_units).astype(BF)
    down_scattered = lax.psum_scatter(down_grad, "fsdp", scatter_dimension=0, tiled=True)
    back_mixed = after(grad_mixed, down_grad)
    grad_hidden = gelu_pull(product("td,df->tf", back_mixed, down_full))[0].astype(BF)
    up_bias_part = jnp.sum(grad_hidden, axis=0, dtype=F32)
    up_grad = product("td,tf->df", normed_two, grad_hidden).astype(BF)
    grad_normed_two = product("tf,df->td", grad_hidden, up_full)
    grad_middle, gain_two_part, shift_two_part = norm_back(
        grad_normed_two, two_hat, two_rstd, gain_two
    )
    grad_middle = grad_two + grad_middle
    grad_branch = grad_middle.astype(BF)
    out_bias_part = jnp.sum(grad_branch, axis=0, dtype=F32)
    out_grad = product("td,ct->dc", grad_branch, flat).astype(BF)
    up_scattered = lax.psum_scatter(up_grad, "fsdp", scatter_dimension=0, tiled=True)

    grad_attended = product("td,dc->ct", grad_branch, out_full).astype(BF)
    grad_attended = grad_attended * valid.astype(BF)
    grad_heads = grad_attended.reshape(heads, HEAD_DIM, here)
    delta = jnp.sum(grad_heads.astype(F32) * attended.astype(F32), axis=1)
    g_added = jnp.concatenate(
        [
            jnp.moveaxis(split3(-delta), 0, 1),
            jnp.zeros((heads, AUG - 3, here), F32),
        ],
        axis=1,
    )
    g_aug = widen([grad_attended], g_added)
    q_added = jnp.concatenate(
        [
            jnp.broadcast_to(q_mask, (heads, pics + 1, here)),
            jnp.moveaxis(split3(-log_total[:, 0]), 0, 1),
            jnp.zeros((heads, spare, here), F32),
        ],
        axis=1,
    )
    q_aug_back = widen([queries], q_added)
    def back_part(part, before, *earlier):
        return attend_back(
            q_aug_back,
            k_aug,
            v_aug,
            g_aug,
            counts,
            indices,
            q_block,
            k_block,
            pair,
            group,
            part,
            2,
            before,
            *earlier,
        )

    parts = back_part(0, (), up_grad, out_grad)
    down_scattered = after(down_scattered, parts[0])
    down_moved = [
        lax.ppermute(
            down_scattered[:, s * units : (s + 1) * units],
            "tp",
            [(i, (i - s) % n) for i in range(n)],
        )
        for s in range(1, n)
    ]
    dq, dkv = back_part(1, parts, down_scattered)
    down_moved = [after(moved, dq) for moved in down_moved]
    dq, dkv = dq.reshape(hh, -1), dkv.reshape(2 * hh, -1)

    def share_of(position, dkv):
        part = slice(position * here, (position + 1) * here)
        return product("ct,dc->td", dkv[:, part], kv_full)

    to_later = [None] * (reach + 1)
    to_prior = [None] * (reach + 1)

    def send_shares(distance, dkv):
        for i, (j, use_later, use_prior) in enumerate(slots):
            if min(j, n - j) != distance:
                continue
            part = share_of(i + 1, dkv).astype(BF)
            zero = jnp.zeros_like(part)
            if use_later and j == distance:
                to_later[j] = jnp.where(me + j < n, part, zero)
            if use_prior and n - j == distance:
                to_prior[n - j] = jnp.where(me + j >= n, part, zero)

    send_shares(reach, dkv)
    moving_right = lax.ppermute(to_later[reach], "tp", to_right)
    moving_left = lax.ppermute(to_prior[reach], "tp", to_left)
    dkv = after(dkv, to_later[reach], to_prior[reach], *down_moved)
    query_grad = product("td,ct->dc", normed, dq).astype(BF)
    kv_grad = product("td,ct->dc", normed_all, dkv).astype(BF)
    out_grad = after(out_grad, kv_grad, query_grad, moving_right, moving_left)
    attn_grad = jnp.concatenate([query_grad, kv_grad, out_grad], axis=1)
    attn_scattered = lax.psum_scatter(attn_grad, "fsdp", scatter_dimension=0, tiled=True)
    query_bias_part = jnp.sum(dq, axis=1, dtype=F32)
    dkv = after(dkv, attn_grad)
    for distance in reversed(range(1, reach)):
        send_shares(distance, dkv)
    up_moved = [
        lax.ppermute(
            up_scattered[:, s * units : (s + 1) * units],
            "tp",
            [(i, (i - s) % n) for i in range(n)],
        )
        for s in range(1, n)
    ]
    near_shares = [t for t in to_later[1:] + to_prior[1:] if t is not None]
    for distance in reversed(range(1, reach)):
        up_moved = [after(moved, *near_shares) for moved in up_moved]
        moving_right = after(moving_right, *near_shares, *up_moved)
        moving_left = after(moving_left, *near_shares)
        moving_right = (moving_right.astype(F32) + to_later[distance].astype(F32)).astype(BF)
        moving_left = (moving_left.astype(F32) + to_prior[distance].astype(F32)).astype(BF)
        dkv = after(dkv, moving_right, moving_left)
        moving_right = lax.ppermute(moving_right, "tp", to_right)
        moving_left = lax.ppermute(moving_left, "tp", to_left)
    own_share = share_of(0, dkv) + product("ct,dc->td", dq, query_full)
    moving_right, moving_left = after(moving_right, own_share), after(moving_left, own_share)
    grad_normed = own_share + moving_right.astype(F32) + moving_left.astype(F32)

    def summed(scattered, moved):
        return sum((m.astype(F32) for m in moved), scattered[:, :units].astype(F32))

    down_weight_grad = summed(down_scattered, down_moved)
    up_weight_grad = summed(up_scattered, up_moved)
    one_hat, one_rstd = xhat_of(x)
    grad_x, gain_one_part, shift_one_part = norm_back(grad_normed, one_hat, one_rstd, gain_one)
    input_grad = grad_middle + grad_x

    value_bias_part = jnp.sum(dkv[hh:], axis=1, dtype=F32)
    vector_part = jnp.concatenate(
        [
            gain_one_part,
            shift_one_part,
            out_bias_part,
            gain_two_part,
            shift_two_part,
            down_bias_part,
        ]
    )
    up_bias_parts = jnp.take(up_bias_part.reshape(n, units), ring_order, axis=0).reshape(-1)
    small = jnp.concatenate([query_bias_part, value_bias_part, up_bias_parts, vector_part])

    def sum_over(value, axis):
        count = lax.axis_size(axis)
        if count & (count - 1):
            return lax.psum(value, axis)
        bit = 1
        while bit < count:
            value = value + lax.ppermute(value, axis, [(i, i ^ bit) for i in range(count)])
            bit *= 2
        return value

    small = sum_over(sum_over(small, "tp"), "fsdp")
    attn_scattered = after(attn_scattered, small)
    attn_owned = by_owner(attn_scattered, n, 4)
    attn_out = lax.psum_scatter(attn_owned, "tp", scatter_dimension=0, tiled=True).astype(F32)
    mixed = product("tf,df->td", after(active_units, attn_owned), down_full) + down_shift
    activations_out = ((middle + mixed) * valid_col).astype(BF)

    bias_size = (2 * cols + units) * n
    query_bias_grad, value_bias_grad, up_bias_grad = (
        lax.dynamic_slice_in_dim(small, start + me * size, size, 0)
        for start, size in ((0, cols), (hh, cols), (2 * hh, units))
    )
    own_vectors = lax.dynamic_slice_in_dim(
        small[bias_size:].reshape(6, width), lax.axis_index("fsdp") * share, share, 1
    )
    return (
        activations_out[None],
        input_grad[None],
        own_vectors[0:1],
        own_vectors[1:2],
        attn_out[None, :, :cols],
        query_bias_grad[None],
        attn_out[None, :, cols : 2 * cols],
        attn_out[None, :, 2 * cols : 3 * cols],
        value_bias_grad[None],
        attn_out[None, :, 3 * cols :],
        own_vectors[2:3],
        own_vectors[3:4],
        own_vectors[4:5],
        up_weight_grad[None],
        up_bias_grad[None],
        down_weight_grad[None],
        own_vectors[5:6],
    )


def solution(mesh):
    token = P("fsdp", "tp", None)
    vector, shift, matrix = P(None, "fsdp"), P(None, "tp"), P(None, "fsdp", "tp")
    in_specs = (
        token,
        P("fsdp", None),
        token,
        vector,
        vector,
        matrix,
        shift,
        matrix,
        matrix,
        shift,
        matrix,
        vector,
        vector,
        vector,
        matrix,
        shift,
        matrix,
        vector,
    )
    out_specs = (
        token,
        token,
        vector,
        vector,
        matrix,
        shift,
        matrix,
        matrix,
        shift,
        matrix,
        vector,
        vector,
        vector,
        matrix,
        shift,
        matrix,
        vector,
    )
    return jax.shard_map(local, mesh=mesh, in_specs=in_specs, out_specs=out_specs, check_vma=False)
```

time: 764 us -> 602 us (0.79)
  the two profiles are of different devices: /device:TPU:30 before, /device:TPU:0 now
where the time goes in v2:
time: 602 us; the launch traced here: 594 us
  matrix products  165 us (27%)
  waiting for transfers between devices  140 us (23%)
  Pallas kernels  75.7 us (13%)
  starting transfers between devices  74.6 us (12%)
  other arithmetic  60.6 us (10%)
  local copies, waits for them, and re-layouts  50.8 us (8%)
  between operations  16.9 us (3%)
  blocking collectives  10.7 us (2%)
    dot_general x21, matrix products, product(): return jnp.einsum(form, left, right, preferred_element_type=F32)  165 us
    pallas_call x2, Pallas kernels, attend_back(): pl.pallas_call(functools.partial(attend_back_kernel, q_block=q_block, k_b...  38.3 us
    ppermute x6, waiting for transfers between devices, slots_along_tp(): lax.ppermute(piece, 'tp', [(i, (i + distance) % count) for i in range(cou...  30.9 us
    pallas_call x1, Pallas kernels, attend(): pl.pallas_call(functools.partial(attend_kernel, q_block=q_block, k_block=...  21.2 us
    unnamed x151, local copies, waits for them, and re-layouts  20 us
    ppermute x1, waiting for transfers between devices, local(): prior.append(lax.ppermute(first, 'tp', to_right))  19.9 us
    ppermute x1, starting transfers between devices, local(): moving_right = lax.ppermute(to_later[reach], 'tp', to_right)  16.1 us
    all_gather x1, waiting for transfers between devices, local(): attn_parts = lax.all_gather(attn_piece, 'tp', axis=0)  15.6 us
  transfers between devices with their start and end apart: 33, of which 18 were waited for; matrix products, arithmetic and copies ran while one was open for 42% of the time, Pallas kernels for 12%

profile of v2, /device:TPU:0, one launch (start us, length us, event | category | flops | bytes accessed | tf_op | source)
XLA Modules:
  0.0 594.4 jit_solution(18318621389101504315)
XLA Ops:
  16.6 10.7 %all-gather.1 = f32[8,144,6]{1,2,0:T(8,128)S(1)} all-gather(f32[1,144,6]{1,2,0:T(8,128)S(1)} %bitcast.167), channel_id=1, replica_groups=mesh['fsdp'=8,'tp'=4] {'fsdp'}, dimensions={0}, use_global_device_ids=true | all-gather | bytes 31104 | tf_op jit(solution)/shard_map/all_gather | solution.py:364
  31.9 15.6 %all-gather.13.cloned.1.call-done = bf16[608,1152]{1,0:T(8,128)(2,1)} async-done(((bf16[152,1152]{1,0:T(8,128)(2,1)}), bf16[608,1152]{1,0:T(8,128)(2,1)}) %all-gather.13.cloned.1.call-update) | async-done | bytes 1400848 | tf_op jit(solution)/shard_map/all_gather | solution.py:362
  62.4 19.9 %collective-permute-done.1.refs_1_.refs_0_ = bf16[512,1152]{1,0:T(8,128)(2,1)S(1)} collective-permute-done((bf16[512,1152]{1,0:T(8,128)(2,1)}, bf16[512,1152]{1,0:T(8,128)(2,1)S(1)}, u32[]{:S(2)}, u32[]{:S(2)}) %collective-permute-start.1) | collective-permute-done | bytes 1179680 | tf_op jit(solution)/shard_map/ppermute | solution.py:434
  82.3 4.1 collective-permute-done.refs_0_
  90.6 3.7 collective-permute-start.2
  94.3 19.6 %collective-permute-done.9 = bf16[144,1076]{1,0:T(8,128)(2,1)S(1)} collective-permute-done((bf16[144,1076]{1,0:T(8,128)(2,1)}, bf16[144,1076]{1,0:T(8,128)(2,1)S(1)}, u32[]{:S(2)}, u32[]{:S(2)}) %collective-permute-start.9) | collective-permute-done | bytes 309920 | tf_op jit(solution)/shard_map/ppermute | solution.py:78
  114.0 3.3 concatenate.152
  120.3 10.3 %collective-permute-start.4 = (bf16[512,1152]{1,0:T(8,128)(2,1)}, bf16[512,1152]{1,0:T(8,128)(2,1)}, u32[]{:S(2)}, u32[]{:S(2)}) collective-permute-start(bf16[512,1152]{1,0:T(8,128)(2,1)} %after.30.refs_2_), channel_id=1, source_target_pairs={{0,1},{1,2},{2,3},{4,5},{5,6},{6,7},{8,9},{9,10},{10,11},{12,13},{... | collective-permute-start | bytes 3538952 | tf_op jit(solution)/shard_map/ppermute | solution.py:450
  132.1 5.5 norm_tokens.2
  139.4 9.5 %convolution_convert_fusion.3.refs_1_ = bf16[1152,1536]{1,0:T(8,128)(2,1)} fusion(bf16[1536,1152]{1,0:T(8,128)(2,1)} %copy-done.7, bf16[1152,4608]{1,0:T(8,128)(2,1)} %all-gather.7.cloned.1.call-done), kind=kOutput, calls=%fused_computation.20 | convolution fusion | flops 4078632960 | bytes 9732096 | tf_op jit(solution)/shard_map/td,dc->ct/dot_general | solution.py:37
  152.2 6.4 %fusion.7.refs_2_ = bf16[1152,1536]{1,0:T(8,128)(2,1)} fusion(bf16[1536,1152]{1,0:T(8,128)(2,1)S(1)} %copy-done.8, f32[1152]{0:T(1024)S(1)} %copy-done.48, bf16[1152,4608]{1,0:T(8,128)(2,1)S(1)} %copy-done.72), kind=kOutput, calls=%fused_computation.19 | convolution fusion | flops 4080402432 | bytes 9740288 | tf_op jit(solution)/shard_map/td,dc->ct/dot_general | solution.py:37
  169.0 4.0 fusion.27
  175.9 3.6 convolution_convert_fusion.7
  182.7 11.2 %collective-permute-done.6.refs_0_ = bf16[144,1076]{1,0:T(8,128)(2,1)} collective-permute-done((bf16[144,1076]{1,0:T(8,128)(2,1)}, bf16[144,1076]{1,0:T(8,128)(2,1)}, u32[]{:S(2)}, u32[]{:S(2)}) %collective-permute-start.6) | collective-permute-done | bytes 309920 | tf_op jit(solution)/shard_map/ppermute | solution.py:78
  194.8 3.5 concatenate.151.rest_0_
  198.4 21.2 %attend.1 = (bf16[16,72,512]{2,1,0:T(8,128)(2,1)}, f32[16,1,512]{2,1,0:T(1,128)}) custom-call(s32[1]{0:T(128)S(6)} %neg.49.refs_2_.count_ref, s32[8]{0:T(128)} %select_reduce_fusion.refs_3_.index_ref, bf16[16,80,512]{2,1,0:T(8,128)(2,1)} %pad_maximum_fusion.3.refs_3_.q_ref, bf16[16,80,2048]{2,1,0:T(8,128)(2,1)} %after.33.refs_1_.k_ref, ...), custom_call_target="tpu_custom_call" | custom-call | flops 5368709120 | bytes 13107200 | tf_op jit(solution)/shard_map/attend/pallas_call | solution.py:193
  219.6 4.1 fusion.97
  225.0 15.3 %multiply_convert_fusion = (bf16[512,4304]{1,0:T(8,128)(2,1)S(1)}, f32[512,4304]{1,0:T(8,128)}) fusion(f32[4304]{0:T(1024)} %reshape.617.refs_2_, bf16[1152,4304]{1,0:T(8,128)(2,1)} %all-gather.9.cloned.1.call-done, f32[512,1152]{1,0:T(8,128)S(1)} %get-tuple-element.107, f32[1152]{0:T(1024)} %get-tuple-element.40, f32[1152]{0:T(1024)S(1)} %copy-done.52, ...), kind=kOutput, calls=%fused_computation.18 | convolution fusion | flops 5102190592 | bytes 25528128 | tf_op jit(solution)/shard_map/td,df->tf/dot_general | solution.py:37
  242.5 8.2 %convolution_convert_fusion.1.refs_1_ = bf16[1152,4304]{1,0:T(8,128)(2,1)} fusion(bf16[512,1152]{1,0:T(8,128)(2,1)S(1)} %copy-done.18, bf16[512,4304]{1,0:T(8,128)(2,1)S(1)} %get-tuple-element.108.refs_0_), kind=kOutput, calls=%fused_computation.3 | convolution fusion | flops 5082163200 | bytes 15503360 | tf_op jit(solution)/shard_map/td,tf->df/dot_general | solution.py:37
  251.0 7.3 %all-gather.11.cloned.1.call-done = bf16[1152,4304]{1,0:T(8,128)(2,1)} async-done(((bf16[144,4304]{1,0:T(8,128)(2,1)}), bf16[1152,4304]{1,0:T(8,128)(2,1)}) %all-gather.11.cloned.1.call-update) | async-done | bytes 9916432 | tf_op jit(solution)/shard_map/all_gather | solution.py:511
  258.2 14.2 %convert_reduce_fusion.1 = (f32[4304]{0:T(1024)}, bf16[512,4304]{1,0:T(8,128)(2,1)S(1)}) fusion(f32[512,4304]{1,0:T(8,128)} %get-tuple-element.109, f32[4304]{0:T(1024)S(1)} %copy-done.43, bf16[512,1152]{1,0:T(8,128)(2,1)} %after.38, bf16[1152,4304]{1,0:T(8,128)(2,1)} %all-gather.11.cloned.1.call-done), kind=kOutput, calls=%fused_computation.17 | convolution fusion | flops 5127884800 | bytes 24352384 | tf_op jit(solution)/shard_map/td,df->tf/dot_general | solution.py:37
  275.0 8.5 %convolution_convert_fusion.rest_0_ = bf16[1152,4304]{1,0:T(8,128)(2,1)} fusion(bf16[512,4304]{1,0:T(8,128)(2,1)S(1)} %get-tuple-element.47, f32[512,1152]{1,0:T(8,128)S(1)} %get-tuple-element.107, f32[1152]{0:T(1024)S(1)} %copy-done.63, f32[1152]{0:T(1024)S(1)} %copy-done.52, f32[512]{0:T(512)S(1)} %copy-done.66, f32[512]{0:T(512)S(1)} %broadcast_multiply_fusion.5), kind=kOutput, calls=%fused_computation.2 | convolution fusion | flops 5085112320 | bytes 16696320 | tf_op jit(solution)/shard_map/td,tf->df/dot_general | solution.py:37
  286.7 12.6 %multiply_reduce_fusion = (f32[1152]{0:T(1024)}, f32[512]{0:T(512)S(1)}, f32[512]{0:T(512)S(1)}, f32[1152]{0:T(1024)}, f32[512,1152]{1,0:T(8,128)S(1)}) fusion(f32[512,1152]{1,0:T(8,128)S(1)} %get-tuple-element.107, f32[512]{0:T(512)S(1)} %copy-done.67, f32[512]{0:T(512)S(1)} %copy-done.57, f32[1152]{0:T(1024)S(1)} %copy-done.52, ...), kind=kOutput, calls=%fused_computation.80 | convolution fusion | flops 5082510336 | bytes 19064320 | tf_op jit(solution)/shard_map/tf,df->td/dot_general | solution.py:37
  301.0 4.5 fusion.37
  307.3 3.2 convolution_convert_fusion.5.rest_1_.refs_0_
  310.5 18.7 %attend_back.2 = (bf16[16,72,512]{2,1,0:T(8,128)(2,1)}, bf16[2,16,72,2048]{3,2,1,0:T(8,128)(2,1)}) custom-call(s32[1]{0:T(128)S(6)} %neg.49.refs_2_.count_ref, s32[8]{0:T(128)} %select_reduce_fusion.refs_3_.index_ref, bf16[16,80,512]{2,1,0:T(8,128)(2,1)} %maximum_maximum_fusion.q_ref, bf16[16,80,2048]{2,1,0:T(8,128)(2,1)} %after.33.refs_1_.k_ref, ...), custom_call_target="tpu_custom_call" | custom-call | flops 13421772800 | bytes 26214400 | tf_op jit(solution)/shard_map/attend_back/pallas_call | solution.py:284
  329.3 11.8 %reduce-scatter.5.cloned.1.call-done.refs_0_ = bf16[144,4304]{1,0:T(8,128)(2,1)} async-done(((bf16[1152,4304]{1,0:T(8,128)(2,1)}), bf16[144,4304]{1,0:T(8,128)(2,1)}) %reduce-scatter.5.cloned.1.call-update) | async-done | bytes 1239568 | tf_op jit(solution)/shard_map/reduce_scatter | solution.py:537
  343.6 6.9 %collective-permute-start.12 = (bf16[144,1076]{1,0:T(8,128)(2,1)S(1)}, bf16[144,1076]{1,0:T(8,128)(2,1)}, u32[]{:S(2)}, u32[]{:S(2)}) collective-permute-start(bf16[144,1076]{1,0:T(8,128)(2,1)S(1)} %get-tuple-element.71), channel_id=1, source_target_pairs={{0,1},{1,2},{2,3},{3,0},{4,5},{5,6},{6,7},{7,4},{8,9},{9,10},{10,1... | collective-permute-start | bytes 929672 | tf_op jit(solution)/shard_map/ppermute | solution.py:594
  352.9 19.5 %attend_back.3 = (bf16[16,72,512]{2,1,0:T(8,128)(2,1)}, bf16[2,16,72,2048]{3,2,1,0:T(8,128)(2,1)}) custom-call(s32[1]{0:T(128)S(6)} %neg.49.refs_2_.count_ref, s32[8]{0:T(128)} %select_reduce_fusion.refs_3_.index_ref, bf16[16,80,512]{2,1,0:T(8,128)(2,1)} %maximum_maximum_fusion.q_ref, ...), custom_call_target="tpu_custom_call", output_to_operand_aliasing={{0}: (6, {}), {1}: (7, {})} | custom-call | flops 13421772800 | bytes 26214400 | tf_op jit(solution)/shard_map/attend_back/pallas_call | solution.py:284
  372.5 8.1 %broadcast_select_fusion = (bf16[512,1152]{1,0:T(8,128)(2,1)}, bf16[512,1152]{1,0:T(8,128)(2,1)}) fusion(pred[]{:T(512)S(6)} %ge.41, pred[]{:T(512)S(6)} %lt.74, bf16[1152,4608]{1,0:T(8,128)(2,1)} %all-gather.7.cloned.1.call-done, bf16[2304,2048]{1,0:T(8,128)(2,1)} %bitcast.140), kind=kOutput, calls=%fused_computation.106 | convolution fusion | flops 2719678464 | bytes 10027010 | tf_op jit(solution)/shard_map/ct,dc->td/dot_general | solution.py:37
  381.9 16.1 %collective-permute-start.13 = (bf16[512,1152]{1,0:T(8,128)(2,1)}, bf16[512,1152]{1,0:T(8,128)(2,1)}, u32[]{:S(2)}, u32[]{:S(2)}) collective-permute-start(bf16[512,1152]{1,0:T(8,128)(2,1)} %get-tuple-element.75.refs_1_.refs_2_), channel_id=1, source_target_pairs={{0,1},{1,2},{2,3},{4,5},{5,6},{6,7},{8,9},{9,10},{10,11},{12,13},{... | collective-permute-start | bytes 3538952 | tf_op jit(solution)/shard_map/ppermute | solution.py:624
  401.2 15.3 %convolution_convert_fusion.2.refs_1_ = bf16[1152,2304]{1,0:T(8,128)(2,1)} fusion(bf16[2304,2048]{1,0:T(8,128)(2,1)} %after.43.refs_0_, bf16[512,1152]{1,0:T(8,128)(2,1)} %copy-done.10, bf16[1536,1152]{1,0:T(8,128)(2,1)S(1)} %copy-done.9), kind=kOutput, calls=%fused_computation.6 | convolution fusion | flops 10883727360 | bytes 19464192 | tf_op jit(solution)/shard_map/td,ct->dc/dot_general | solution.py:37
  416.5 4.1 collective-permute-done.14.refs_4_.refs_0_
  421.8 8.6 %pad_maximum_fusion.refs_1_ = bf16[1152,4608]{1,0:T(8,128)(2,1)} fusion(bf16[1152,1152]{1,0:T(8,128)(2,1)} %after.44, bf16[1152,2304]{1,0:T(8,128)(2,1)} %convolution_convert_fusion.2.refs_1_, bf16[1152,1152]{1,0:T(8,128)(2,1)S(1)} %copy-done.19), kind=kLoop, calls=%fused_computation.7 | loop fusion | flops 31850496 | bytes 21233664 | tf_op jit(solution)/shard_map/concatenate | solution.py:630
  435.5 5.1 fusion.70
  440.7 9.2 %fusion.46.refs_1_ = bf16[512,1152]{1,0:T(8,128)(2,1)} fusion(bf16[1152,4608]{1,0:T(8,128)(2,1)} %all-gather.7.cloned.1.call-done, bf16[2304,2048]{1,0:T(8,128)(2,1)} %after.45.refs_0_, pred[]{:T(512)S(6)} %lt.64), kind=kOutput, calls=%fused_computation.62 | convolution fusion | flops 2719088640 | bytes 8847361 | tf_op jit(solution)/shard_map/ct,dc->td/dot_general | solution.py:37
  449.9 7.6 %fusion.43.refs_3_ = bf16[512,1152]{1,0:T(8,128)(2,1)} fusion(bf16[1152,4608]{1,0:T(8,128)(2,1)} %all-gather.7.cloned.1.call-done, bf16[2304,2048]{1,0:T(8,128)(2,1)} %after.45.refs_0_, pred[]{:T(512)S(6)} %ge.42), kind=kOutput, calls=%fused_computation.61 | convolution fusion | flops 2719088640 | bytes 8847361 | tf_op jit(solution)/shard_map/ct,dc->td/dot_general | solution.py:37
  473.4 11.2 %collective-permute-done.16.refs_0_ = bf16[144,1076]{1,0:T(8,128)(2,1)S(1)} collective-permute-done((bf16[144,1076]{1,0:T(8,128)(2,1)}, bf16[144,1076]{1,0:T(8,128)(2,1)S(1)}, u32[]{:S(2)}, u32[]{:S(2)}) %collective-permute-start.16) | collective-permute-done | bytes 309920 | tf_op jit(solution)/shard_map/ppermute | solution.py:637
  489.9 10.1 %collective-permute-start.18 = (bf16[512,1152]{1,0:T(8,128)(2,1)}, bf16[512,1152]{1,0:T(8,128)(2,1)}, u32[]{:S(2)}, u32[]{:S(2)}) collective-permute-start(bf16[512,1152]{1,0:T(8,128)(2,1)} %add_convert_fusion.1.refs_1_), channel_id=1, source_target_pairs={{0,1},{1,2},{2,3},{4,5},{5,6},{6,7},{8,9},{9,10},{10,11},{12,13},{... | collective-permute-start | bytes 3538952 | tf_op jit(solution)/shard_map/ppermute | solution.py:652
  500.0 8.7 %fusion.19.refs_1_ = f32[512,1152]{1,0:T(8,128)} fusion(f32[512,1152]{1,0:T(8,128)} %fusion.70, bf16[1152,4608]{1,0:T(8,128)(2,1)} %all-gather.7.cloned.1.call-done, bf16[2304,2048]{1,0:T(8,128)(2,1)} %after.51), kind=kOutput, calls=%fused_computation.39 | convolution fusion | flops 2718498816 | bytes 12386304 | tf_op jit(solution)/shard_map/ct,dc->td/dot_general | solution.py:37
  510.7 3.7 convert_reduce_fusion
  514.4 9.9 %collective-permute-done.18.refs_0_ = bf16[512,1152]{1,0:T(8,128)(2,1)} collective-permute-done((bf16[512,1152]{1,0:T(8,128)(2,1)}, bf16[512,1152]{1,0:T(8,128)(2,1)}, u32[]{:S(2)}, u32[]{:S(2)}) %collective-permute-start.18) | collective-permute-done | bytes 1179680 | tf_op jit(solution)/shard_map/ppermute | solution.py:652
  524.3 4.7 fusion.52
  536.5 3.3 collective-permute-done.21
  547.3 3.6 collective-permute-done.24
  555.2 3.9 fusion.56
  563.3 11.6 %fusion.49 = bf16[1,512,1152]{2,1,0:T(8,128)(2,1)} fusion(f32[512,1152]{1,0:T(8,128)S(1)} %copy-done.21, bf16[512,4304]{1,0:T(8,128)(2,1)} %after.55, bf16[1152,4304]{1,0:T(8,128)(2,1)} %all-gather.11.cloned.1.call-done, f32[1152]{0:T(1024)S(1)} %copy-done.62, f32[512]{0:T(512)S(1)} %copy-done.60), kind=kOutput, calls=%fused_computation.63 | convolution fusion | flops 5079564288 | bytes 17869312 | tf_op jit(solution)/shard_map/tf,df->td/dot_general | solution.py:37
  575.0 10.1 %reduce-scatter.11.cloned.1.call-done = bf16[144,1152]{1,0:T(8,128)(2,1)} async-done(((bf16[576,1152]{1,0:T(8,128)(2,1)}), bf16[144,1152]{1,0:T(8,128)(2,1)}) %reduce-scatter.11.cloned.1.call-update) | async-done | bytes 331792 | tf_op jit(solution)/shard_map/reduce_scatter | solution.py:694
  (360 shorter events, 135.5 us)
Async XLA Ops:
  7.2 22.1 %copy-start.26 = (bf16[1,512,1152]{2,1,0:T(8,128)(2,1)S(1)}, bf16[1,512,1152]{2,1,0:T(8,128)(2,1)}, u32[]{:S(2)}) copy-start(bf16[1,512,1152]{2,1,0:T(8,128)(2,1)} %param.22) | copy-start | bytes 3538948
  7.2 40.4 %all-gather.13.cloned.1.call-start = ((), (), s32[]{:S(2)}) async-start(), calls=%async_computation.11 | async-start | bytes 1751040 | tf_op jit(solution)/shard_map/all_gather | solution.py:362
  10.5 128.9 %all-gather.7.cloned.1.call-start = ((), (), s32[]{:S(2)}) async-start(), calls=%async_computation.4 | async-start | bytes 11943936 | tf_op jit(solution)/shard_map/all_gather | solution.py:471
  13.3 34.2 %copy-start.45 = (f32[3,512]{1,0:T(4,128)}, f32[3,512]{1,0:T(4,128)S(1)}, u32[]{:S(2)}) copy-start(f32[3,512]{1,0:T(4,128)S(1)} %get-tuple-element.104) | copy-start | bytes 18436
  29.2 18.4 %copy-start.58 = (f32[512]{0:T(512)}, f32[512]{0:T(512)S(1)}, u32[]{:S(2)}) copy-start(f32[512]{0:T(512)S(1)} %compare_convert_fusion) | copy-start | bytes 6148
  52.0 173.1 %all-gather.9.cloned.1.call-start = ((), (), s32[]{:S(2)}) async-start(), calls=%async_computation.5 | async-start | bytes 11280384 | tf_op jit(solution)/shard_map/all_gather | solution.py:472
  54.5 27.8 %collective-permute-start.1 = (bf16[512,1152]{1,0:T(8,128)(2,1)}, bf16[512,1152]{1,0:T(8,128)(2,1)S(1)}, u32[]{:S(2)}, u32[]{:S(2)}) collective-permute-start(bf16[512,1152]{1,0:T(8,128)(2,1)} %copy_after.3), channel_id=1, source_target_pairs={{0,1},{1,2},{2,3},{4,5},{5,6},{6,7},{8,9},{9,10},{10,11},{12,13},{... | collective-permute-start | bytes 3538952 | tf_op jit(solution)/shard_map/ppermute | solution.py:434
  57.1 29.3 %collective-permute-start = (bf16[512,1152]{1,0:T(8,128)(2,1)}, bf16[512,1152]{1,0:T(8,128)(2,1)S(1)}, u32[]{:S(2)}, u32[]{:S(2)}) collective-permute-start(bf16[512,1152]{1,0:T(8,128)(2,1)} %copy_after.3), channel_id=1, source_target_pairs={{1,0},{2,1},{3,2},{5,4},{6,5},{7,6},{9,8},{10,9},{11,10},{13,12},{... | collective-permute-start | bytes 3538952 | tf_op jit(solution)/shard_map/ppermute | solution.py:433
  89.2 29.1 %copy-start.42 = (f32[1152,6]{0,1:T(8,128)S(1)}, f32[1152,6]{0,1:T(8,128)}, u32[]{:S(2)}) copy-start(f32[1152,6]{0,1:T(8,128)} %reshape.656) | copy-start | bytes 82948
  89.2 24.8 %collective-permute-start.9 = (bf16[144,1076]{1,0:T(8,128)(2,1)}, bf16[144,1076]{1,0:T(8,128)(2,1)S(1)}, u32[]{:S(2)}, u32[]{:S(2)}) collective-permute-start(bf16[144,1076]{1,0:T(8,128)(2,1)} %copy_after.4), channel_id=1, source_target_pairs={{0,2},{1,3},{2,0},{3,1},{4,6},{5,7},{6,4},{7,5},{8,10},{9,11},{10,... | collective-permute-start | bytes 929672 | tf_op jit(solution)/shard_map/ppermute | solution.py:78
  90.5 23.5 %collective-permute-start.8 = (bf16[144,1076]{1,0:T(8,128)(2,1)}, bf16[144,1076]{1,0:T(8,128)(2,1)S(1)}, u32[]{:S(2)}, u32[]{:S(2)}) collective-permute-start(bf16[144,1076]{1,0:T(8,128)(2,1)} %copy_after.4), channel_id=1, source_target_pairs={{0,1},{1,2},{2,3},{3,0},{4,5},{5,6},{6,7},{7,4},{8,9},{9,10},{10,1... | collective-permute-start | bytes 929672 | tf_op jit(solution)/shard_map/ppermute | solution.py:78
  90.6 23.4 %collective-permute-start.2 = (bf16[144,1076]{1,0:T(8,128)(2,1)}, bf16[144,1076]{1,0:T(8,128)(2,1)S(1)}, u32[]{:S(2)}, u32[]{:S(2)}) collective-permute-start(bf16[144,1076]{1,0:T(8,128)(2,1)} %copy_after.4), channel_id=1, source_target_pairs={{0,3},{1,0},{2,1},{3,2},{4,7},{5,4},{6,5},{7,6},{8,11},{9,8},{10,9... | collective-permute-start | bytes 929672 | tf_op jit(solution)/shard_map/ppermute | solution.py:78
  117.3 140.9 %all-gather.11.cloned.1.call-start = ((), (), s32[]{:S(2)}) async-start(), calls=%async_computation.6 | async-start | bytes 11280384 | tf_op jit(solution)/shard_map/all_gather | solution.py:511
  118.9 39.7 %collective-permute-start.3 = (bf16[512,1152]{1,0:T(8,128)(2,1)}, bf16[512,1152]{1,0:T(8,128)(2,1)S(1)}, u32[]{:S(2)}, u32[]{:S(2)}) collective-permute-start(bf16[512,1152]{1,0:T(8,128)(2,1)} %after.29.refs_1_), channel_id=1, source_target_pairs={{1,0},{2,1},{3,2},{5,4},{6,5},{7,6},{9,8},{10,9},{11,10},{13,12},{... | collective-permute-start | bytes 3538952 | tf_op jit(solution)/shard_map/ppermute | solution.py:449
  120.3 38.2 %collective-permute-start.4 = (bf16[512,1152]{1,0:T(8,128)(2,1)}, bf16[512,1152]{1,0:T(8,128)(2,1)}, u32[]{:S(2)}, u32[]{:S(2)}) collective-permute-start(bf16[512,1152]{1,0:T(8,128)(2,1)} %after.30.refs_2_), channel_id=1, source_target_pairs={{0,1},{1,2},{2,3},{4,5},{5,6},{6,7},{8,9},{9,10},{10,11},{12,13},{... | collective-permute-start | bytes 3538952 | tf_op jit(solution)/shard_map/ppermute | solution.py:450
  163.8 18.8 %collective-permute-start.7 = (bf16[144,1076]{1,0:T(8,128)(2,1)}, bf16[144,1076]{1,0:T(8,128)(2,1)}, u32[]{:S(2)}, u32[]{:S(2)}) collective-permute-start(bf16[144,1076]{1,0:T(8,128)(2,1)} %copy_after.5), channel_id=1, source_target_pairs={{0,3},{1,0},{2,1},{3,2},{4,7},{5,4},{6,5},{7,6},{8,11},{9,8},{10,9... | collective-permute-start | bytes 929672 | tf_op jit(solution)/shard_map/ppermute | solution.py:78
  163.8 30.0 %collective-permute-start.6 = (bf16[144,1076]{1,0:T(8,128)(2,1)}, bf16[144,1076]{1,0:T(8,128)(2,1)}, u32[]{:S(2)}, u32[]{:S(2)}) collective-permute-start(bf16[144,1076]{1,0:T(8,128)(2,1)} %copy_after.5), channel_id=1, source_target_pairs={{0,2},{1,3},{2,0},{3,1},{4,6},{5,7},{6,4},{7,5},{8,10},{9,11},{10,... | collective-permute-start | bytes 929672 | tf_op jit(solution)/shard_map/ppermute | solution.py:78
  166.2 27.7 %collective-permute-start.5 = (bf16[144,1076]{1,0:T(8,128)(2,1)}, bf16[144,1076]{1,0:T(8,128)(2,1)}, u32[]{:S(2)}, u32[]{:S(2)}) collective-permute-start(bf16[144,1076]{1,0:T(8,128)(2,1)} %copy_after.5), channel_id=1, source_target_pairs={{0,1},{1,2},{2,3},{3,0},{4,5},{5,6},{6,7},{7,4},{8,9},{9,10},{10,1... | collective-permute-start | bytes 929672 | tf_op jit(solution)/shard_map/ppermute | solution.py:78
  198.4 142.8 %reduce-scatter.5.cloned.1.call-start = ((), (), s32[]{:S(2)}) async-start(), calls=%async_computation.7 | async-start | bytes 11280384 | tf_op jit(solution)/shard_map/reduce_scatter | solution.py:537
  198.4 21.2 %copy-start.64 = (f32[1152]{0:T(1024)S(1)}, f32[1152]{0:T(1024)}, u32[]{:S(2)}) copy-start(f32[1152]{0:T(1024)} %get-tuple-element.42) | copy-start | bytes 13828
  223.7 75.5 %copy-start.20 = (f32[512,1152]{1,0:T(8,128)}, f32[512,1152]{1,0:T(8,128)S(1)}, u32[]{:S(2)}) copy-start(f32[512,1152]{1,0:T(8,128)S(1)} %get-tuple-element.107) | copy-start | bytes 7077892
  223.8 48.7 %copy-start.56 = (f32[512]{0:T(512)}, f32[512]{0:T(512)S(1)}, u32[]{:S(2)}) copy-start(f32[512]{0:T(512)S(1)} %broadcast_multiply_fusion.5) | copy-start | bytes 6148
  225.0 17.4 %copy-start.18 = (bf16[512,1152]{1,0:T(8,128)(2,1)S(1)}, bf16[512,1152]{1,0:T(8,128)(2,1)}, u32[]{:S(2)}) copy-start(bf16[512,1152]{1,0:T(8,128)(2,1)} %get-tuple-element.51.refs_7_.refs_0_) | copy-start | bytes 3538948
  250.7 206.8 %reduce-scatter.9.cloned.1.call-start = ((), (), s32[]{:S(2)}) async-start(), calls=%async_computation.9 | async-start | bytes 11280384 | tf_op jit(solution)/shard_map/reduce_scatter | solution.py:550
  258.2 16.7 %copy-start.63 = (f32[1152]{0:T(1024)S(1)}, f32[1152]{0:T(1024)}, u32[]{:S(2)}) copy-start(f32[1152]{0:T(1024)} %get-tuple-element.40) | copy-start | bytes 13828
  258.2 16.7 %copy-start.66 = (f32[512]{0:T(512)S(1)}, f32[512]{0:T(512)}, u32[]{:S(2)}) copy-start(f32[512]{0:T(512)} %add_rsqrt_fusion.1) | copy-start | bytes 6148
  283.5 268.0 %reduce-scatter.7.cloned.1.call-start = ((), (), s32[]{:S(2)}) async-start(), calls=%async_computation.8 | async-start | bytes 11943936 | tf_op jit(solution)/shard_map/reduce_scatter | solution.py:631
  343.6 57.6 %collective-permute-start.12 = (bf16[144,1076]{1,0:T(8,128)(2,1)S(1)}, bf16[144,1076]{1,0:T(8,128)(2,1)}, u32[]{:S(2)}, u32[]{:S(2)}) collective-permute-start(bf16[144,1076]{1,0:T(8,128)(2,1)S(1)} %get-tuple-element.71), channel_id=1, source_target_pairs={{0,1},{1,2},{2,3},{3,0},{4,5},{5,6},{6,7},{7,4},{8,9},{9,10},{10,1... | collective-permute-start | bytes 929672 | tf_op jit(solution)/shard_map/ppermute | solution.py:594
  350.5 50.7 %collective-permute-start.11 = (bf16[144,1076]{1,0:T(8,128)(2,1)}, bf16[144,1076]{1,0:T(8,128)(2,1)}, u32[]{:S(2)}, u32[]{:S(2)}) collective-permute-start(bf16[144,1076]{1,0:T(8,128)(2,1)} %get-tuple-element.72), channel_id=1, source_target_pairs={{0,2},{1,3},{2,0},{3,1},{4,6},{5,7},{6,4},{7,5},{8,10},{9,11},{10,... | collective-permute-start | bytes 929672 | tf_op jit(solution)/shard_map/ppermute | solution.py:594
  350.5 50.7 %collective-permute-start.10 = (bf16[144,1076]{1,0:T(8,128)(2,1)}, bf16[144,1076]{1,0:T(8,128)(2,1)}, u32[]{:S(2)}, u32[]{:S(2)}) collective-permute-start(bf16[144,1076]{1,0:T(8,128)(2,1)} %get-tuple-element.73), channel_id=1, source_target_pairs={{0,3},{1,0},{2,1},{3,2},{4,7},{5,4},{6,5},{7,6},{8,11},{9,8},{10,9... | collective-permute-start | bytes 929672 | tf_op jit(solution)/shard_map/ppermute | solution.py:594
  372.4 25.5 %copy-start.9 = (bf16[1536,1152]{1,0:T(8,128)(2,1)S(1)}, bf16[1536,1152]{1,0:T(8,128)(2,1)}, u32[]{:S(2)}) copy-start(bf16[1536,1152]{1,0:T(8,128)(2,1)} %copy-done.7) | copy-start | bytes 10616836
  372.4 25.5 %copy-start.15 = (bf16[16,72,512]{2,1,0:T(8,128)(2,1)S(1)}, bf16[16,72,512]{2,1,0:T(8,128)(2,1)}, u32[]{:S(2)}) copy-start(bf16[16,72,512]{2,1,0:T(8,128)(2,1)} %get-tuple-element.28.refs_1_) | copy-start | bytes 3538948
  380.6 40.0 %collective-permute-start.14 = (bf16[512,1152]{1,0:T(8,128)(2,1)}, bf16[512,1152]{1,0:T(8,128)(2,1)}, u32[]{:S(2)}, u32[]{:S(2)}) collective-permute-start(bf16[512,1152]{1,0:T(8,128)(2,1)} %get-tuple-element.74.refs_2_.refs_4_), channel_id=1, source_target_pairs={{1,0},{2,1},{3,2},{5,4},{6,5},{7,6},{9,8},{10,9},{11,10},{13,12},{... | collective-permute-start | bytes 3538952 | tf_op jit(solution)/shard_map/ppermute | solution.py:625
  381.9 39.9 %collective-permute-start.13 = (bf16[512,1152]{1,0:T(8,128)(2,1)}, bf16[512,1152]{1,0:T(8,128)(2,1)}, u32[]{:S(2)}, u32[]{:S(2)}) collective-permute-start(bf16[512,1152]{1,0:T(8,128)(2,1)} %get-tuple-element.75.refs_1_.refs_2_), channel_id=1, source_target_pairs={{0,1},{1,2},{2,3},{4,5},{5,6},{6,7},{8,9},{9,10},{10,11},{12,13},{... | collective-permute-start | bytes 3538952 | tf_op jit(solution)/shard_map/ppermute | solution.py:624
  430.4 154.6 %reduce-scatter.11.cloned.1.call-start = ((), (), s32[]{:S(2)}) async-start(), calls=%async_computation.10 | async-start | bytes 1658880 | tf_op jit(solution)/shard_map/reduce_scatter | solution.py:694
  460.0 12.7 %collective-permute-start.17 = (bf16[144,1076]{1,0:T(8,128)(2,1)S(1)}, bf16[144,1076]{1,0:T(8,128)(2,1)S(1)}, u32[]{:S(2)}, u32[]{:S(2)}) collective-permute-start(bf16[144,1076]{1,0:T(8,128)(2,1)S(1)} %get-tuple-element.68), channel_id=1, source_target_pairs={{0,1},{1,2},{2,3},{3,0},{4,5},{5,6},{6,7},{7,4},{8,9},{9,10},{10,1... | collective-permute-start | bytes 929672 | tf_op jit(solution)/shard_map/ppermute | solution.py:637
  462.4 22.1 %collective-permute-start.16 = (bf16[144,1076]{1,0:T(8,128)(2,1)}, bf16[144,1076]{1,0:T(8,128)(2,1)S(1)}, u32[]{:S(2)}, u32[]{:S(2)}) collective-permute-start(bf16[144,1076]{1,0:T(8,128)(2,1)} %get-tuple-element.69), channel_id=1, source_target_pairs={{0,2},{1,3},{2,0},{3,1},{4,6},{5,7},{6,4},{7,5},{8,10},{9,11},{10,... | collective-permute-start | bytes 929672 | tf_op jit(solution)/shard_map/ppermute | solution.py:637
  464.0 21.3 %collective-permute-start.15 = (bf16[144,1076]{1,0:T(8,128)(2,1)}, bf16[144,1076]{1,0:T(8,128)(2,1)S(1)}, u32[]{:S(2)}, u32[]{:S(2)}) collective-permute-start(bf16[144,1076]{1,0:T(8,128)(2,1)} %get-tuple-element.70), channel_id=1, source_target_pairs={{0,3},{1,0},{2,1},{3,2},{4,7},{5,4},{6,5},{7,6},{8,11},{9,8},{10,9... | collective-permute-start | bytes 929672 | tf_op jit(solution)/shard_map/ppermute | solution.py:637
  469.5 40.2 %collective-permute-start.19 = (bf16[512,1152]{1,0:T(8,128)(2,1)}, bf16[512,1152]{1,0:T(8,128)(2,1)S(1)}, u32[]{:S(2)}, u32[]{:S(2)}) collective-permute-start(bf16[512,1152]{1,0:T(8,128)(2,1)} %add_convert_fusion.refs_2_), channel_id=1, source_target_pairs={{1,0},{2,1},{3,2},{5,4},{6,5},{7,6},{9,8},{10,9},{11,10},{13,12},{... | collective-permute-start | bytes 3538952 | tf_op jit(solution)/shard_map/ppermute | solution.py:653
  489.9 34.4 %collective-permute-start.18 = (bf16[512,1152]{1,0:T(8,128)(2,1)}, bf16[512,1152]{1,0:T(8,128)(2,1)}, u32[]{:S(2)}, u32[]{:S(2)}) collective-permute-start(bf16[512,1152]{1,0:T(8,128)(2,1)} %add_convert_fusion.1.refs_1_), channel_id=1, source_target_pairs={{0,1},{1,2},{2,3},{4,5},{5,6},{6,7},{8,9},{9,10},{10,11},{12,13},{... | collective-permute-start | bytes 3538952 | tf_op jit(solution)/shard_map/ppermute | solution.py:652
  529.0 13.3 %copy-start.34 = (bf16[144,1076]{1,0:T(8,128)(2,1)S(1)}, bf16[144,1076]{1,0:T(8,128)(2,1)}, u32[]{:S(2)}) copy-start(bf16[144,1076]{1,0:T(8,128)(2,1)} %after.47.refs_6_) | copy-start | bytes 929668
  529.0 13.3 %copy-start.36 = (bf16[144,1076]{1,0:T(8,128)(2,1)S(1)}, bf16[144,1076]{1,0:T(8,128)(2,1)}, u32[]{:S(2)}) copy-start(bf16[144,1076]{1,0:T(8,128)(2,1)} %after.48.refs_7_) | copy-start | bytes 929668
  529.9 16.7 %copy-start.65 = (f32[512]{0:T(512)S(1)}, f32[512]{0:T(512)}, u32[]{:S(2)}) copy-start(f32[512]{0:T(512)} %get-tuple-element.32) | copy-start | bytes 6148
  530.0 4.7 collective-permute-start.20
  534.7 5.1 collective-permute-start.21
  539.8 2.4 collective-permute-start.22
  542.2 4.4 collective-permute-start.23
  546.6 4.2 collective-permute-start.24
  (59 other events, 271.7 us)
Sparse Core Ops, SparseCore 0:
  10.6 36.9 all-gather.12
  52.1 62.7 all-gather.6
  117.4 65.3 all-gather.8
  198.5 59.7 all-gather.10
  261.7 79.3 reduce-scatter.4
  345.0 79.1 reduce-scatter.8
  430.5 81.6 reduce-scatter.6
  554.6 30.4 reduce-scatter.10

commit v3 on v2

--- a/solution.py
+++ b/solution.py
@@ -54,6 +54,7 @@
         out_specs=pl.BlockSpec(memory_space=pl.ANY),
         out_shape=jax.ShapeDtypeStruct(value.shape, value.dtype),
         input_output_aliases={0: 0},
+        compiler_params=pltpu.CompilerParams(vmem_limit_bytes=54 << 20),
         name="after",
     )(value, *earlier)
 
@@ -68,6 +69,7 @@
         in_specs=[vmem] + [pl.BlockSpec(memory_space=pl.ANY)] * len(earlier),
         out_specs=vmem,
         out_shape=jax.ShapeDtypeStruct(value.shape, value.dtype),
+        compiler_params=pltpu.CompilerParams(vmem_limit_bytes=54 << 20),
         name="copy_after",
     )(value, *earlier)
 
@@ -98,45 +100,38 @@
         in_specs=[vmem],
         out_specs=vmem,
         out_shape=jax.ShapeDtypeStruct((owners, rows, kinds * size), value.dtype),
+        compiler_params=pltpu.CompilerParams(vmem_limit_bytes=54 << 20),
         name="by_owner",
     )(value).reshape(owners * rows, kinds * size)
 
 
-def norm_kernel(*refs):
-    x_refs, gain_ref, shift_ref, out_ref = refs[:-3], refs[-3], refs[-2], refs[-1]
-    here, width = x_refs[0].shape
-    block = math.gcd(here, 64)
-    gain, shift = gain_ref[...], shift_ref[...]
-    for position, x_ref in enumerate(x_refs):
-
-        def step(i, carry):
-            start = pl.multiple_of(i * block, block)
-            values = x_ref[pl.ds(start, block), :].astype(F32)
-            center = values - jnp.mean(values, axis=1, keepdims=True)
-            spread = jnp.mean(center * center, axis=1, keepdims=True)
-            result = center * lax.rsqrt(spread + 1e-06) * gain + shift
-            target = pl.multiple_of(position * here + i * block, block)
-            out_ref[pl.ds(target, block), :] = result.astype(BF)
-            return carry
-
-        lax.fori_loop(0, here // block, step, 0)
-
-
-def norm_tokens(tokens, gain, shift):
-    here, width = tokens[0].shape
-    rows = here * len(tokens)
-    vmem = pl.BlockSpec(memory_space=pltpu.VMEM)
+def norm_kernel(x_ref, gain_ref, shift_ref, *rest):
+    values = x_ref[...].astype(F32)
+    center = values - jnp.mean(values, axis=1, keepdims=True)
+    spread = jnp.mean(center * center, axis=1, keepdims=True)
+    result = center * lax.rsqrt(spread + 1e-06) * gain_ref[...] + shift_ref[...]
+    rest[-1][...] = result.astype(BF)
+
+
+def norm_slot(tokens, gain, shift, slot, slots, *into):
+    here, width = tokens.shape
+    block = math.gcd(here, 128)
+    steps = here // block
+    whole = pl.BlockSpec((1, width), lambda i: (0, 0))
     return pl.pallas_call(
         norm_kernel,
-        in_specs=[vmem] * (len(tokens) + 2),
-        out_specs=vmem,
-        out_shape=jax.ShapeDtypeStruct((rows, width), BF),
-        compiler_params=pltpu.CompilerParams(vmem_limit_bytes=32 << 20),
+        grid=(steps,),
+        in_specs=[pl.BlockSpec((block, width), lambda i: (i, 0)), whole, whole]
+        + [pl.BlockSpec(memory_space=pl.ANY)] * len(into),
+        out_specs=pl.BlockSpec((block, width), lambda i: (slot * steps + i, 0)),
+        out_shape=jax.ShapeDtypeStruct((slots * here, width), BF),
+        input_output_aliases={3: 0} if into else {},
         cost_estimate=pl.CostEstimate(
-            flops=10 * rows * width, bytes_accessed=4 * rows * width, transcendentals=rows
+            flops=10 * here * width, bytes_accessed=4 * here * width, transcendentals=here
         ),
-        name="norm_tokens",
-    )(*tokens, gain[None], shift[None])
+        compiler_params=pltpu.CompilerParams(vmem_limit_bytes=54 << 20),
+        name="norm_slot",
+    )(tokens, gain[None], shift[None], *into)
 
 
 def attend_kernel(
@@ -208,7 +203,7 @@
             jax.ShapeDtypeStruct((heads, dim, q_len), BF),
             jax.ShapeDtypeStruct((heads, 1, q_len), F32),
         ],
-        compiler_params=pltpu.CompilerParams(vmem_limit_bytes=56 << 20),
+        compiler_params=pltpu.CompilerParams(vmem_limit_bytes=54 << 20),
         cost_estimate=pl.CostEstimate(
             flops=4 * heads * rows * q_len * k_len,
             bytes_accessed=4 * heads * rows * (q_len + k_len),
@@ -301,7 +296,7 @@
             jax.ShapeDtypeStruct((heads, dim, q_len), BF),
             jax.ShapeDtypeStruct((2, heads, dim, k_len), BF),
         ],
-        compiler_params=pltpu.CompilerParams(vmem_limit_bytes=56 << 20),
+        compiler_params=pltpu.CompilerParams(vmem_limit_bytes=54 << 20),
         cost_estimate=pl.CostEstimate(
             flops=10 * heads * rows * q_len * k_len,
             bytes_accessed=8 * heads * rows * (q_len + k_len),
@@ -353,12 +348,10 @@
     own_seg = lax.dynamic_slice_in_dim(segment, me * here, here, 0)
     bias_piece = jnp.concatenate([query_bias[0], value_bias[0], up_bias[0]])
     bias_terms = split3(bias_piece).astype(BF).reshape(-1)
-    bias_rows = -(-bias_terms.shape[0] // (4 * cols * 8)) * 8
-    bias_terms = jnp.pad(bias_terms, (0, bias_rows * 4 * cols - bias_terms.shape[0]))
-    attn_piece = jnp.concatenate(
-        [query_weight[0], key_weight[0], value_weight[0], out_weight[0]], axis=1
-    )
-    attn_piece = jnp.concatenate([attn_piece, bias_terms.reshape(bias_rows, 4 * cols)], axis=0)
+    bias_rows = -(-bias_terms.shape[0] // (3 * cols * 8)) * 8
+    bias_terms = jnp.pad(bias_terms, (0, bias_rows * 3 * cols - bias_terms.shape[0]))
+    attn_piece = jnp.concatenate([query_weight[0], key_weight[0], value_weight[0]], axis=1)
+    attn_piece = jnp.concatenate([attn_piece, bias_terms.reshape(bias_rows, 3 * cols)], axis=0)
     attn_parts = lax.all_gather(attn_piece, "tp", axis=0)
     vectors = jnp.concatenate([ln1_gain, ln1_bias, out_bias, ln2_gain, ln2_bias, down_bias], axis=0)
     vectors = lax.all_gather(vectors, "fsdp", axis=1, tiled=True)
@@ -369,7 +362,6 @@
         if use_later or use_prior:
             slots.append((j, use_later, use_prior))
     slots.sort(key=lambda slot: min(slot[0], n - slot[0]))
-    near = 1 + sum(min(j, n - j) == 1 for j, _, _ in slots)
 
     key_segs = [own_seg]
     for j, use_later, use_prior in slots:
@@ -417,8 +409,19 @@
     grad_two = cotangent[0].astype(F32) * valid_col
     grad_mixed = grad_two.astype(BF)
     down_bias_part = jnp.sum(grad_mixed, axis=0, dtype=F32)
+    later = [x_own, lax.ppermute(x_own, "tp", to_left)]
+    prior = [x_own, lax.ppermute(x_own, "tp", to_right)]
     attn_parts = after(
-        attn_parts, vectors, counts, indices, k_added, q_mask, down_bias_part, grad_mixed
+        attn_parts,
+        vectors,
+        counts,
+        indices,
+        k_added,
+        q_mask,
+        down_bias_part,
+        grad_mixed,
+        later[1],
+        prior[1],
     )
     share = query_weight.shape[1]
     all_biases = jnp.sum(
@@ -428,85 +431,73 @@
         .astype(F32),
         axis=1,
     )
-    first = copy_after(x_own, attn_parts)
-    later, prior = [first], [first]
-    later.append(lax.ppermute(first, "tp", to_left))
-    prior.append(lax.ppermute(first, "tp", to_right))
     query_shift = all_biases[:, :cols].reshape(-1)
     value_shift = all_biases[:, cols : 2 * cols].reshape(-1)
     ring_order = (me - jnp.arange(n)) % n
     up_shift = jnp.take(all_biases[:, 2 * cols :], ring_order, axis=0).reshape(-1)
-
-    first_up = copy_after(
-        up_weight[0], later[1], prior[1], up_shift, query_shift, value_shift
-    )
-    up_slots = slots_along_tp(first_up, n)
-    far_later, far_prior = [later[1]], [prior[1]]
-    if reach > 1:
-        far_later = [after(later[1], up_slots[-1])]
-        far_prior = [after(prior[1], up_slots[-1])]
+    wide_piece = jnp.concatenate([out_weight[0], up_weight[0]], axis=1)
+    wide_slots = slots_along_tp(
+        copy_after(wide_piece, attn_parts, up_shift, query_shift, value_shift), n
+    )
+    later[1], prior[1] = after(later[1], *wide_slots[1:]), after(prior[1], *wide_slots[1:])
     for _ in range(reach - 1):
-        far_later.append(lax.ppermute(far_later[-1], "tp", to_left))
-        far_prior.append(lax.ppermute(far_prior[-1], "tp", to_right))
-    later, prior = [x_own] + far_later, [x_own] + far_prior
-
-    def tokens_of(slot, *gates):
-        j, use_later, use_prior = slot
-        from_later = after(later[j], *gates) if use_later and gates else later[j] if use_later else None
-        from_prior = after(prior[n - j], *gates) if use_prior and gates else prior[n - j] if use_prior else None
+        later.append(lax.ppermute(later[-1], "tp", to_left))
+        prior.append(lax.ppermute(prior[-1], "tp", to_right))
+
+    slot_count = 1 + len(slots)
+    normed_all = norm_slot(x_own, gain_one, shift_one, 0, slot_count)
+    for position, (j, use_later, use_prior) in enumerate(slots):
         if use_later and use_prior:
-            return jnp.where(me + j < n, from_later, from_prior)
-        return from_later if use_later else from_prior
-
-    def widen(parts, added):
-        parts = [part.reshape(heads, HEAD_DIM, part.shape[-1]) for part in parts]
-        body = jnp.concatenate(parts, axis=2) if len(parts) > 1 else parts[0]
+            tokens = jnp.where(me + j < n, later[j], prior[n - j])
+        else:
+            tokens = later[j] if use_later else prior[n - j]
+        if min(j, n - j) == 1:
+            normed_all = norm_slot(
+                tokens, gain_one, shift_one, position + 1, slot_count, normed_all
+            )
+        else:
+            normed_all = norm_slot(
+                tokens, gain_one, shift_one, position + 1, slot_count, normed_all
+            )
+    first_down = copy_after(down_weight[0], later[-1], prior[-1])
+
+    def widen(body, added):
+        body = body.reshape(heads, HEAD_DIM, body.shape[-1])
         added = jnp.broadcast_to(added, (heads, AUG, body.shape[-1]))
         return jnp.concatenate([body, added.astype(BF)], axis=1)
 
     attn_shard = jnp.concatenate(
-        [attn_parts[o, :share, t * cols : (t + 1) * cols] for t in range(4) for o in range(n)],
+        [attn_parts[o, :share, t * cols : (t + 1) * cols] for t in range(3) for o in range(n)],
         axis=1,
     )
     attn_full = lax.all_gather(attn_shard, "fsdp", axis=0, tiled=True)
-    up_full = lax.all_gather(jnp.concatenate(up_slots, axis=1), "fsdp", axis=0, tiled=True)
+    out_slots = jnp.take(jnp.stack([s[:, :cols] for s in wide_slots]), ring_order, axis=0)
+    wide_shard = jnp.concatenate(
+        [out_slots[o] for o in range(n)] + [s[:, cols:] for s in wide_slots], axis=1
+    )
+    wide_full = lax.all_gather(wide_shard, "fsdp", axis=0, tiled=True)
+    out_full, up_full = wide_full[:, :hh], wide_full[:, hh:]
 
     query_full = attn_full[:, :hh]
     key_full = attn_full[:, hh : 2 * hh]
     value_full = attn_full[:, 2 * hh : 3 * hh]
     kv_full = attn_full[:, hh : 3 * hh]
-    out_full = attn_full[:, 3 * hh : 4 * hh]
 
     x = x_own.astype(F32)
-    normed_near = norm_tokens(
-        [x_own] + [tokens_of(slot) for slot in slots[: near - 1]], gain_one, shift_one
-    )
-    normed = normed_near[:here]
+    normed = normed_all[:here]
     queries = (
         (product("td,dc->ct", normed, query_full) + query_shift[:, None])
         * (scale * math.log2(math.e))
     ).astype(BF)
     q_rest = jnp.zeros((AUG - (pics + 1), here), F32)
-    q_aug = widen([queries], jnp.concatenate([q_mask, q_rest], axis=0))
-
-    def keys_values(tokens):
-        keys = product("td,dc->ct", tokens, key_full).astype(BF)
-        values = product("td,dc->ct", tokens, value_full) + value_shift[:, None]
-        return keys, values.astype(BF)
-
-    pieces = [keys_values(normed_near)]
-    gates = (pieces[0][0], pieces[0][1], q_aug)
-    down_first = far_later[-1], far_prior[-1]
-    if slots[near - 1 :]:
-        far_tokens = [tokens_of(slot, *gates) for slot in slots[near - 1 :]]
-        normed_far = norm_tokens(far_tokens, gain_one, shift_one)
-        pieces.append(keys_values(normed_far))
-        down_first = far_tokens
-    normed_all = jnp.concatenate([normed_near] + [normed_far] * (len(pieces) - 1), axis=0)
-    k_aug = after(widen([piece[0] for piece in pieces], k_added))
-    v_aug = after(widen([piece[1] for piece in pieces], v_added))
+    q_aug = widen(queries, jnp.concatenate([q_mask, q_rest], axis=0))
+
+    keys = product("td,dc->ct", normed_all, key_full).astype(BF)
+    values = product("td,dc->ct", normed_all, value_full) + value_shift[:, None]
+    k_aug = after(widen(keys, k_added))
+    v_aug = after(widen(values.astype(BF), v_added))
+    down_slots = slots_along_tp(first_down, n, k_aug, v_aug)
     group = 4 if heads % 8 == 0 else 1
-    down_slots = slots_along_tp(copy_after(down_weight[0], *down_first), n, k_aug, v_aug)
     down_shard = jnp.concatenate(down_slots, axis=1)
     down_full = lax.all_gather(down_shard, "fsdp", axis=0, tiled=True)
     attended, log_total = attend(
@@ -560,7 +551,7 @@
         ],
         axis=1,
     )
-    g_aug = widen([grad_attended], g_added)
+    g_aug = widen(grad_attended, g_added)
     q_added = jnp.concatenate(
         [
             jnp.broadcast_to(q_mask, (heads, pics + 1, here)),
@@ -569,7 +560,7 @@
         ],
         axis=1,
     )
-    q_aug_back = widen([queries], q_added)
+    q_aug_back = widen(queries, q_added)
     def back_part(part, before, *earlier):
         return attend_back(
             q_aug_back,
@@ -609,16 +600,21 @@
     to_later = [None] * (reach + 1)
     to_prior = [None] * (reach + 1)
 
-    def send_shares(distance, dkv):
+    def send_shares(distance, dkv, sides="both"):
         for i, (j, use_later, use_prior) in enumerate(slots):
-            if min(j, n - j) != distance:
+            to_right_here = use_later and j == distance and sides != "prior"
+            to_left_here = use_prior and n - j == distance and sides != "later"
+            if not (to_right_here or to_left_here):
                 continue
             part = share_of(i + 1, dkv).astype(BF)
             zero = jnp.zeros_like(part)
-            if use_later and j == distance:
+            if to_right_here:
                 to_later[j] = jnp.where(me + j < n, part, zero)
-            if use_prior and n - j == distance:
+            if to_left_here:
                 to_prior[n - j] = jnp.where(me + j >= n, part, zero)
+
+    def joined(moving, share_here):
+        return (moving.astype(F32) + share_here.astype(F32)).astype(BF)
 
     send_shares(reach, dkv)
     moving_right = lax.ppermute(to_later[reach], "tp", to_right)
@@ -626,13 +622,15 @@
     dkv = after(dkv, to_later[reach], to_prior[reach], *down_moved)
     query_grad = product("td,ct->dc", normed, dq).astype(BF)
     kv_grad = product("td,ct->dc", normed_all, dkv).astype(BF)
-    out_grad = after(out_grad, kv_grad, query_grad, moving_right, moving_left)
-    attn_grad = jnp.concatenate([query_grad, kv_grad, out_grad], axis=1)
+    gates = (kv_grad, query_grad)
+    if reach > 1:
+        dkv = after(dkv, *gates)
+        for distance in reversed(range(2, reach)):
+            send_shares(distance, dkv)
+        gates = (*gates, moving_right, moving_left)
+    attn_grad = jnp.concatenate([query_grad, kv_grad, after(out_grad, *gates)], axis=1)
     attn_scattered = lax.psum_scatter(attn_grad, "fsdp", scatter_dimension=0, tiled=True)
-    query_bias_part = jnp.sum(dq, axis=1, dtype=F32)
-    dkv = after(dkv, attn_grad)
-    for distance in reversed(range(1, reach)):
-        send_shares(distance, dkv)
+    dkv, up_scattered = after(dkv, attn_grad), after(up_scattered, attn_grad)
     up_moved = [
         lax.ppermute(
             up_scattered[:, s * units : (s + 1) * units],
@@ -641,29 +639,29 @@
         )
         for s in range(1, n)
     ]
-    near_shares = [t for t in to_later[1:] + to_prior[1:] if t is not None]
-    for distance in reversed(range(1, reach)):
-        up_moved = [after(moved, *near_shares) for moved in up_moved]
-        moving_right = after(moving_right, *near_shares, *up_moved)
-        moving_left = after(moving_left, *near_shares)
-        moving_right = (moving_right.astype(F32) + to_later[distance].astype(F32)).astype(BF)
-        moving_left = (moving_left.astype(F32) + to_prior[distance].astype(F32)).astype(BF)
-        dkv = after(dkv, moving_right, moving_left)
+    for distance in reversed(range(2, reach)):
+        moving_right = lax.ppermute(joined(moving_right, to_later[distance]), "tp", to_right)
+        moving_left = lax.ppermute(joined(moving_left, to_prior[distance]), "tp", to_left)
+    if reach > 1:
+        send_shares(1, dkv, "later")
+        moving_right = joined(moving_right, to_later[1])
+        dkv, dq = after(dkv, moving_right), after(dq, moving_right)
         moving_right = lax.ppermute(moving_right, "tp", to_right)
-        moving_left = lax.ppermute(moving_left, "tp", to_left)
     own_share = share_of(0, dkv) + product("ct,dc->td", dq, query_full)
-    moving_right, moving_left = after(moving_right, own_share), after(moving_left, own_share)
+    up_moved = [after(moved, own_share) for moved in up_moved]
+    if reach > 1:
+        dkv = after(dkv, *up_moved)
+        send_shares(1, dkv, "prior")
+        moving_right = after(moving_right, to_prior[1])
+        moving_left = lax.ppermute(joined(moving_left, to_prior[1]), "tp", to_left)
+    last_sent = [t for t in (own_share, to_prior[1]) if t is not None]
     grad_normed = own_share + moving_right.astype(F32) + moving_left.astype(F32)
 
-    def summed(scattered, moved):
-        return sum((m.astype(F32) for m in moved), scattered[:, :units].astype(F32))
-
-    down_weight_grad = summed(down_scattered, down_moved)
-    up_weight_grad = summed(up_scattered, up_moved)
     one_hat, one_rstd = xhat_of(x)
     grad_x, gain_one_part, shift_one_part = norm_back(grad_normed, one_hat, one_rstd, gain_one)
     input_grad = grad_middle + grad_x
 
+    query_bias_part = jnp.sum(dq, axis=1, dtype=F32)
     value_bias_part = jnp.sum(dkv[hh:], axis=1, dtype=F32)
     vector_part = jnp.concatenate(
         [
@@ -688,9 +686,14 @@
             bit *= 2
         return value
 
+    def summed(scattered, moved):
+        return sum((m.astype(F32) for m in moved), scattered[:, :units].astype(F32))
+
+    down_weight_grad = summed(down_scattered, down_moved)
+    up_weight_grad = summed(up_scattered, up_moved)
+    attn_owned = by_owner(after(attn_scattered, *last_sent), n, 4)
+    small = after(small, attn_owned)
     small = sum_over(sum_over(small, "tp"), "fsdp")
-    attn_scattered = after(attn_scattered, small)
-    attn_owned = by_owner(attn_scattered, n, 4)
     attn_out = lax.psum_scatter(attn_owned, "tp", scatter_dimension=0, tiled=True).astype(F32)
     mixed = product("tf,df->td", after(active_units, attn_owned), down_full) + down_shift
     activations_out = ((middle + mixed) * valid_col).astype(BF)

time: 602 us -> 588 us (0.977)
  starting transfers between devices: 74.6 us -> 55.7 us
  local copies, waits for them, and re-layouts: 50.8 us -> 63.9 us
  matrix products: 165 us -> 154 us
  waiting for transfers between devices: 140 us -> 133 us
  Pallas kernels: 75.7 us -> 82 us
  other arithmetic: 60.6 us -> 66.7 us
    ppermute x5, waiting for transfers between devices: 24.9 us -> 41.9 us  [the longest x1 25.4 us: local(): moving_left = lax.ppermute(joined(moving_left, to_prior[1]), 'tp', to_left)]
    all_gather x1, waiting for transfers between devices: 15.6 us -> 0.87 us  [local(): attn_parts = lax.all_gather(attn_piece, 'tp', axis=0)]
    dot_general x21 -> x19, matrix products: 165 us -> 154 us  [product(): return jnp.einsum(form, left, right, preferred_element_type=F32)]
    ppermute x1, waiting for transfers between devices: 9.88 us -> 0.01 us  [local(): moving_right = lax.ppermute(moving_right, 'tp', to_right)]
    pallas_call x2 -> x4, Pallas kernels: 7.34 us -> 16 us  [norm_slot(): pl.pallas_call(norm_kernel, grid=(steps,), in_specs=[pl.BlockSpec((block,...]
    ppermute x3, waiting for transfers between devices: 13.1 us -> 21.3 us  [local(): lax.ppermute(up_scattered[:, s * units:(s + 1) * units], 'tp', [(i, (i -...]
    ppermute x5, waiting for transfers between devices: 11.3 us -> 3.75 us  [sum_over(): lax.ppermute(value, axis, [(i, i ^ bit) for i in range(count)])]
    ppermute x1, starting transfers between devices: 16.1 us -> 9.8 us  [local(): moving_right = lax.ppermute(to_later[reach], 'tp', to_right)]
  transfers between devices with their start and end apart: 33 -> 33, of which waited for: 18 -> 19; matrix products, arithmetic and copies ran while one was open for 42% -> 44% of each run, Pallas kernels for 12% -> 14%
where the time goes in v3:
time: 588 us; the launch traced here: 582 us
  matrix products  154 us (26%)
  waiting for transfers between devices  133 us (23%)
  Pallas kernels  82 us (14%)
  other arithmetic  66.7 us (11%)
  local copies, waits for them, and re-layouts  63.9 us (11%)
  starting transfers between devices  55.7 us (9%)
  between operations  17 us (3%)
  blocking collectives  9.36 us (2%)
    dot_general x19, matrix products, product(): return jnp.einsum(form, left, right, preferred_element_type=F32)  154 us
    pallas_call x2, Pallas kernels, attend_back(): pl.pallas_call(functools.partial(attend_back_kernel, q_block=q_block, k_b...  38.4 us
    ppermute x6, waiting for transfers between devices, slots_along_tp(): lax.ppermute(piece, 'tp', [(i, (i + distance) % count) for i in range(cou...  32.1 us
    ppermute x1, waiting for transfers between devices, local(): moving_left = lax.ppermute(joined(moving_left, to_prior[1]), 'tp', to_left)  25.4 us
    unnamed x183, local copies, waits for them, and re-layouts  24.9 us
    ppermute x3, waiting for transfers between devices, local(): lax.ppermute(up_scattered[:, s * units:(s + 1) * units], 'tp', [(i, (i -...  21.3 us
    pallas_call x1, Pallas kernels, attend(): pl.pallas_call(functools.partial(attend_kernel, q_block=q_block, k_block=...  21.2 us
    pallas_call x4, Pallas kernels, norm_slot(): pl.pallas_call(norm_kernel, grid=(steps,), in_specs=[pl.BlockSpec((block,...  16 us
  transfers between devices with their start and end apart: 33, of which 19 were waited for; matrix products, arithmetic and copies ran while one was open for 44% of the time, Pallas kernels for 14%

profile of v3, /device:TPU:0, one launch (start us, length us, event | category | flops | bytes accessed | tf_op | source)
XLA Modules:
  0.0 581.7 jit_solution(716977715494287963)
XLA Ops:
  7.2 5.1 collective-permute-start.1
  37.7 9.4 %all-gather.1 = f32[8,144,6]{1,2,0:T(8,128)S(1)} all-gather(f32[1,144,6]{1,2,0:T(8,128)} %bitcast.172), channel_id=1, replica_groups=mesh['fsdp'=8,'tp'=4] {'fsdp'}, dimensions={0}, use_global_device_ids=true | all-gather | bytes 31104 | tf_op jit(solution)/shard_map/all_gather | solution.py:357
  54.0 5.2 collective-permute-done.refs_8_.refs_0_
  77.4 5.0 collective-permute-done.4.refs_3_
  82.4 27.1 %collective-permute-done.3.refs_2_ = bf16[144,1364]{1,0:T(8,128)(2,1)S(1)} collective-permute-done((bf16[144,1364]{1,0:T(8,128)(2,1)}, bf16[144,1364]{1,0:T(8,128)(2,1)S(1)}, u32[]{:S(2)}, u32[]{:S(2)}) %collective-permute-start.3) | collective-permute-done | bytes 392864 | tf_op jit(solution)/shard_map/ppermute | solution.py:80
  111.0 3.2 concatenate.145
  115.6 4.6 collective-permute-start.6
  121.5 3.9 norm_slot.4.rest_0_
  125.4 4.0 norm_slot.5.rest_0_
  129.5 4.0 norm_slot.6.rest_0_
  133.4 10.1 %collective-permute-done.5.refs_0_ = bf16[512,1152]{1,0:T(8,128)(2,1)S(1)} collective-permute-done((bf16[512,1152]{1,0:T(8,128)(2,1)}, bf16[512,1152]{1,0:T(8,128)(2,1)S(1)}, u32[]{:S(2)}, u32[]{:S(2)}) %collective-permute-start.5) | collective-permute-done | bytes 1179680 | tf_op jit(solution)/shard_map/ppermute | solution.py:444
  147.6 3.7 collective-permute-start.9
  155.2 4.1 norm_slot.7
  159.2 9.2 %add_convert_fusion = bf16[1152,2048]{1,0:T(8,128)(2,1)S(1)} fusion(bf16[2048,1152]{1,0:T(8,128)(2,1)} %norm_slot.7, f32[1152]{0:T(1024)S(1)} %copy-done.54, bf16[1152,3456]{1,0:T(8,128)(2,1)} %all-gather.7.cloned.1.call-done), kind=kOutput, calls=%fused_computation.10 | convolution fusion | flops 5440536576 | bytes 12096000 | tf_op jit(solution)/shard_map/td,dc->ct/dot_general | solution.py:37
  172.9 8.5 %convolution_convert_fusion.5 = bf16[1152,2048]{1,0:T(8,128)(2,1)S(1)} fusion(bf16[2048,1152]{1,0:T(8,128)(2,1)S(1)} %bitcast.143, bf16[1152,3456]{1,0:T(8,128)(2,1)} %all-gather.7.cloned.1.call-done), kind=kOutput, calls=%fused_computation.27 | convolution fusion | flops 5438177280 | bytes 12091392 | tf_op jit(solution)/shard_map/td,dc->ct/dot_general | solution.py:37
  187.1 3.2 concatenate.144.rest_0_
  190.8 3.8 fusion.26
  196.1 21.2 %attend.1 = (bf16[16,72,512]{2,1,0:T(8,128)(2,1)}, f32[16,1,512]{2,1,0:T(1,128)}) custom-call(s32[1]{0:T(128)S(6)} %neg.49.refs_2_.count_ref, s32[8]{0:T(128)} %select_reduce_fusion.refs_3_.index_ref, bf16[16,80,512]{2,1,0:T(8,128)(2,1)} %pad_maximum_fusion.3.q_ref, bf16[16,80,2048]{2,1,0:T(8,128)(2,1)} %after.31.refs_1_.k_ref, ...), custom_call_target="tpu_custom_call" | custom-call | flops 5368709120 | bytes 13107200 | tf_op jit(solution)/shard_map/attend/pallas_call | solution.py:188
  217.3 4.2 fusion.100
  224.0 9.1 %multiply_convert_fusion = (bf16[512,4304]{1,0:T(8,128)(2,1)S(1)}, f32[512,4304]{1,0:T(8,128)}) fusion(f32[4304]{0:T(1024)S(1)} %copy-done.46, bf16[1152,5456]{1,0:T(8,128)(2,1)S(1)} %copy-done.84, f32[512,1152]{1,0:T(8,128)S(1)} %get-tuple-element.107, f32[1152]{0:T(1024)S(1)} %copy-done.72, f32[1152]{0:T(1024)S(1)} %get-tuple-element.41, ...), kind=kOutput, calls=%fused_computation.19 | convolution fusion | flops 5102190592 | bytes 25649152 | tf_op jit(solution)/shard_map/td,df->tf/dot_general | solution.py:37
  235.1 8.2 %convolution_convert_fusion.1.refs_1_ = bf16[1152,4304]{1,0:T(8,128)(2,1)} fusion(bf16[512,1152]{1,0:T(8,128)(2,1)S(1)} %copy-done.9, bf16[512,4304]{1,0:T(8,128)(2,1)S(1)} %get-tuple-element.108.refs_0_), kind=kOutput, calls=%fused_computation.4 | convolution fusion | flops 5082163200 | bytes 15503360 | tf_op jit(solution)/shard_map/td,tf->df/dot_general | solution.py:37
  243.7 11.2 %all-gather.11.cloned.1.call-done = bf16[1152,4304]{1,0:T(8,128)(2,1)} async-done(((bf16[144,4304]{1,0:T(8,128)(2,1)}), bf16[1152,4304]{1,0:T(8,128)(2,1)}) %all-gather.11.cloned.1.call-update) | async-done | bytes 9916432 | tf_op jit(solution)/shard_map/all_gather | solution.py:502
  254.9 13.9 %convert_reduce_fusion.1 = (f32[4304]{0:T(1024)}, bf16[512,4304]{1,0:T(8,128)(2,1)S(1)}) fusion(f32[512,4304]{1,0:T(8,128)} %get-tuple-element.109, bf16[512,1152]{1,0:T(8,128)(2,1)} %after.36, bf16[1152,4304]{1,0:T(8,128)(2,1)} %all-gather.11.cloned.1.call-done), kind=kOutput, calls=%fused_computation.18 | convolution fusion | flops 5125681152 | bytes 24335168 | tf_op jit(solution)/shard_map/td,df->tf/dot_general | solution.py:37
  271.3 8.7 %convolution_convert_fusion.rest_0_ = bf16[1152,4304]{1,0:T(8,128)(2,1)} fusion(bf16[512,4304]{1,0:T(8,128)(2,1)S(1)} %get-tuple-element.46, f32[512,1152]{1,0:T(8,128)S(1)} %get-tuple-element.107, f32[1152]{0:T(1024)S(1)} %copy-done.73, f32[1152]{0:T(1024)S(1)} %get-tuple-element.41, f32[512]{0:T(512)S(1)} %copy-done.75, f32[512]{0:T(512)S(1)} %broadcast_multiply_fusion.5), kind=kOutput, calls=%fused_computation.3 | convolution fusion | flops 5085112320 | bytes 16696320 | tf_op jit(solution)/shard_map/td,tf->df/dot_general | solution.py:37
  283.2 13.0 %multiply_reduce_fusion = (f32[1152]{0:T(1024)}, f32[512]{0:T(512)S(1)}, f32[512]{0:T(512)S(1)}, f32[1152]{0:T(1024)}, f32[512,1152]{1,0:T(8,128)S(1)}) fusion(f32[512,1152]{1,0:T(8,128)S(1)} %get-tuple-element.107, f32[512]{0:T(512)} %copy-done.74, f32[512]{0:T(512)S(1)} %copy-done.62, f32[1152]{0:T(1024)S(1)} %get-tuple-element.41, ...), kind=kOutput, calls=%fused_computation.82 | convolution fusion | flops 5082510336 | bytes 19224064 | tf_op jit(solution)/shard_map/tf,df->td/dot_general | solution.py:37
  298.4 4.5 fusion.36
  304.7 3.3 convolution_convert_fusion.4.rest_1_.refs_0_
  308.0 18.7 %attend_back.2 = (bf16[16,72,512]{2,1,0:T(8,128)(2,1)}, bf16[2,16,72,2048]{3,2,1,0:T(8,128)(2,1)}) custom-call(s32[1]{0:T(128)S(6)} %neg.49.refs_2_.count_ref, s32[8]{0:T(128)} %select_reduce_fusion.refs_3_.index_ref, bf16[16,80,512]{2,1,0:T(8,128)(2,1)} %maximum_maximum_fusion.q_ref, bf16[16,80,2048]{2,1,0:T(8,128)(2,1)} %after.31.refs_1_.k_ref, ...), custom_call_target="tpu_custom_call" | custom-call | flops 13421772800 | bytes 26214400 | tf_op jit(solution)/shard_map/attend_back/pallas_call | solution.py:279
  326.7 13.2 %reduce-scatter.5.cloned.1.call-done.refs_0_ = bf16[144,4304]{1,0:T(8,128)(2,1)} async-done(((bf16[1152,4304]{1,0:T(8,128)(2,1)}), bf16[144,4304]{1,0:T(8,128)(2,1)}) %reduce-scatter.5.cloned.1.call-update) | async-done | bytes 1239568 | tf_op jit(solution)/shard_map/reduce_scatter | solution.py:528
  347.0 19.7 %attend_back.3 = (bf16[16,72,512]{2,1,0:T(8,128)(2,1)}, bf16[2,16,72,2048]{3,2,1,0:T(8,128)(2,1)}) custom-call(s32[1]{0:T(128)S(6)} %neg.49.refs_2_.count_ref, s32[8]{0:T(128)} %select_reduce_fusion.refs_3_.index_ref, bf16[16,80,512]{2,1,0:T(8,128)(2,1)} %maximum_maximum_fusion.q_ref, ...), custom_call_target="tpu_custom_call", output_to_operand_aliasing={{0}: (6, {}), {1}: (7, {})} | custom-call | flops 13421772800 | bytes 26214400 | tf_op jit(solution)/shard_map/attend_back/pallas_call | solution.py:279
  366.8 6.7 %broadcast_select_fusion = (bf16[512,1152]{1,0:T(8,128)(2,1)S(1)}, bf16[512,1152]{1,0:T(8,128)(2,1)S(1)}) fusion(pred[]{:T(512)S(6)} %ge.49, pred[]{:T(512)S(6)} %lt.90, bf16[1152,3456]{1,0:T(8,128)(2,1)} %all-gather.7.cloned.1.call-done, bf16[2304,2048]{1,0:T(8,128)(2,1)} %bitcast.140), kind=kOutput, calls=%fused_computation.103 | convolution fusion | flops 2719678464 | bytes 10027010 | tf_op jit(solution)/shard_map/ct,dc->td/dot_general | solution.py:37
  374.8 9.8 %collective-permute-start.13 = (bf16[512,1152]{1,0:T(8,128)(2,1)S(1)}, bf16[512,1152]{1,0:T(8,128)(2,1)}, u32[]{:S(2)}, u32[]{:S(2)}) collective-permute-start(bf16[512,1152]{1,0:T(8,128)(2,1)S(1)} %get-tuple-element.59.refs_1_), channel_id=1, source_target_pairs={{0,1},{1,2},{2,3},{4,5},{5,6},{6,7},{8,9},{9,10},{10,11},{12,13},{... | collective-permute-start | bytes 3538952 | tf_op jit(solution)/shard_map/ppermute | solution.py:620
  384.6 3.2 convolution_convert_fusion.3.refs_2_
  390.1 15.1 %convolution_convert_fusion.2.refs_1_ = bf16[1152,2304]{1,0:T(8,128)(2,1)} fusion(bf16[2048,1152]{1,0:T(8,128)(2,1)S(1)} %bitcast.145, bf16[2304,2048]{1,0:T(8,128)(2,1)} %after.41.refs_0_), kind=kOutput, calls=%fused_computation.7 | convolution fusion | flops 10874290176 | bytes 19464192 | tf_op jit(solution)/shard_map/td,ct->dc/dot_general | solution.py:37
  410.6 6.2 %pad_maximum_fusion.refs_1_ = bf16[1152,4608]{1,0:T(8,128)(2,1)} fusion(bf16[1152,1152]{1,0:T(8,128)(2,1)} %after.42, bf16[1152,2304]{1,0:T(8,128)(2,1)S(1)} %copy-done.1, bf16[1152,1152]{1,0:T(8,128)(2,1)S(1)} %copy-done.6), kind=kLoop, calls=%fused_computation.8 | loop fusion | flops 31850496 | bytes 21233664 | tf_op jit(solution)/shard_map/concatenate | solution.py:631
  420.8 7.9 %add_convert_fusion.2.refs_1_ = bf16[512,1152]{1,0:T(8,128)(2,1)} fusion(bf16[512,1152]{1,0:T(8,128)(2,1)} %collective-permute-done.13.refs_3_, bf16[1152,3456]{1,0:T(8,128)(2,1)} %all-gather.7.cloned.1.call-done, bf16[2304,2048]{1,0:T(8,128)(2,1)} %after.44.refs_0_, pred[]{:T(512)S(6)} %lt.81), kind=kOutput, calls=%fused_computation.87 | convolution fusion | flops 2721447936 | bytes 10027009 | tf_op jit(solution)/shard_map/ct,dc->td/dot_general | solution.py:37
  430.0 5.5 collective-permute-start.18
  435.5 9.6 %fusion.16 = f32[512,1152]{1,0:T(8,128)} fusion(bf16[1152,3456]{1,0:T(8,128)(2,1)} %all-gather.7.cloned.1.call-done, bf16[2304,2048]{1,0:T(8,128)(2,1)} %after.45.refs_0_), kind=kOutput, calls=%fused_computation.35 | convolution fusion | flops 2717908992 | bytes 10027008 | tf_op jit(solution)/shard_map/ct,dc->td/dot_general | solution.py:37
  451.6 5.2 convolution_add_fusion.refs_1_
  456.7 11.2 %collective-permute-done.17.refs_0_ = bf16[144,1076]{1,0:T(8,128)(2,1)S(1)} collective-permute-done((bf16[144,1076]{1,0:T(8,128)(2,1)S(1)}, bf16[144,1076]{1,0:T(8,128)(2,1)S(1)}, u32[]{:S(2)}, u32[]{:S(2)}) %collective-permute-start.17) | collective-permute-done | bytes 309920 | tf_op jit(solution)/shard_map/ppermute | solution.py:635
  468.7 6.4 %collective-permute-done.16.refs_0_ = bf16[144,1076]{1,0:T(8,128)(2,1)S(1)} collective-permute-done((bf16[144,1076]{1,0:T(8,128)(2,1)S(1)}, bf16[144,1076]{1,0:T(8,128)(2,1)S(1)}, u32[]{:S(2)}, u32[]{:S(2)}) %collective-permute-start.16) | collective-permute-done | bytes 309920 | tf_op jit(solution)/shard_map/ppermute | solution.py:635
  475.9 3.6 collective-permute-done.15.refs_0_
  481.5 8.0 %add_convert_fusion.1 = (bf16[512,1152]{1,0:T(8,128)(2,1)}, bf16[512,1152]{1,0:T(8,128)(2,1)}) fusion(bf16[512,1152]{1,0:T(8,128)(2,1)S(1)} %copy-done.41, bf16[1152,3456]{1,0:T(8,128)(2,1)} %all-gather.7.cloned.1.call-done, bf16[2304,2048]{1,0:T(8,128)(2,1)} %after.51, pred[]{:T(512)S(6)} %ge.50), kind=kOutput, calls=%fused_computation.86 | convolution fusion | flops 2721447936 | bytes 11206657 | tf_op jit(solution)/shard_map/ct,dc->td/dot_general | solution.py:37
  498.6 25.4 %collective-permute-done.19 = bf16[512,1152]{1,0:T(8,128)(2,1)} collective-permute-done((bf16[512,1152]{1,0:T(8,128)(2,1)}, bf16[512,1152]{1,0:T(8,128)(2,1)}, u32[]{:S(2)}, u32[]{:S(2)}) %collective-permute-start.19) | collective-permute-done | bytes 1179680 | tf_op jit(solution)/shard_map/ppermute | solution.py:656
  524.1 4.7 fusion.60
  546.5 3.9 fusion.59
  552.1 11.6 %fusion.51 = bf16[1,512,1152]{2,1,0:T(8,128)(2,1)} fusion(f32[512,1152]{1,0:T(8,128)S(1)} %copy-done.11, bf16[512,4304]{1,0:T(8,128)(2,1)} %after.53, bf16[1152,4304]{1,0:T(8,128)(2,1)} %all-gather.11.cloned.1.call-done, f32[1152]{0:T(1024)S(1)} %copy-done.69, f32[512]{0:T(512)S(1)} %copy-done.65), kind=kOutput, calls=%fused_computation.63 | convolution fusion | flops 5079564288 | bytes 17869312 | tf_op jit(solution)/shard_map/tf,df->td/dot_general | solution.py:37
  566.4 5.9 %reduce-scatter.11.cloned.1.call-done = bf16[144,1152]{1,0:T(8,128)(2,1)} async-done(((bf16[576,1152]{1,0:T(8,128)(2,1)}), bf16[144,1152]{1,0:T(8,128)(2,1)}) %reduce-scatter.11.cloned.1.call-update) | async-done | bytes 331792 | tf_op jit(solution)/shard_map/reduce_scatter | solution.py:697
  (406 shorter events, 151.6 us)
Async XLA Ops:
  7.2 44.1 %copy-start.17 = (bf16[1,512,1152]{2,1,0:T(8,128)(2,1)S(1)}, bf16[1,512,1152]{2,1,0:T(8,128)(2,1)}, u32[]{:S(2)}) copy-start(bf16[1,512,1152]{2,1,0:T(8,128)(2,1)} %param.22) | copy-start | bytes 3538948
  7.2 52.8 %all-gather.13.cloned.1.call-start = ((), (), s32[]{:S(2)}) async-start(), calls=%async_computation.11 | async-start | bytes 1361920 | tf_op jit(solution)/shard_map/all_gather | solution.py:355
  7.2 46.7 %collective-permute-start.1 = (bf16[512,1152]{1,0:T(8,128)(2,1)}, bf16[512,1152]{1,0:T(8,128)(2,1)S(1)}, u32[]{:S(2)}, u32[]{:S(2)}) collective-permute-start(bf16[512,1152]{1,0:T(8,128)(2,1)} %bitcast.148), channel_id=1, source_target_pairs={{0,1},{1,2},{2,3},{4,5},{5,6},{6,7},{8,9},{9,10},{10,11},{12,13},{... | collective-permute-start | bytes 3538952 | tf_op jit(solution)/shard_map/ppermute | solution.py:413
  12.4 46.8 %collective-permute-start = (bf16[512,1152]{1,0:T(8,128)(2,1)}, bf16[512,1152]{1,0:T(8,128)(2,1)S(1)}, u32[]{:S(2)}, u32[]{:S(2)}) collective-permute-start(bf16[512,1152]{1,0:T(8,128)(2,1)} %bitcast.149), channel_id=1, source_target_pairs={{1,0},{2,1},{3,2},{5,4},{6,5},{7,6},{9,8},{10,9},{11,10},{13,12},{... | collective-permute-start | bytes 3538952 | tf_op jit(solution)/shard_map/ppermute | solution.py:412
  18.6 140.7 %all-gather.7.cloned.1.call-start = ((), (), s32[]{:S(2)}) async-start(), calls=%async_computation.4 | async-start | bytes 8957952 | tf_op jit(solution)/shard_map/all_gather | solution.py:473
  30.6 29.6 %copy-start.49 = (f32[3,512]{1,0:T(4,128)}, f32[3,512]{1,0:T(4,128)S(1)}, u32[]{:S(2)}) copy-start(f32[3,512]{1,0:T(4,128)S(1)} %get-tuple-element.104) | copy-start | bytes 18436
  64.1 153.2 %all-gather.9.cloned.1.call-start = ((), (), s32[]{:S(2)}) async-start(), calls=%async_computation.5 | async-start | bytes 14266368 | tf_op jit(solution)/shard_map/all_gather | solution.py:478
  64.2 46.6 %copy-start.78 = (pred[4]{0:T(512)(128)(4,1)}, pred[4]{0:T(512)(128)(4,1)S(1)}, u32[]{:S(2)}) copy-start(pred[4]{0:T(512)(128)(4,1)S(1)} %compare_and_fusion) | copy-start | bytes 16
  64.2 18.2 %copy-start.77 = (s32[1024]{0:T(1024)}, s32[1024]{0:T(1024)S(1)}, u32[]{:S(2)}) copy-start(s32[1024]{0:T(1024)S(1)} %pad_clamp_fusion.1) | copy-start | bytes 12292
  71.0 11.4 %collective-permute-start.4 = (bf16[144,1364]{1,0:T(8,128)(2,1)}, bf16[144,1364]{1,0:T(8,128)(2,1)S(1)}, u32[]{:S(2)}, u32[]{:S(2)}) collective-permute-start(bf16[144,1364]{1,0:T(8,128)(2,1)} %copy_after.2), channel_id=1, source_target_pairs={{0,3},{1,0},{2,1},{3,2},{4,7},{5,4},{6,5},{7,6},{8,11},{9,8},{10,9... | collective-permute-start | bytes 1178504 | tf_op jit(solution)/shard_map/ppermute | solution.py:80
  73.2 36.3 %collective-permute-start.3 = (bf16[144,1364]{1,0:T(8,128)(2,1)}, bf16[144,1364]{1,0:T(8,128)(2,1)S(1)}, u32[]{:S(2)}, u32[]{:S(2)}) collective-permute-start(bf16[144,1364]{1,0:T(8,128)(2,1)} %copy_after.2), channel_id=1, source_target_pairs={{0,2},{1,3},{2,0},{3,1},{4,6},{5,7},{6,4},{7,5},{8,10},{9,11},{10,... | collective-permute-start | bytes 1178504 | tf_op jit(solution)/shard_map/ppermute | solution.py:80
  75.2 34.3 %collective-permute-start.2 = (bf16[144,1364]{1,0:T(8,128)(2,1)}, bf16[144,1364]{1,0:T(8,128)(2,1)S(1)}, u32[]{:S(2)}, u32[]{:S(2)}) collective-permute-start(bf16[144,1364]{1,0:T(8,128)(2,1)} %copy_after.2), channel_id=1, source_target_pairs={{0,1},{1,2},{2,3},{3,0},{4,5},{5,6},{6,7},{7,4},{8,9},{9,10},{10,1... | collective-permute-start | bytes 1178504 | tf_op jit(solution)/shard_map/ppermute | solution.py:80
  82.4 28.6 %copy-start.22 = (bf16[144,1364]{1,0:T(8,128)(2,1)}, bf16[144,1364]{1,0:T(8,128)(2,1)S(1)}, u32[]{:S(2)}) copy-start(bf16[144,1364]{1,0:T(8,128)(2,1)S(1)} %collective-permute-done.4.refs_3_) | copy-start | bytes 1178500
  114.2 140.6 %all-gather.11.cloned.1.call-start = ((), (), s32[]{:S(2)}) async-start(), calls=%async_computation.6 | async-start | bytes 11280384 | tf_op jit(solution)/shard_map/all_gather | solution.py:502
  114.3 29.2 %collective-permute-start.5 = (bf16[512,1152]{1,0:T(8,128)(2,1)}, bf16[512,1152]{1,0:T(8,128)(2,1)S(1)}, u32[]{:S(2)}, u32[]{:S(2)}) collective-permute-start(bf16[512,1152]{1,0:T(8,128)(2,1)} %after.29.x_ref), channel_id=1, source_target_pairs={{1,0},{2,1},{3,2},{5,4},{6,5},{7,6},{9,8},{10,9},{11,10},{13,12},{... | collective-permute-start | bytes 3538952 | tf_op jit(solution)/shard_map/ppermute | solution.py:444
  115.6 29.2 %collective-permute-start.6 = (bf16[512,1152]{1,0:T(8,128)(2,1)}, bf16[512,1152]{1,0:T(8,128)(2,1)S(1)}, u32[]{:S(2)}, u32[]{:S(2)}) collective-permute-start(bf16[512,1152]{1,0:T(8,128)(2,1)} %after.30.x_ref), channel_id=1, source_target_pairs={{0,1},{1,2},{2,3},{4,5},{5,6},{6,7},{8,9},{9,10},{10,11},{12,13},{... | collective-permute-start | bytes 3538952 | tf_op jit(solution)/shard_map/ppermute | solution.py:445
  147.6 36.7 %collective-permute-start.9 = (bf16[144,1076]{1,0:T(8,128)(2,1)}, bf16[144,1076]{1,0:T(8,128)(2,1)S(1)}, u32[]{:S(2)}, u32[]{:S(2)}) collective-permute-start(bf16[144,1076]{1,0:T(8,128)(2,1)} %copy_after.3), channel_id=1, source_target_pairs={{0,3},{1,0},{2,1},{3,2},{4,7},{5,4},{6,5},{7,6},{8,11},{9,8},{10,9... | collective-permute-start | bytes 929672 | tf_op jit(solution)/shard_map/ppermute | solution.py:80
  151.3 33.8 %collective-permute-start.8 = (bf16[144,1076]{1,0:T(8,128)(2,1)}, bf16[144,1076]{1,0:T(8,128)(2,1)S(1)}, u32[]{:S(2)}, u32[]{:S(2)}) collective-permute-start(bf16[144,1076]{1,0:T(8,128)(2,1)} %copy_after.3), channel_id=1, source_target_pairs={{0,2},{1,3},{2,0},{3,1},{4,6},{5,7},{6,4},{7,5},{8,10},{9,11},{10,... | collective-permute-start | bytes 929672 | tf_op jit(solution)/shard_map/ppermute | solution.py:80
  151.4 34.4 %collective-permute-start.7 = (bf16[144,1076]{1,0:T(8,128)(2,1)}, bf16[144,1076]{1,0:T(8,128)(2,1)S(1)}, u32[]{:S(2)}, u32[]{:S(2)}) collective-permute-start(bf16[144,1076]{1,0:T(8,128)(2,1)} %copy_after.3), channel_id=1, source_target_pairs={{0,1},{1,2},{2,3},{3,0},{4,5},{5,6},{6,7},{7,4},{8,9},{9,10},{10,1... | collective-permute-start | bytes 929672 | tf_op jit(solution)/shard_map/ppermute | solution.py:80
  190.3 149.6 %reduce-scatter.5.cloned.1.call-start = ((), (), s32[]{:S(2)}) async-start(), calls=%async_computation.7 | async-start | bytes 11280384 | tf_op jit(solution)/shard_map/reduce_scatter | solution.py:528
  196.1 21.2 %copy-start.4 = (bf16[1,512,1152]{2,1,0:T(8,128)(2,1)S(1)}, bf16[1,512,1152]{2,1,0:T(8,128)(2,1)}, u32[]{:S(2)}) copy-start(bf16[1,512,1152]{2,1,0:T(8,128)(2,1)} %param.20) | copy-start | bytes 3538948
  221.6 74.7 %copy-start.10 = (f32[512,1152]{1,0:T(8,128)}, f32[512,1152]{1,0:T(8,128)S(1)}, u32[]{:S(2)}) copy-start(f32[512,1152]{1,0:T(8,128)S(1)} %get-tuple-element.107) | copy-start | bytes 7077892
  221.6 47.1 %copy-start.61 = (f32[512]{0:T(512)}, f32[512]{0:T(512)S(1)}, u32[]{:S(2)}) copy-start(f32[512]{0:T(512)S(1)} %broadcast_multiply_fusion.5) | copy-start | bytes 6148
  243.4 201.7 %reduce-scatter.9.cloned.1.call-start = ((), (), s32[]{:S(2)}) async-start(), calls=%async_computation.9 | async-start | bytes 11280384 | tf_op jit(solution)/shard_map/reduce_scatter | solution.py:541
  280.0 249.5 %reduce-scatter.7.cloned.1.call-start = ((), (), s32[]{:S(2)}) async-start(), calls=%async_computation.8 | async-start | bytes 11943936 | tf_op jit(solution)/shard_map/reduce_scatter | solution.py:632
  339.9 44.7 %slice-start.2 = ((s8[4718592]{0:T(1024)(128)(4,1)}), s8[4194304]{0:T(1024)(128)(4,1)S(1)}, s32[]{:S(2)}) async-start(s8[4718592]{0:T(1024)(128)(4,1)} %bitcast.144), calls=%async_computation.14 | async-start | bytes 8388608
  341.7 46.2 %collective-permute-start.12 = (bf16[144,1076]{1,0:T(8,128)(2,1)S(1)}, bf16[144,1076]{1,0:T(8,128)(2,1)S(1)}, u32[]{:S(2)}, u32[]{:S(2)}) collective-permute-start(bf16[144,1076]{1,0:T(8,128)(2,1)S(1)} %get-tuple-element.55), channel_id=1, source_target_pairs={{0,1},{1,2},{2,3},{3,0},{4,5},{5,6},{6,7},{7,4},{8,9},{9,10},{10,1... | collective-permute-start | bytes 929672 | tf_op jit(solution)/shard_map/ppermute | solution.py:585
  343.2 45.4 %collective-permute-start.11 = (bf16[144,1076]{1,0:T(8,128)(2,1)S(1)}, bf16[144,1076]{1,0:T(8,128)(2,1)S(1)}, u32[]{:S(2)}, u32[]{:S(2)}) collective-permute-start(bf16[144,1076]{1,0:T(8,128)(2,1)S(1)} %get-tuple-element.56), channel_id=1, source_target_pairs={{0,2},{1,3},{2,0},{3,1},{4,6},{5,7},{6,4},{7,5},{8,10},{9,11},{10,... | collective-permute-start | bytes 929672 | tf_op jit(solution)/shard_map/ppermute | solution.py:585
  345.6 43.7 %collective-permute-start.10 = (bf16[144,1076]{1,0:T(8,128)(2,1)S(1)}, bf16[144,1076]{1,0:T(8,128)(2,1)S(1)}, u32[]{:S(2)}, u32[]{:S(2)}) collective-permute-start(bf16[144,1076]{1,0:T(8,128)(2,1)S(1)} %get-tuple-element.57), channel_id=1, source_target_pairs={{0,3},{1,0},{2,1},{3,2},{4,7},{5,4},{6,5},{7,6},{8,11},{9,8},{10,9... | collective-permute-start | bytes 929672 | tf_op jit(solution)/shard_map/ppermute | solution.py:585
  347.0 37.6 %slice-start.3 = ((s8[4718592]{0:T(1024)(128)(4,1)}), s8[524288]{0:T(1024)(128)(4,1)S(1)}, s32[]{:S(2)}) async-start(s8[4718592]{0:T(1024)(128)(4,1)} %bitcast.144), calls=%async_computation.15 | async-start | bytes 1048576
  366.8 17.8 %copy-start.2 = (bf16[16,72,512]{2,1,0:T(8,128)(2,1)S(1)}, bf16[16,72,512]{2,1,0:T(8,128)(2,1)}, u32[]{:S(2)}) copy-start(bf16[16,72,512]{2,1,0:T(8,128)(2,1)} %get-tuple-element.28.refs_1_) | copy-start | bytes 3538948
  373.5 33.4 %collective-permute-start.14 = (bf16[512,1152]{1,0:T(8,128)(2,1)S(1)}, bf16[512,1152]{1,0:T(8,128)(2,1)S(1)}, u32[]{:S(2)}, u32[]{:S(2)}) collective-permute-start(bf16[512,1152]{1,0:T(8,128)(2,1)S(1)} %get-tuple-element.58.refs_2_), channel_id=1, source_target_pairs={{1,0},{2,1},{3,2},{5,4},{6,5},{7,6},{9,8},{10,9},{11,10},{13,12},{... | collective-permute-start | bytes 3538952 | tf_op jit(solution)/shard_map/ppermute | solution.py:621
  374.8 33.3 %collective-permute-start.13 = (bf16[512,1152]{1,0:T(8,128)(2,1)S(1)}, bf16[512,1152]{1,0:T(8,128)(2,1)}, u32[]{:S(2)}, u32[]{:S(2)}) collective-permute-start(bf16[512,1152]{1,0:T(8,128)(2,1)S(1)} %get-tuple-element.59.refs_1_), channel_id=1, source_target_pairs={{0,1},{1,2},{2,3},{4,5},{5,6},{6,7},{8,9},{9,10},{10,11},{12,13},{... | collective-permute-start | bytes 3538952 | tf_op jit(solution)/shard_map/ppermute | solution.py:620
  416.9 155.4 %reduce-scatter.11.cloned.1.call-start = ((), (), s32[]{:S(2)}) async-start(), calls=%async_computation.10 | async-start | bytes 1658880 | tf_op jit(solution)/shard_map/reduce_scatter | solution.py:697
  430.0 65.4 %collective-permute-start.18 = (bf16[512,1152]{1,0:T(8,128)(2,1)S(1)}, bf16[512,1152]{1,0:T(8,128)(2,1)}, u32[]{:S(2)}, u32[]{:S(2)}) collective-permute-start(bf16[512,1152]{1,0:T(8,128)(2,1)S(1)} %copy-done.14), channel_id=1, source_target_pairs={{0,1},{1,2},{2,3},{4,5},{5,6},{6,7},{8,9},{9,10},{10,11},{12,13},{... | collective-permute-start | bytes 3538952 | tf_op jit(solution)/shard_map/ppermute | solution.py:649
  446.9 21.0 %collective-permute-start.17 = (bf16[144,1076]{1,0:T(8,128)(2,1)S(1)}, bf16[144,1076]{1,0:T(8,128)(2,1)S(1)}, u32[]{:S(2)}, u32[]{:S(2)}) collective-permute-start(bf16[144,1076]{1,0:T(8,128)(2,1)S(1)} %get-tuple-element.52), channel_id=1, source_target_pairs={{0,1},{1,2},{2,3},{3,0},{4,5},{5,6},{6,7},{7,4},{8,9},{9,10},{10,1... | collective-permute-start | bytes 929672 | tf_op jit(solution)/shard_map/ppermute | solution.py:635
  447.8 27.4 %collective-permute-start.16 = (bf16[144,1076]{1,0:T(8,128)(2,1)S(1)}, bf16[144,1076]{1,0:T(8,128)(2,1)S(1)}, u32[]{:S(2)}, u32[]{:S(2)}) collective-permute-start(bf16[144,1076]{1,0:T(8,128)(2,1)S(1)} %get-tuple-element.53), channel_id=1, source_target_pairs={{0,2},{1,3},{2,0},{3,1},{4,6},{5,7},{6,4},{7,5},{8,10},{9,11},{10,... | collective-permute-start | bytes 929672 | tf_op jit(solution)/shard_map/ppermute | solution.py:635
  448.5 31.0 %collective-permute-start.15 = (bf16[144,1076]{1,0:T(8,128)(2,1)S(1)}, bf16[144,1076]{1,0:T(8,128)(2,1)S(1)}, u32[]{:S(2)}, u32[]{:S(2)}) collective-permute-start(bf16[144,1076]{1,0:T(8,128)(2,1)S(1)} %get-tuple-element.54), channel_id=1, source_target_pairs={{0,3},{1,0},{2,1},{3,2},{4,7},{5,4},{6,5},{7,6},{8,11},{9,8},{10,9... | collective-permute-start | bytes 929672 | tf_op jit(solution)/shard_map/ppermute | solution.py:635
  489.5 34.5 %collective-permute-start.19 = (bf16[512,1152]{1,0:T(8,128)(2,1)}, bf16[512,1152]{1,0:T(8,128)(2,1)}, u32[]{:S(2)}, u32[]{:S(2)}) collective-permute-start(bf16[512,1152]{1,0:T(8,128)(2,1)} %get-tuple-element.111), channel_id=1, source_target_pairs={{1,0},{2,1},{3,2},{5,4},{6,5},{7,6},{9,8},{10,9},{11,10},{13,12},{... | collective-permute-start | bytes 3538952 | tf_op jit(solution)/shard_map/ppermute | solution.py:656
  495.4 28.6 %copy-start = (f32[512,1152]{1,0:T(8,128)S(1)}, f32[512,1152]{1,0:T(8,128)}, u32[]{:S(2)}) copy-start(f32[512,1152]{1,0:T(8,128)} %convolution_add_fusion.refs_1_) | copy-start | bytes 7077892
  495.4 28.6 %copy-start.52 = (f32[1152]{0:T(1024)S(1)}, f32[1152]{0:T(1024)}, u32[]{:S(2)}) copy-start(f32[1152]{0:T(1024)} %get-tuple-element.38) | copy-start | bytes 13828
  495.4 28.6 %copy-start.58 = (f32[512]{0:T(512)S(1)}, f32[512]{0:T(512)}, u32[]{:S(2)}) copy-start(f32[512]{0:T(512)} %copy-done.57) | copy-start | bytes 6148
  495.5 28.6 %copy-start.66 = (f32[512]{0:T(512)S(1)}, f32[512]{0:T(512)}, u32[]{:S(2)}) copy-start(f32[512]{0:T(512)} %add_rsqrt_fusion) | copy-start | bytes 6148
  532.3 5.1 collective-permute-start.20
  538.9 5.4 collective-permute-start.21
  545.1 1.3 collective-permute-start.22
  546.4 4.2 collective-permute-start.23
  550.7 13.1 %collective-permute-start.24 = (f32[13520]{0:T(1024)S(1)}, f32[13520]{0:T(1024)S(1)}, u32[]{:S(2)}, u32[]{:S(2)}) collective-permute-start(f32[13520]{0:T(1024)S(1)} %add.323), channel_id=1, source_target_pairs={{0,16},{4,20},{8,24},{12,28},{16,0},{20,4},{24,8},{28,12},{1,17},{... | collective-permute-start | bytes 162248 | tf_op jit(solution)/shard_map/ppermute | solution.py:685
  (76 other events, 359.9 us)
Sparse Core Ops, SparseCore 0:
  18.7 41.3 all-gather.12
  64.2 52.4 all-gather.6
  119.2 72.5 all-gather.8
  193.5 61.3 all-gather.10
  258.3 81.5 reduce-scatter.4
  343.8 79.1 reduce-scatter.8
  426.5 82.1 reduce-scatter.6
  542.4 29.8 reduce-scatter.10

commit v4 on v3

--- a/solution.py
+++ b/solution.py
@@ -645,16 +645,16 @@
     if reach > 1:
         send_shares(1, dkv, "later")
         moving_right = joined(moving_right, to_later[1])
-        dkv, dq = after(dkv, moving_right), after(dq, moving_right)
+        dkv = after(dkv, moving_right, *up_moved[:1])
+        dq = after(dq, moving_right, *up_moved[1:2])
         moving_right = lax.ppermute(moving_right, "tp", to_right)
     own_share = share_of(0, dkv) + product("ct,dc->td", dq, query_full)
-    up_moved = [after(moved, own_share) for moved in up_moved]
     if reach > 1:
-        dkv = after(dkv, *up_moved)
+        dkv = after(dkv, own_share)
         send_shares(1, dkv, "prior")
         moving_right = after(moving_right, to_prior[1])
         moving_left = lax.ppermute(joined(moving_left, to_prior[1]), "tp", to_left)
-    last_sent = [t for t in (own_share, to_prior[1]) if t is not None]
+    last_sent = [t for t in (own_share, to_prior[1], *up_moved) if t is not None]
     grad_normed = own_share + moving_right.astype(F32) + moving_left.astype(F32)
 
     one_hat, one_rstd = xhat_of(x)

time: 588 us -> 569 us (0.968)
  waiting for transfers between devices: 133 us -> 114 us
    ppermute x3, waiting for transfers between devices: 21.3 us -> 8.52 us  [local(): lax.ppermute(up_scattered[:, s * units:(s + 1) * units], 'tp', [(i, (i -...]
    ppermute x1, waiting for transfers between devices: 25.4 us -> 18.1 us  [local(): moving_left = lax.ppermute(joined(moving_left, to_prior[1]), 'tp', to_left)]
    ppermute x3, starting transfers between devices: 4.63 us -> 10.8 us  [local(): lax.ppermute(up_scattered[:, s * units:(s + 1) * units], 'tp', [(i, (i -...]
    unnamed x183 -> x179, local copies, waits for them, and re-layouts: 24.9 us -> 25 us
  transfers between devices with their start and end apart: 33 -> 33, of which waited for: 19 -> 18; matrix products, arithmetic and copies ran while one was open for 44% -> 45% of each run, Pallas kernels for 14% -> 14%
where the time goes in v4:
time: 569 us; the launch traced here: 562 us
  matrix products  150 us (26%)
  waiting for transfers between devices  114 us (20%)
  Pallas kernels  82.2 us (14%)
  other arithmetic  66.8 us (12%)
  local copies, waits for them, and re-layouts  64.5 us (11%)
  starting transfers between devices  57.2 us (10%)
  between operations  16.8 us (3%)
  blocking collectives  9.36 us (2%)
    dot_general x19, matrix products, product(): return jnp.einsum(form, left, right, preferred_element_type=F32)  150 us
    pallas_call x2, Pallas kernels, attend_back(): pl.pallas_call(functools.partial(attend_back_kernel, q_block=q_block, k_b...  38.6 us
    ppermute x6, waiting for transfers between devices, slots_along_tp(): lax.ppermute(piece, 'tp', [(i, (i + distance) % count) for i in range(cou...  32.1 us
    unnamed x179, local copies, waits for them, and re-layouts  25 us
    pallas_call x1, Pallas kernels, attend(): pl.pallas_call(functools.partial(attend_kernel, q_block=q_block, k_block=...  21.2 us
    ppermute x1, waiting for transfers between devices, local(): moving_left = lax.ppermute(joined(moving_left, to_prior[1]), 'tp', to_left)  18.1 us
    pallas_call x4, Pallas kernels, norm_slot(): pl.pallas_call(norm_kernel, grid=(steps,), in_specs=[pl.BlockSpec((block,...  16 us
    all_gather x1, waiting for transfers between devices, local(): down_full = lax.all_gather(down_shard, 'fsdp', axis=0, tiled=True)  11.4 us
  transfers between devices with their start and end apart: 33, of which 18 were waited for; matrix products, arithmetic and copies ran while one was open for 45% of the time, Pallas kernels for 14%

profile of v4, /device:TPU:0, one launch (start us, length us, event | category | flops | bytes accessed | tf_op | source)
XLA Modules:
  0.0 561.6 jit_solution(8734984666657309703)
XLA Ops:
  7.2 5.1 collective-permute-start.1
  37.7 9.4 %all-gather.1 = f32[8,144,6]{1,2,0:T(8,128)S(1)} all-gather(f32[1,144,6]{1,2,0:T(8,128)} %bitcast.172), channel_id=1, replica_groups=mesh['fsdp'=8,'tp'=4] {'fsdp'}, dimensions={0}, use_global_device_ids=true | all-gather | bytes 31104 | tf_op jit(solution)/shard_map/all_gather | solution.py:357
  54.0 5.2 collective-permute-done.refs_8_.refs_0_
  77.4 5.0 collective-permute-done.4.refs_3_
  82.4 27.1 %collective-permute-done.3.refs_2_ = bf16[144,1364]{1,0:T(8,128)(2,1)S(1)} collective-permute-done((bf16[144,1364]{1,0:T(8,128)(2,1)}, bf16[144,1364]{1,0:T(8,128)(2,1)S(1)}, u32[]{:S(2)}, u32[]{:S(2)}) %collective-permute-start.3) | collective-permute-done | bytes 392864 | tf_op jit(solution)/shard_map/ppermute | solution.py:80
  115.6 4.6 collective-permute-start.6
  121.5 3.9 norm_slot.4.rest_0_
  125.4 4.0 norm_slot.5.rest_0_
  129.5 4.0 norm_slot.6.rest_0_
  133.4 10.1 %collective-permute-done.5.refs_0_ = bf16[512,1152]{1,0:T(8,128)(2,1)S(1)} collective-permute-done((bf16[512,1152]{1,0:T(8,128)(2,1)}, bf16[512,1152]{1,0:T(8,128)(2,1)S(1)}, u32[]{:S(2)}, u32[]{:S(2)}) %collective-permute-start.5) | collective-permute-done | bytes 1179680 | tf_op jit(solution)/shard_map/ppermute | solution.py:444
  147.6 3.7 collective-permute-start.9
  154.8 4.1 norm_slot.7
  158.9 9.1 %add_convert_fusion = bf16[1152,2048]{1,0:T(8,128)(2,1)S(1)} fusion(bf16[2048,1152]{1,0:T(8,128)(2,1)} %norm_slot.7, f32[1152]{0:T(1024)S(1)} %copy-done.53, bf16[1152,3456]{1,0:T(8,128)(2,1)} %all-gather.7.cloned.1.call-done), kind=kOutput, calls=%fused_computation.10 | convolution fusion | flops 5440536576 | bytes 12096000 | tf_op jit(solution)/shard_map/td,dc->ct/dot_general | solution.py:37
  172.5 8.5 %convolution_convert_fusion.5 = bf16[1152,2048]{1,0:T(8,128)(2,1)S(1)} fusion(bf16[2048,1152]{1,0:T(8,128)(2,1)S(1)} %bitcast.143, bf16[1152,3456]{1,0:T(8,128)(2,1)} %all-gather.7.cloned.1.call-done), kind=kOutput, calls=%fused_computation.27 | convolution fusion | flops 5438177280 | bytes 12091392 | tf_op jit(solution)/shard_map/td,dc->ct/dot_general | solution.py:37
  186.5 3.2 concatenate.144.rest_0_
  190.6 3.8 fusion.29
  195.9 21.2 %attend.1 = (bf16[16,72,512]{2,1,0:T(8,128)(2,1)}, f32[16,1,512]{2,1,0:T(1,128)}) custom-call(s32[1]{0:T(128)S(6)} %neg.49.refs_2_.count_ref, s32[8]{0:T(128)} %select_reduce_fusion.refs_3_.index_ref, bf16[16,80,512]{2,1,0:T(8,128)(2,1)} %pad_maximum_fusion.3.q_ref, bf16[16,80,2048]{2,1,0:T(8,128)(2,1)} %after.28.refs_1_.k_ref, ...), custom_call_target="tpu_custom_call" | custom-call | flops 5368709120 | bytes 13107200 | tf_op jit(solution)/shard_map/attend/pallas_call | solution.py:188
  217.1 4.2 fusion.104
  223.7 9.1 %multiply_convert_fusion = (bf16[512,4304]{1,0:T(8,128)(2,1)S(1)}, f32[512,4304]{1,0:T(8,128)}) fusion(f32[4304]{0:T(1024)S(1)} %copy-done.45, bf16[1152,5456]{1,0:T(8,128)(2,1)S(1)} %copy-done.83, f32[512,1152]{1,0:T(8,128)S(1)} %get-tuple-element.107, f32[1152]{0:T(1024)S(1)} %copy-done.71, f32[1152]{0:T(1024)S(1)} %get-tuple-element.41, ...), kind=kOutput, calls=%fused_computation.19 | convolution fusion | flops 5102190592 | bytes 25649152 | tf_op jit(solution)/shard_map/td,df->tf/dot_general | solution.py:37
  234.9 8.3 %convolution_convert_fusion.1.refs_1_ = bf16[1152,4304]{1,0:T(8,128)(2,1)} fusion(bf16[512,1152]{1,0:T(8,128)(2,1)S(1)} %copy-done.9, bf16[512,4304]{1,0:T(8,128)(2,1)S(1)} %get-tuple-element.108.refs_0_), kind=kOutput, calls=%fused_computation.4 | convolution fusion | flops 5082163200 | bytes 15503360 | tf_op jit(solution)/shard_map/td,tf->df/dot_general | solution.py:37
  243.5 11.4 %all-gather.11.cloned.1.call-done = bf16[1152,4304]{1,0:T(8,128)(2,1)} async-done(((bf16[144,4304]{1,0:T(8,128)(2,1)}), bf16[1152,4304]{1,0:T(8,128)(2,1)}) %all-gather.11.cloned.1.call-update) | async-done | bytes 9916432 | tf_op jit(solution)/shard_map/all_gather | solution.py:502
  254.9 13.9 %convert_reduce_fusion.1 = (f32[4304]{0:T(1024)}, bf16[512,4304]{1,0:T(8,128)(2,1)S(1)}) fusion(f32[512,4304]{1,0:T(8,128)} %get-tuple-element.109, bf16[512,1152]{1,0:T(8,128)(2,1)} %after.33, bf16[1152,4304]{1,0:T(8,128)(2,1)} %all-gather.11.cloned.1.call-done), kind=kOutput, calls=%fused_computation.18 | convolution fusion | flops 5125681152 | bytes 24335168 | tf_op jit(solution)/shard_map/td,df->tf/dot_general | solution.py:37
  271.3 8.7 %convolution_convert_fusion.rest_0_ = bf16[1152,4304]{1,0:T(8,128)(2,1)} fusion(bf16[512,4304]{1,0:T(8,128)(2,1)S(1)} %get-tuple-element.46, f32[512,1152]{1,0:T(8,128)S(1)} %get-tuple-element.107, f32[1152]{0:T(1024)S(1)} %copy-done.72, f32[1152]{0:T(1024)S(1)} %get-tuple-element.41, f32[512]{0:T(512)S(1)} %copy-done.74, f32[512]{0:T(512)S(1)} %broadcast_multiply_fusion.5), kind=kOutput, calls=%fused_computation.3 | convolution fusion | flops 5085112320 | bytes 16696320 | tf_op jit(solution)/shard_map/td,tf->df/dot_general | solution.py:37
  283.2 13.0 %multiply_reduce_fusion = (f32[1152]{0:T(1024)}, f32[512]{0:T(512)S(1)}, f32[512]{0:T(512)S(1)}, f32[1152]{0:T(1024)}, f32[512,1152]{1,0:T(8,128)S(1)}) fusion(f32[512,1152]{1,0:T(8,128)S(1)} %get-tuple-element.107, f32[512]{0:T(512)} %copy-done.73, f32[512]{0:T(512)S(1)} %copy-done.61, f32[1152]{0:T(1024)S(1)} %get-tuple-element.41, ...), kind=kOutput, calls=%fused_computation.82 | convolution fusion | flops 5082510336 | bytes 19224064 | tf_op jit(solution)/shard_map/tf,df->td/dot_general | solution.py:37
  298.3 4.4 fusion.39
  304.5 3.3 convolution_convert_fusion.4.rest_1_.refs_0_
  307.8 18.7 %attend_back.2 = (bf16[16,72,512]{2,1,0:T(8,128)(2,1)}, bf16[2,16,72,2048]{3,2,1,0:T(8,128)(2,1)}) custom-call(s32[1]{0:T(128)S(6)} %neg.49.refs_2_.count_ref, s32[8]{0:T(128)} %select_reduce_fusion.refs_3_.index_ref, bf16[16,80,512]{2,1,0:T(8,128)(2,1)} %maximum_maximum_fusion.q_ref, bf16[16,80,2048]{2,1,0:T(8,128)(2,1)} %after.28.refs_1_.k_ref, ...), custom_call_target="tpu_custom_call" | custom-call | flops 13421772800 | bytes 26214400 | tf_op jit(solution)/shard_map/attend_back/pallas_call | solution.py:279
  326.5 11.2 %reduce-scatter.5.cloned.1.call-done.refs_0_ = bf16[144,4304]{1,0:T(8,128)(2,1)} async-done(((bf16[1152,4304]{1,0:T(8,128)(2,1)}), bf16[144,4304]{1,0:T(8,128)(2,1)}) %reduce-scatter.5.cloned.1.call-update) | async-done | bytes 1239568 | tf_op jit(solution)/shard_map/reduce_scatter | solution.py:528
  344.9 20.0 %attend_back.3 = (bf16[16,72,512]{2,1,0:T(8,128)(2,1)}, bf16[2,16,72,2048]{3,2,1,0:T(8,128)(2,1)}) custom-call(s32[1]{0:T(128)S(6)} %neg.49.refs_2_.count_ref, s32[8]{0:T(128)} %select_reduce_fusion.refs_3_.index_ref, bf16[16,80,512]{2,1,0:T(8,128)(2,1)} %maximum_maximum_fusion.q_ref, ...), custom_call_target="tpu_custom_call", output_to_operand_aliasing={{0}: (6, {}), {1}: (7, {})} | custom-call | flops 13421772800 | bytes 26214400 | tf_op jit(solution)/shard_map/attend_back/pallas_call | solution.py:279
  364.9 6.9 %broadcast_select_fusion = (bf16[512,1152]{1,0:T(8,128)(2,1)S(1)}, bf16[512,1152]{1,0:T(8,128)(2,1)S(1)}) fusion(pred[]{:T(512)S(6)} %ge.49, pred[]{:T(512)S(6)} %lt.90, bf16[1152,3456]{1,0:T(8,128)(2,1)} %all-gather.7.cloned.1.call-done, bf16[2304,2048]{1,0:T(8,128)(2,1)} %bitcast.140), kind=kOutput, calls=%fused_computation.104 | convolution fusion | flops 2719678464 | bytes 10027010 | tf_op jit(solution)/shard_map/ct,dc->td/dot_general | solution.py:37
  373.1 9.7 %collective-permute-start.13 = (bf16[512,1152]{1,0:T(8,128)(2,1)S(1)}, bf16[512,1152]{1,0:T(8,128)(2,1)}, u32[]{:S(2)}, u32[]{:S(2)}) collective-permute-start(bf16[512,1152]{1,0:T(8,128)(2,1)S(1)} %get-tuple-element.59.refs_1_), channel_id=1, source_target_pairs={{0,1},{1,2},{2,3},{4,5},{5,6},{6,7},{8,9},{9,10},{10,11},{12,13},{... | collective-permute-start | bytes 3538952 | tf_op jit(solution)/shard_map/ppermute | solution.py:620
  382.8 3.2 convolution_convert_fusion.3.refs_2_
  388.2 15.0 %convolution_convert_fusion.2.refs_1_ = bf16[1152,2304]{1,0:T(8,128)(2,1)} fusion(bf16[2048,1152]{1,0:T(8,128)(2,1)S(1)} %bitcast.145, bf16[2304,2048]{1,0:T(8,128)(2,1)} %after.38.refs_0_), kind=kOutput, calls=%fused_computation.7 | convolution fusion | flops 10874290176 | bytes 19464192 | tf_op jit(solution)/shard_map/td,ct->dc/dot_general | solution.py:37
  408.7 6.2 %pad_maximum_fusion.refs_1_ = bf16[1152,4608]{1,0:T(8,128)(2,1)} fusion(bf16[1152,1152]{1,0:T(8,128)(2,1)} %after.39, bf16[1152,2304]{1,0:T(8,128)(2,1)S(1)} %copy-done, bf16[1152,1152]{1,0:T(8,128)(2,1)S(1)} %copy-done.5), kind=kLoop, calls=%fused_computation.8 | loop fusion | flops 31850496 | bytes 21233664 | tf_op jit(solution)/shard_map/concatenate | solution.py:631
  427.0 7.6 %add_convert_fusion.2.refs_1_ = bf16[512,1152]{1,0:T(8,128)(2,1)S(1)} fusion(bf16[512,1152]{1,0:T(8,128)(2,1)} %collective-permute-done.13.refs_3_, bf16[1152,3456]{1,0:T(8,128)(2,1)} %all-gather.7.cloned.1.call-done, bf16[2304,2048]{1,0:T(8,128)(2,1)} %after.41.refs_0_, pred[]{:T(512)S(6)} %lt.81), kind=kOutput, calls=%fused_computation.87 | convolution fusion | flops 2721447936 | bytes 10027009 | tf_op jit(solution)/shard_map/ct,dc->td/dot_general | solution.py:37
  437.5 4.3 collective-permute-done.16.refs_2_.refs_4_
  444.0 3.6 fusion.73
  447.6 7.9 %fusion.22.refs_1_ = f32[512,1152]{1,0:T(8,128)} fusion(f32[512,1152]{1,0:T(8,128)S(1)} %fusion.73, bf16[1152,3456]{1,0:T(8,128)(2,1)} %all-gather.7.cloned.1.call-done, bf16[2304,2048]{1,0:T(8,128)(2,1)} %after.43.refs_0_), kind=kOutput, calls=%fused_computation.41 | convolution fusion | flops 2718498816 | bytes 12386304 | tf_op jit(solution)/shard_map/ct,dc->td/dot_general | solution.py:37
  456.8 8.3 %add_convert_fusion.1 = (bf16[512,1152]{1,0:T(8,128)(2,1)}, bf16[512,1152]{1,0:T(8,128)(2,1)}) fusion(bf16[512,1152]{1,0:T(8,128)(2,1)S(1)} %copy-done.40, bf16[1152,3456]{1,0:T(8,128)(2,1)} %all-gather.7.cloned.1.call-done, bf16[2304,2048]{1,0:T(8,128)(2,1)} %after.45, pred[]{:T(512)S(6)} %ge.50), kind=kOutput, calls=%fused_computation.86 | convolution fusion | flops 2721447936 | bytes 11206657 | tf_op jit(solution)/shard_map/ct,dc->td/dot_general | solution.py:37
  471.0 7.0 %collective-permute-start.17 = (bf16[144,1076]{1,0:T(8,128)(2,1)}, bf16[144,1076]{1,0:T(8,128)(2,1)}, u32[]{:S(2)}, u32[]{:S(2)}) collective-permute-start(bf16[144,1076]{1,0:T(8,128)(2,1)} %get-tuple-element.52), channel_id=1, source_target_pairs={{0,1},{1,2},{2,3},{3,0},{4,5},{5,6},{6,7},{7,4},{8,9},{9,10},{10,1... | collective-permute-start | bytes 929672 | tf_op jit(solution)/shard_map/ppermute | solution.py:635
  478.2 3.3 convert_reduce_fusion
  481.5 18.1 %collective-permute-done.19 = bf16[512,1152]{1,0:T(8,128)(2,1)} collective-permute-done((bf16[512,1152]{1,0:T(8,128)(2,1)}, bf16[512,1152]{1,0:T(8,128)(2,1)}, u32[]{:S(2)}, u32[]{:S(2)}) %collective-permute-start.19) | collective-permute-done | bytes 1179680 | tf_op jit(solution)/shard_map/ppermute | solution.py:656
  499.7 4.7 fusion.63
  505.1 4.3 collective-permute-done.17.refs_5_
  519.4 4.2 collective-permute-done.21
  528.9 3.9 fusion.62
  534.4 11.6 %fusion.54 = bf16[1,512,1152]{2,1,0:T(8,128)(2,1)} fusion(f32[512,1152]{1,0:T(8,128)S(1)} %copy-done.11, bf16[512,4304]{1,0:T(8,128)(2,1)} %after.47, bf16[1152,4304]{1,0:T(8,128)(2,1)} %all-gather.11.cloned.1.call-done, f32[1152]{0:T(1024)S(1)} %copy-done.68, f32[512]{0:T(512)S(1)} %copy-done.64), kind=kOutput, calls=%fused_computation.63 | convolution fusion | flops 5079564288 | bytes 17869312 | tf_op jit(solution)/shard_map/tf,df->td/dot_general | solution.py:37
  548.7 3.7 reduce-scatter.11.cloned.1.call-done
  (399 shorter events, 153.2 us)
Async XLA Ops:
  7.2 44.1 %copy-start.17 = (bf16[1,512,1152]{2,1,0:T(8,128)(2,1)S(1)}, bf16[1,512,1152]{2,1,0:T(8,128)(2,1)}, u32[]{:S(2)}) copy-start(bf16[1,512,1152]{2,1,0:T(8,128)(2,1)} %param.22) | copy-start | bytes 3538948
  7.2 52.8 %all-gather.13.cloned.1.call-start = ((), (), s32[]{:S(2)}) async-start(), calls=%async_computation.11 | async-start | bytes 1361920 | tf_op jit(solution)/shard_map/all_gather | solution.py:355
  7.2 46.7 %collective-permute-start.1 = (bf16[512,1152]{1,0:T(8,128)(2,1)}, bf16[512,1152]{1,0:T(8,128)(2,1)S(1)}, u32[]{:S(2)}, u32[]{:S(2)}) collective-permute-start(bf16[512,1152]{1,0:T(8,128)(2,1)} %bitcast.148), channel_id=1, source_target_pairs={{0,1},{1,2},{2,3},{4,5},{5,6},{6,7},{8,9},{9,10},{10,11},{12,13},{... | collective-permute-start | bytes 3538952 | tf_op jit(solution)/shard_map/ppermute | solution.py:413
  12.4 46.8 %collective-permute-start = (bf16[512,1152]{1,0:T(8,128)(2,1)}, bf16[512,1152]{1,0:T(8,128)(2,1)S(1)}, u32[]{:S(2)}, u32[]{:S(2)}) collective-permute-start(bf16[512,1152]{1,0:T(8,128)(2,1)} %bitcast.149), channel_id=1, source_target_pairs={{1,0},{2,1},{3,2},{5,4},{6,5},{7,6},{9,8},{10,9},{11,10},{13,12},{... | collective-permute-start | bytes 3538952 | tf_op jit(solution)/shard_map/ppermute | solution.py:412
  18.6 140.3 %all-gather.7.cloned.1.call-start = ((), (), s32[]{:S(2)}) async-start(), calls=%async_computation.4 | async-start | bytes 8957952 | tf_op jit(solution)/shard_map/all_gather | solution.py:473
  30.6 29.7 %copy-start.48 = (f32[3,512]{1,0:T(4,128)}, f32[3,512]{1,0:T(4,128)S(1)}, u32[]{:S(2)}) copy-start(f32[3,512]{1,0:T(4,128)S(1)} %get-tuple-element.104) | copy-start | bytes 18436
  64.2 152.9 %all-gather.9.cloned.1.call-start = ((), (), s32[]{:S(2)}) async-start(), calls=%async_computation.5 | async-start | bytes 14266368 | tf_op jit(solution)/shard_map/all_gather | solution.py:478
  64.3 46.5 %copy-start.77 = (pred[4]{0:T(512)(128)(4,1)}, pred[4]{0:T(512)(128)(4,1)S(1)}, u32[]{:S(2)}) copy-start(pred[4]{0:T(512)(128)(4,1)S(1)} %compare_and_fusion) | copy-start | bytes 16
  64.3 18.0 %copy-start.76 = (s32[1024]{0:T(1024)}, s32[1024]{0:T(1024)S(1)}, u32[]{:S(2)}) copy-start(s32[1024]{0:T(1024)S(1)} %pad_clamp_fusion.1) | copy-start | bytes 12292
  71.1 11.3 %collective-permute-start.4 = (bf16[144,1364]{1,0:T(8,128)(2,1)}, bf16[144,1364]{1,0:T(8,128)(2,1)S(1)}, u32[]{:S(2)}, u32[]{:S(2)}) collective-permute-start(bf16[144,1364]{1,0:T(8,128)(2,1)} %copy_after.2), channel_id=1, source_target_pairs={{0,3},{1,0},{2,1},{3,2},{4,7},{5,4},{6,5},{7,6},{8,11},{9,8},{10,9... | collective-permute-start | bytes 1178504 | tf_op jit(solution)/shard_map/ppermute | solution.py:80
  73.2 36.3 %collective-permute-start.3 = (bf16[144,1364]{1,0:T(8,128)(2,1)}, bf16[144,1364]{1,0:T(8,128)(2,1)S(1)}, u32[]{:S(2)}, u32[]{:S(2)}) collective-permute-start(bf16[144,1364]{1,0:T(8,128)(2,1)} %copy_after.2), channel_id=1, source_target_pairs={{0,2},{1,3},{2,0},{3,1},{4,6},{5,7},{6,4},{7,5},{8,10},{9,11},{10,... | collective-permute-start | bytes 1178504 | tf_op jit(solution)/shard_map/ppermute | solution.py:80
  75.2 34.3 %collective-permute-start.2 = (bf16[144,1364]{1,0:T(8,128)(2,1)}, bf16[144,1364]{1,0:T(8,128)(2,1)S(1)}, u32[]{:S(2)}, u32[]{:S(2)}) collective-permute-start(bf16[144,1364]{1,0:T(8,128)(2,1)} %copy_after.2), channel_id=1, source_target_pairs={{0,1},{1,2},{2,3},{3,0},{4,5},{5,6},{6,7},{7,4},{8,9},{9,10},{10,1... | collective-permute-start | bytes 1178504 | tf_op jit(solution)/shard_map/ppermute | solution.py:80
  82.3 28.6 %copy-start.22 = (bf16[144,1364]{1,0:T(8,128)(2,1)}, bf16[144,1364]{1,0:T(8,128)(2,1)S(1)}, u32[]{:S(2)}) copy-start(bf16[144,1364]{1,0:T(8,128)(2,1)S(1)} %collective-permute-done.4.refs_3_) | copy-start | bytes 1178500
  114.2 140.7 %all-gather.11.cloned.1.call-start = ((), (), s32[]{:S(2)}) async-start(), calls=%async_computation.6 | async-start | bytes 11280384 | tf_op jit(solution)/shard_map/all_gather | solution.py:502
  114.3 29.2 %collective-permute-start.5 = (bf16[512,1152]{1,0:T(8,128)(2,1)}, bf16[512,1152]{1,0:T(8,128)(2,1)S(1)}, u32[]{:S(2)}, u32[]{:S(2)}) collective-permute-start(bf16[512,1152]{1,0:T(8,128)(2,1)} %after.26.x_ref), channel_id=1, source_target_pairs={{1,0},{2,1},{3,2},{5,4},{6,5},{7,6},{9,8},{10,9},{11,10},{13,12},{... | collective-permute-start | bytes 3538952 | tf_op jit(solution)/shard_map/ppermute | solution.py:444
  115.6 29.2 %collective-permute-start.6 = (bf16[512,1152]{1,0:T(8,128)(2,1)}, bf16[512,1152]{1,0:T(8,128)(2,1)S(1)}, u32[]{:S(2)}, u32[]{:S(2)}) collective-permute-start(bf16[512,1152]{1,0:T(8,128)(2,1)} %after.27.x_ref), channel_id=1, source_target_pairs={{0,1},{1,2},{2,3},{4,5},{5,6},{6,7},{8,9},{9,10},{10,11},{12,13},{... | collective-permute-start | bytes 3538952 | tf_op jit(solution)/shard_map/ppermute | solution.py:445
  121.5 161.7 %copy-start.55 = (f32[1152]{0:T(1024)}, f32[1152]{0:T(1024)S(1)}, u32[]{:S(2)}) copy-start(f32[1152]{0:T(1024)S(1)} %get-tuple-element.41) | copy-start | bytes 13828
  147.6 36.2 %collective-permute-start.9 = (bf16[144,1076]{1,0:T(8,128)(2,1)}, bf16[144,1076]{1,0:T(8,128)(2,1)S(1)}, u32[]{:S(2)}, u32[]{:S(2)}) collective-permute-start(bf16[144,1076]{1,0:T(8,128)(2,1)} %copy_after.3), channel_id=1, source_target_pairs={{0,3},{1,0},{2,1},{3,2},{4,7},{5,4},{6,5},{7,6},{8,11},{9,8},{10,9... | collective-permute-start | bytes 929672 | tf_op jit(solution)/shard_map/ppermute | solution.py:80
  151.3 33.2 %collective-permute-start.8 = (bf16[144,1076]{1,0:T(8,128)(2,1)}, bf16[144,1076]{1,0:T(8,128)(2,1)S(1)}, u32[]{:S(2)}, u32[]{:S(2)}) collective-permute-start(bf16[144,1076]{1,0:T(8,128)(2,1)} %copy_after.3), channel_id=1, source_target_pairs={{0,2},{1,3},{2,0},{3,1},{4,6},{5,7},{6,4},{7,5},{8,10},{9,11},{10,... | collective-permute-start | bytes 929672 | tf_op jit(solution)/shard_map/ppermute | solution.py:80
  151.4 33.8 %collective-permute-start.7 = (bf16[144,1076]{1,0:T(8,128)(2,1)}, bf16[144,1076]{1,0:T(8,128)(2,1)S(1)}, u32[]{:S(2)}, u32[]{:S(2)}) collective-permute-start(bf16[144,1076]{1,0:T(8,128)(2,1)} %copy_after.3), channel_id=1, source_target_pairs={{0,1},{1,2},{2,3},{3,0},{4,5},{5,6},{6,7},{7,4},{8,9},{9,10},{10,1... | collective-permute-start | bytes 929672 | tf_op jit(solution)/shard_map/ppermute | solution.py:80
  189.8 148.0 %reduce-scatter.5.cloned.1.call-start = ((), (), s32[]{:S(2)}) async-start(), calls=%async_computation.7 | async-start | bytes 11280384 | tf_op jit(solution)/shard_map/reduce_scatter | solution.py:528
  195.8 21.2 %copy-start.3 = (bf16[1,512,1152]{2,1,0:T(8,128)(2,1)S(1)}, bf16[1,512,1152]{2,1,0:T(8,128)(2,1)}, u32[]{:S(2)}) copy-start(bf16[1,512,1152]{2,1,0:T(8,128)(2,1)} %param.20) | copy-start | bytes 3538948
  221.3 74.9 %copy-start.10 = (f32[512,1152]{1,0:T(8,128)}, f32[512,1152]{1,0:T(8,128)S(1)}, u32[]{:S(2)}) copy-start(f32[512,1152]{1,0:T(8,128)S(1)} %get-tuple-element.107) | copy-start | bytes 7077892
  221.4 47.4 %copy-start.60 = (f32[512]{0:T(512)}, f32[512]{0:T(512)S(1)}, u32[]{:S(2)}) copy-start(f32[512]{0:T(512)S(1)} %broadcast_multiply_fusion.5) | copy-start | bytes 6148
  243.2 177.6 %reduce-scatter.9.cloned.1.call-start = ((), (), s32[]{:S(2)}) async-start(), calls=%async_computation.9 | async-start | bytes 11280384 | tf_op jit(solution)/shard_map/reduce_scatter | solution.py:541
  280.0 229.3 %reduce-scatter.7.cloned.1.call-start = ((), (), s32[]{:S(2)}) async-start(), calls=%async_computation.8 | async-start | bytes 11943936 | tf_op jit(solution)/shard_map/reduce_scatter | solution.py:632
  337.7 45.0 %slice-start.2 = ((s8[4718592]{0:T(1024)(128)(4,1)}), s8[4194304]{0:T(1024)(128)(4,1)S(1)}, s32[]{:S(2)}) async-start(s8[4718592]{0:T(1024)(128)(4,1)} %bitcast.144), calls=%async_computation.14 | async-start | bytes 8388608
  339.5 46.5 %collective-permute-start.12 = (bf16[144,1076]{1,0:T(8,128)(2,1)S(1)}, bf16[144,1076]{1,0:T(8,128)(2,1)S(1)}, u32[]{:S(2)}, u32[]{:S(2)}) collective-permute-start(bf16[144,1076]{1,0:T(8,128)(2,1)S(1)} %get-tuple-element.55), channel_id=1, source_target_pairs={{0,1},{1,2},{2,3},{3,0},{4,5},{5,6},{6,7},{7,4},{8,9},{9,10},{10,1... | collective-permute-start | bytes 929672 | tf_op jit(solution)/shard_map/ppermute | solution.py:585
  341.0 45.7 %collective-permute-start.11 = (bf16[144,1076]{1,0:T(8,128)(2,1)S(1)}, bf16[144,1076]{1,0:T(8,128)(2,1)S(1)}, u32[]{:S(2)}, u32[]{:S(2)}) collective-permute-start(bf16[144,1076]{1,0:T(8,128)(2,1)S(1)} %get-tuple-element.56), channel_id=1, source_target_pairs={{0,2},{1,3},{2,0},{3,1},{4,6},{5,7},{6,4},{7,5},{8,10},{9,11},{10,... | collective-permute-start | bytes 929672 | tf_op jit(solution)/shard_map/ppermute | solution.py:585
  343.4 44.1 %collective-permute-start.10 = (bf16[144,1076]{1,0:T(8,128)(2,1)S(1)}, bf16[144,1076]{1,0:T(8,128)(2,1)S(1)}, u32[]{:S(2)}, u32[]{:S(2)}) collective-permute-start(bf16[144,1076]{1,0:T(8,128)(2,1)S(1)} %get-tuple-element.57), channel_id=1, source_target_pairs={{0,3},{1,0},{2,1},{3,2},{4,7},{5,4},{6,5},{7,6},{8,11},{9,8},{10,9... | collective-permute-start | bytes 929672 | tf_op jit(solution)/shard_map/ppermute | solution.py:585
  344.9 37.9 %slice-start.3 = ((s8[4718592]{0:T(1024)(128)(4,1)}), s8[524288]{0:T(1024)(128)(4,1)S(1)}, s32[]{:S(2)}) async-start(s8[4718592]{0:T(1024)(128)(4,1)} %bitcast.144), calls=%async_computation.15 | async-start | bytes 1048576
  371.8 33.2 %collective-permute-start.14 = (bf16[512,1152]{1,0:T(8,128)(2,1)S(1)}, bf16[512,1152]{1,0:T(8,128)(2,1)S(1)}, u32[]{:S(2)}, u32[]{:S(2)}) collective-permute-start(bf16[512,1152]{1,0:T(8,128)(2,1)S(1)} %get-tuple-element.58.refs_2_), channel_id=1, source_target_pairs={{1,0},{2,1},{3,2},{5,4},{6,5},{7,6},{9,8},{10,9},{11,10},{13,12},{... | collective-permute-start | bytes 3538952 | tf_op jit(solution)/shard_map/ppermute | solution.py:621
  373.1 33.1 %collective-permute-start.13 = (bf16[512,1152]{1,0:T(8,128)(2,1)S(1)}, bf16[512,1152]{1,0:T(8,128)(2,1)}, u32[]{:S(2)}, u32[]{:S(2)}) collective-permute-start(bf16[512,1152]{1,0:T(8,128)(2,1)S(1)} %get-tuple-element.59.refs_1_), channel_id=1, source_target_pairs={{0,1},{1,2},{2,3},{4,5},{5,6},{6,7},{8,9},{9,10},{10,11},{12,13},{... | collective-permute-start | bytes 3538952 | tf_op jit(solution)/shard_map/ppermute | solution.py:620
  415.0 137.4 %reduce-scatter.11.cloned.1.call-start = ((), (), s32[]{:S(2)}) async-start(), calls=%async_computation.10 | async-start | bytes 1658880 | tf_op jit(solution)/shard_map/reduce_scatter | solution.py:697
  423.2 18.6 %collective-permute-start.16 = (bf16[144,1076]{1,0:T(8,128)(2,1)S(1)}, bf16[144,1076]{1,0:T(8,128)(2,1)S(1)}, u32[]{:S(2)}, u32[]{:S(2)}) collective-permute-start(bf16[144,1076]{1,0:T(8,128)(2,1)S(1)} %get-tuple-element.53), channel_id=1, source_target_pairs={{0,2},{1,3},{2,0},{3,1},{4,6},{5,7},{6,4},{7,5},{8,10},{9,11},{10,... | collective-permute-start | bytes 929672 | tf_op jit(solution)/shard_map/ppermute | solution.py:635
  425.5 17.0 %collective-permute-start.15 = (bf16[144,1076]{1,0:T(8,128)(2,1)S(1)}, bf16[144,1076]{1,0:T(8,128)(2,1)S(1)}, u32[]{:S(2)}, u32[]{:S(2)}) collective-permute-start(bf16[144,1076]{1,0:T(8,128)(2,1)S(1)} %get-tuple-element.54), channel_id=1, source_target_pairs={{0,3},{1,0},{2,1},{3,2},{4,7},{5,4},{6,5},{7,6},{8,11},{9,8},{10,9... | collective-permute-start | bytes 929672 | tf_op jit(solution)/shard_map/ppermute | solution.py:635
  434.7 43.3 %collective-permute-start.18 = (bf16[512,1152]{1,0:T(8,128)(2,1)S(1)}, bf16[512,1152]{1,0:T(8,128)(2,1)}, u32[]{:S(2)}, u32[]{:S(2)}) collective-permute-start(bf16[512,1152]{1,0:T(8,128)(2,1)S(1)} %add_convert_fusion.2.refs_1_), channel_id=1, source_target_pairs={{0,1},{1,2},{2,3},{4,5},{5,6},{6,7},{8,9},{9,10},{10,11},{12,13},{... | collective-permute-start | bytes 3538952 | tf_op jit(solution)/shard_map/ppermute | solution.py:650
  465.1 34.6 %collective-permute-start.19 = (bf16[512,1152]{1,0:T(8,128)(2,1)}, bf16[512,1152]{1,0:T(8,128)(2,1)}, u32[]{:S(2)}, u32[]{:S(2)}) collective-permute-start(bf16[512,1152]{1,0:T(8,128)(2,1)} %get-tuple-element.111), channel_id=1, source_target_pairs={{1,0},{2,1},{3,2},{5,4},{6,5},{7,6},{9,8},{10,9},{11,10},{13,12},{... | collective-permute-start | bytes 3538952 | tf_op jit(solution)/shard_map/ppermute | solution.py:656
  471.0 38.4 %collective-permute-start.17 = (bf16[144,1076]{1,0:T(8,128)(2,1)}, bf16[144,1076]{1,0:T(8,128)(2,1)}, u32[]{:S(2)}, u32[]{:S(2)}) collective-permute-start(bf16[144,1076]{1,0:T(8,128)(2,1)} %get-tuple-element.52), channel_id=1, source_target_pairs={{0,1},{1,2},{2,3},{3,0},{4,5},{5,6},{6,7},{7,4},{8,9},{9,10},{10,1... | collective-permute-start | bytes 929672 | tf_op jit(solution)/shard_map/ppermute | solution.py:635
  478.2 21.5 %copy-start.6 = (f32[512,1152]{1,0:T(8,128)S(1)}, f32[512,1152]{1,0:T(8,128)}, u32[]{:S(2)}) copy-start(f32[512,1152]{1,0:T(8,128)} %fusion.22.refs_1_) | copy-start | bytes 7077892
  478.2 21.4 %copy-start.51 = (f32[1152]{0:T(1024)S(1)}, f32[1152]{0:T(1024)}, u32[]{:S(2)}) copy-start(f32[1152]{0:T(1024)} %get-tuple-element.38) | copy-start | bytes 13828
  478.2 21.4 %copy-start.57 = (f32[512]{0:T(512)S(1)}, f32[512]{0:T(512)}, u32[]{:S(2)}) copy-start(f32[512]{0:T(512)} %copy-done.56) | copy-start | bytes 6148
  478.2 21.4 %copy-start.65 = (f32[512]{0:T(512)S(1)}, f32[512]{0:T(512)}, u32[]{:S(2)}) copy-start(f32[512]{0:T(512)} %add_rsqrt_fusion) | copy-start | bytes 6148
  512.2 4.4 collective-permute-start.20
  518.1 5.4 collective-permute-start.21
  524.4 1.3 collective-permute-start.22
  525.7 7.1 %collective-permute-start.23 = (f32[13520]{0:T(1024)S(1)}, f32[13520]{0:T(1024)S(1)}, u32[]{:S(2)}, u32[]{:S(2)}) collective-permute-start(f32[13520]{0:T(1024)S(1)} %add.322), channel_id=1, source_target_pairs={{0,8},{4,12},{8,0},{12,4},{16,24},{20,28},{24,16},{28,20},{1,9},{5... | collective-permute-start | bytes 162248 | tf_op jit(solution)/shard_map/ppermute | solution.py:685
  532.8 13.3 %collective-permute-start.24 = (f32[13520]{0:T(1024)S(1)}, f32[13520]{0:T(1024)S(1)}, u32[]{:S(2)}, u32[]{:S(2)}) collective-permute-start(f32[13520]{0:T(1024)S(1)} %add.323), channel_id=1, source_target_pairs={{0,16},{4,20},{8,24},{12,28},{16,0},{20,4},{24,8},{28,12},{1,17},{... | collective-permute-start | bytes 162248 | tf_op jit(solution)/shard_map/ppermute | solution.py:685
  (74 other events, 374.9 us)
Sparse Core Ops, SparseCore 0:
  18.7 41.3 all-gather.12
  64.3 52.2 all-gather.6
  119.2 72.5 all-gather.8
  193.5 61.3 all-gather.10
  258.4 79.3 reduce-scatter.4
  341.6 79.1 reduce-scatter.8
  424.3 82.2 reduce-scatter.6
  519.5 32.8 reduce-scatter.10

commit v5 on v4

--- a/solution.py
+++ b/solution.py
@@ -148,10 +148,13 @@
         out = []
         for (b, h), (top, acc) in zip(jobs, carry):
             q_part = q_ref[h, :, b * q_block : (b + 1) * q_block]
-            starts = [index_ref[b * chunks + t * pair + u] * k_block for u in range(pair)]
-            heres = [pl.ds(pl.multiple_of(start, k_block), k_block) for start in starts]
-            k_part = jnp.concatenate([k_ref[h, :, here] for here in heres], axis=1)
-            v_part = jnp.concatenate([v_ref[h, :, here] for here in heres], axis=1)
+            if pair == chunks:
+                k_part, v_part = k_ref[h], v_ref[h]
+            else:
+                starts = [index_ref[b * chunks + t * pair + u] * k_block for u in range(pair)]
+                heres = [pl.ds(pl.multiple_of(start, k_block), k_block) for start in starts]
+                k_part = jnp.concatenate([k_ref[h, :, here] for here in heres], axis=1)
+                v_part = jnp.concatenate([v_ref[h, :, here] for here in heres], axis=1)
             scores = lax.dot_general(
                 k_part, q_part, (((0,), (0,)), ((), ())), preferred_element_type=F32
             )
@@ -166,7 +169,7 @@
     first = tuple(
         (jnp.full((1, q_block), MASKED, F32), jnp.zeros((rows, q_block), F32)) for _ in jobs
     )
-    final = lax.fori_loop(0, count_ref[0], step, first)
+    final = step(0, first) if pair == chunks else lax.fori_loop(0, count_ref[0], step, first)
     for (b, h), (top, acc) in zip(jobs, final):
         cols = slice(b * q_block, (b + 1) * q_block)
         live = valid_ref[:, cols] > 0
@@ -230,10 +233,13 @@
         for (b, h), dq in zip(jobs, carry):
             cols = slice(b * q_block, (b + 1) * q_block)
             q_part, g_part = q_ref[h, :, cols], g_ref[h, :, cols]
-            starts = [index_ref[b * chunks + t * pair + u] * k_block for u in range(pair)]
-            heres = [pl.ds(pl.multiple_of(start, k_block), k_block) for start in starts]
-            k_part = jnp.concatenate([k_ref[h, :, here] for here in heres], axis=1)
-            v_part = jnp.concatenate([v_ref[h, :, here] for here in heres], axis=1)
+            if pair == chunks:
+                k_part, v_part = k_ref[h], v_ref[h]
+            else:
+                starts = [index_ref[b * chunks + t * pair + u] * k_block for u in range(pair)]
+                heres = [pl.ds(pl.multiple_of(start, k_block), k_block) for start in starts]
+                k_part = jnp.concatenate([k_ref[h, :, here] for here in heres], axis=1)
+                v_part = jnp.concatenate([v_ref[h, :, here] for here in heres], axis=1)
             scores = lax.dot_general(
                 k_part, q_part, (((0,), (0,)), ((), ())), preferred_element_type=F32
             )
@@ -249,6 +255,8 @@
             dv = lax.dot_general(
                 g_part, probs.astype(BF), (((1,), (1,)), ((), ())), preferred_element_type=F32
             )
+            if pair == chunks:
+                heres = [slice(u * k_block, (u + 1) * k_block) for u in range(pair)]
             sums.append((h, heres, dk, dv))
             out.append(dq)
         for h, heres, dk, dv in sums:
@@ -258,7 +266,7 @@
         return tuple(out)
 
     first = tuple(jnp.zeros((rows, q_block), F32) for _ in jobs)
-    final = lax.fori_loop(0, count_ref[0], step, first)
+    final = step(0, first) if pair == chunks else lax.fori_loop(0, count_ref[0], step, first)
     for (b, h), dq in zip(jobs, final):
         cols = slice(b * q_block, (b + 1) * q_block)
         dq_ref[h, :, cols] = (dq[:dim] * dim**-0.5).astype(BF)
@@ -374,7 +382,7 @@
     valid_col = valid[:, None]
     q_block = min(512, here)
     k_block = min(256, here)
-    pair = 2 if k_len % (2 * k_block) == 0 else 1
+    pair = k_len // k_block
     picture = jnp.arange(pics, dtype=jnp.int32)
     q_has = jnp.any(own_seg.reshape(-1, q_block, 1) == picture, axis=1)
     k_has = jnp.any(key_seg.reshape(-1, k_block, 1) == picture, axis=1)
@@ -459,7 +467,6 @@
             normed_all = norm_slot(
                 tokens, gain_one, shift_one, position + 1, slot_count, normed_all
             )
-    first_down = copy_after(down_weight[0], later[-1], prior[-1])
 
     def widen(body, added):
         body = body.reshape(heads, HEAD_DIM, body.shape[-1])
@@ -489,6 +496,7 @@
         (product("td,dc->ct", normed, query_full) + query_shift[:, None])
         * (scale * math.log2(math.e))
     ).astype(BF)
+    first_down = copy_after(down_weight[0], later[-1], prior[-1], queries)
     q_rest = jnp.zeros((AUG - (pics + 1), here), F32)
     q_aug = widen(queries, jnp.concatenate([q_mask, q_rest], axis=0))
 
@@ -497,7 +505,7 @@
     k_aug = after(widen(keys, k_added))
     v_aug = after(widen(values.astype(BF), v_added))
     down_slots = slots_along_tp(first_down, n, k_aug, v_aug)
-    group = 4 if heads % 8 == 0 else 1
+    group = 2 if heads % 4 == 0 else 1
     down_shard = jnp.concatenate(down_slots, axis=1)
     down_full = lax.all_gather(down_shard, "fsdp", axis=0, tiled=True)
     attended, log_total = attend(

time: 569 us -> 569 us (level)
  Pallas kernels: 82.2 us -> 104 us
  waiting for transfers between devices: 114 us -> 100 us
    pallas_call x2, Pallas kernels: 38.6 us -> 52 us  [attend_back(): pl.pallas_call(functools.partial(attend_back_kernel, q_block=q_block, k_b...]
    pallas_call x1, Pallas kernels: 21.2 us -> 29.9 us  [attend(): pl.pallas_call(functools.partial(attend_kernel, q_block=q_block, k_block=...]
    all_gather x1, waiting for transfers between devices: 11.4 us -> 3.21 us  [local(): down_full = lax.all_gather(down_shard, 'fsdp', axis=0, tiled=True)]
    reduce_scatter x1, waiting for transfers between devices: 11.2 us -> 4.93 us  [local(): lax.psum_scatter(down_grad, 'fsdp', scatter_dimension=0, tiled=True)]
    unnamed x179 -> x163, local copies, waits for them, and re-layouts: 25 us -> 22.2 us
  transfers between devices with their start and end apart: 33 -> 33, of which waited for: 18 -> 19; matrix products, arithmetic and copies ran while one was open for 45% -> 44% of each run, Pallas kernels for 14% -> 18%
where the time goes in v5:
time: 569 us; the launch traced here: 560 us
  matrix products  151 us (27%)
  Pallas kernels  104 us (18%)
  waiting for transfers between devices  100 us (18%)
  other arithmetic  63.8 us (11%)
  local copies, waits for them, and re-layouts  61.8 us (11%)
  starting transfers between devices  52 us (9%)
  between operations  17 us (3%)
  blocking collectives  9.37 us (2%)
    dot_general x19, matrix products, product(): return jnp.einsum(form, left, right, preferred_element_type=F32)  151 us
    pallas_call x2, Pallas kernels, attend_back(): pl.pallas_call(functools.partial(attend_back_kernel, q_block=q_block, k_b...  52 us
    ppermute x6, waiting for transfers between devices, slots_along_tp(): lax.ppermute(piece, 'tp', [(i, (i + distance) % count) for i in range(cou...  35.1 us
    pallas_call x1, Pallas kernels, attend(): pl.pallas_call(functools.partial(attend_kernel, q_block=q_block, k_block=...  29.9 us
    unnamed x163, local copies, waits for them, and re-layouts  22.2 us
    ppermute x1, waiting for transfers between devices, local(): moving_left = lax.ppermute(joined(moving_left, to_prior[1]), 'tp', to_left)  18.1 us
    pallas_call x4, Pallas kernels, norm_slot(): pl.pallas_call(norm_kernel, grid=(steps,), in_specs=[pl.BlockSpec((block,...  15.9 us
  transfers between devices with their start and end apart: 33, of which 19 were waited for; matrix products, arithmetic and copies ran while one was open for 44% of the time, Pallas kernels for 18%

profile of v5, /device:TPU:0, one launch (start us, length us, event | category | flops | bytes accessed | tf_op | source)
XLA Modules:
  0.0 560.0 jit_solution(10965817837608801612)
XLA Ops:
  7.2 5.1 collective-permute-start.1
  37.7 9.4 %all-gather.1 = f32[8,144,6]{1,2,0:T(8,128)S(1)} all-gather(f32[1,144,6]{1,2,0:T(8,128)} %bitcast.170), channel_id=1, replica_groups=mesh['fsdp'=8,'tp'=4] {'fsdp'}, dimensions={0}, use_global_device_ids=true | all-gather | bytes 31104 | tf_op jit(solution)/shard_map/all_gather | solution.py:365
  54.0 5.2 collective-permute-done.refs_8_.refs_0_
  77.4 5.0 collective-permute-done.4.refs_3_
  82.4 27.1 %collective-permute-done.3.refs_2_ = bf16[144,1364]{1,0:T(8,128)(2,1)S(1)} collective-permute-done((bf16[144,1364]{1,0:T(8,128)(2,1)}, bf16[144,1364]{1,0:T(8,128)(2,1)S(1)}, u32[]{:S(2)}, u32[]{:S(2)}) %collective-permute-start.3) | collective-permute-done | bytes 392864 | tf_op jit(solution)/shard_map/ppermute | solution.py:80
  115.6 4.6 collective-permute-start.6
  121.5 4.0 norm_slot.4.rest_0_
  125.4 4.0 norm_slot.5.rest_0_
  129.4 4.0 norm_slot.6.rest_0_
  133.4 10.1 %collective-permute-done.5.refs_0_ = bf16[512,1152]{1,0:T(8,128)(2,1)S(1)} collective-permute-done((bf16[512,1152]{1,0:T(8,128)(2,1)}, bf16[512,1152]{1,0:T(8,128)(2,1)S(1)}, u32[]{:S(2)}, u32[]{:S(2)}) %collective-permute-start.5) | collective-permute-done | bytes 1179680 | tf_op jit(solution)/shard_map/ppermute | solution.py:452
  146.1 3.9 norm_slot.7
  150.0 5.0 fusion.29.refs_2_
  156.8 3.7 collective-permute-start.9
  161.8 8.3 %add_convert_fusion = bf16[1152,2048]{1,0:T(8,128)(2,1)S(1)} fusion(bf16[2048,1152]{1,0:T(8,128)(2,1)S(1)} %copy-done, f32[1152]{0:T(1024)S(1)} %copy-done.54, bf16[1152,3456]{1,0:T(8,128)(2,1)} %all-gather.7.cloned.1.call-done), kind=kOutput, calls=%fused_computation.10 | convolution fusion | flops 5440536576 | bytes 12096000 | tf_op jit(solution)/shard_map/td,dc->ct/dot_general | solution.py:37
  172.9 8.5 %convolution_convert_fusion.5 = bf16[1152,2048]{1,0:T(8,128)(2,1)S(1)} fusion(bf16[2048,1152]{1,0:T(8,128)(2,1)S(1)} %copy-done, bf16[1152,3456]{1,0:T(8,128)(2,1)} %all-gather.7.cloned.1.call-done), kind=kOutput, calls=%fused_computation.27 | convolution fusion | flops 5438177280 | bytes 12091392 | tf_op jit(solution)/shard_map/td,dc->ct/dot_general | solution.py:37
  190.1 3.3 concatenate.144.rest_0_
  195.2 29.9 %attend.1 = (bf16[16,72,512]{2,1,0:T(8,128)(2,1)}, f32[16,1,512]{2,1,0:T(1,128)}) custom-call(s32[1]{0:T(128)S(6)} %neg.49.refs_2_.count_ref, s32[8]{0:T(128)} %select_reduce_fusion.refs_3_.index_ref, bf16[16,80,512]{2,1,0:T(8,128)(2,1)} %pad_maximum_fusion.3.q_ref, bf16[16,80,2048]{2,1,0:T(8,128)(2,1)} %after.28.refs_1_.k_ref, ...), custom_call_target="tpu_custom_call" | custom-call | flops 5368709120 | bytes 13107200 | tf_op jit(solution)/shard_map/attend/pallas_call | solution.py:191
  225.1 4.3 fusion.104
  231.7 9.2 %multiply_convert_fusion = (bf16[512,4304]{1,0:T(8,128)(2,1)S(1)}, f32[512,4304]{1,0:T(8,128)}) fusion(f32[4304]{0:T(1024)S(1)} %copy-done.47, bf16[1152,5456]{1,0:T(8,128)(2,1)S(1)} %copy-done.77, f32[512,1152]{1,0:T(8,128)S(1)} %get-tuple-element.107, f32[1152]{0:T(1024)S(1)} %get-tuple-element.40, f32[1152]{0:T(1024)S(1)} %get-tuple-element.41, ...), kind=kOutput, calls=%fused_computation.19 | convolution fusion | flops 5102190592 | bytes 25649152 | tf_op jit(solution)/shard_map/td,df->tf/dot_general | solution.py:37
  243.0 8.3 %convolution_convert_fusion.1.refs_1_ = bf16[1152,4304]{1,0:T(8,128)(2,1)} fusion(bf16[512,1152]{1,0:T(8,128)(2,1)S(1)} %copy-done.10, bf16[512,4304]{1,0:T(8,128)(2,1)S(1)} %get-tuple-element.108.refs_0_), kind=kOutput, calls=%fused_computation.4 | convolution fusion | flops 5082163200 | bytes 15503360 | tf_op jit(solution)/shard_map/td,tf->df/dot_general | solution.py:37
  251.6 3.2 all-gather.11.cloned.1.call-done
  254.8 13.4 %convert_reduce_fusion.1 = (f32[4304]{0:T(1024)S(1)}, bf16[512,4304]{1,0:T(8,128)(2,1)S(1)}) fusion(f32[512,4304]{1,0:T(8,128)} %get-tuple-element.109, bf16[512,1152]{1,0:T(8,128)(2,1)} %after.33, bf16[1152,4304]{1,0:T(8,128)(2,1)} %all-gather.11.cloned.1.call-done), kind=kOutput, calls=%fused_computation.18 | convolution fusion | flops 5125681152 | bytes 24335168 | tf_op jit(solution)/shard_map/td,df->tf/dot_general | solution.py:37
  270.8 8.7 %convolution_convert_fusion.rest_0_ = bf16[1152,4304]{1,0:T(8,128)(2,1)} fusion(bf16[512,4304]{1,0:T(8,128)(2,1)S(1)} %get-tuple-element.46, f32[512,1152]{1,0:T(8,128)S(1)} %copy-done.13, f32[1152]{0:T(1024)S(1)} %get-tuple-element.40, f32[1152]{0:T(1024)S(1)} %get-tuple-element.41, f32[512]{0:T(512)S(1)} %add_rsqrt_fusion.1, ...), kind=kOutput, calls=%fused_computation.3 | convolution fusion | flops 5085112320 | bytes 16696320 | tf_op jit(solution)/shard_map/td,tf->df/dot_general | solution.py:37
  281.9 13.7 %multiply_reduce_fusion = (f32[1152]{0:T(1024)}, f32[512]{0:T(512)S(1)}, f32[512]{0:T(512)S(1)}, f32[1152]{0:T(1024)}, f32[512,1152]{1,0:T(8,128)S(1)}) fusion(f32[512,1152]{1,0:T(8,128)} %copy-done.12, f32[512]{0:T(512)S(1)} %add_rsqrt_fusion.1, f32[512]{0:T(512)S(1)} %broadcast_multiply_fusion.5, f32[1152]{0:T(1024)S(1)} %get-tuple-element.41, ...), kind=kOutput, calls=%fused_computation.82 | convolution fusion | flops 5082510336 | bytes 19224064 | tf_op jit(solution)/shard_map/tf,df->td/dot_general | solution.py:37
  297.3 4.5 fusion.39
  303.6 3.3 convolution_convert_fusion.4.rest_1_.refs_0_
  306.8 25.7 %attend_back.2 = (bf16[16,72,512]{2,1,0:T(8,128)(2,1)}, bf16[2,16,72,2048]{3,2,1,0:T(8,128)(2,1)}) custom-call(s32[1]{0:T(128)S(6)} %neg.49.refs_2_.count_ref, s32[8]{0:T(128)} %select_reduce_fusion.refs_3_.index_ref, bf16[16,80,512]{2,1,0:T(8,128)(2,1)} %maximum_maximum_fusion.q_ref, bf16[16,80,2048]{2,1,0:T(8,128)(2,1)} %after.28.refs_1_.k_ref, ...), custom_call_target="tpu_custom_call" | custom-call | flops 13421772800 | bytes 26214400 | tf_op jit(solution)/shard_map/attend_back/pallas_call | solution.py:287
  332.6 4.9 reduce-scatter.5.cloned.1.call-done.refs_0_
  344.7 26.3 %attend_back.3 = (bf16[16,72,512]{2,1,0:T(8,128)(2,1)}, bf16[2,16,72,2048]{3,2,1,0:T(8,128)(2,1)}) custom-call(s32[1]{0:T(128)S(6)} %neg.49.refs_2_.count_ref, s32[8]{0:T(128)} %select_reduce_fusion.refs_3_.index_ref, bf16[16,80,512]{2,1,0:T(8,128)(2,1)} %maximum_maximum_fusion.q_ref, ...), custom_call_target="tpu_custom_call", output_to_operand_aliasing={{0}: (6, {}), {1}: (7, {})} | custom-call | flops 13421772800 | bytes 26214400 | tf_op jit(solution)/shard_map/attend_back/pallas_call | solution.py:287
  370.9 6.6 %broadcast_select_fusion = (bf16[512,1152]{1,0:T(8,128)(2,1)S(1)}, bf16[512,1152]{1,0:T(8,128)(2,1)S(1)}) fusion(pred[]{:T(512)S(6)} %ge.49, pred[]{:T(512)S(6)} %lt.90, bf16[1152,3456]{1,0:T(8,128)(2,1)} %all-gather.7.cloned.1.call-done, bf16[2304,2048]{1,0:T(8,128)(2,1)} %bitcast.140), kind=kOutput, calls=%fused_computation.104 | convolution fusion | flops 2719678464 | bytes 10027010 | tf_op jit(solution)/shard_map/ct,dc->td/dot_general | solution.py:37
  378.9 5.6 %collective-permute-start.13 = (bf16[512,1152]{1,0:T(8,128)(2,1)S(1)}, bf16[512,1152]{1,0:T(8,128)(2,1)}, u32[]{:S(2)}, u32[]{:S(2)}) collective-permute-start(bf16[512,1152]{1,0:T(8,128)(2,1)S(1)} %get-tuple-element.59.refs_1_), channel_id=1, source_target_pairs={{0,1},{1,2},{2,3},{4,5},{5,6},{6,7},{8,9},{9,10},{10,11},{12,13},{... | collective-permute-start | bytes 3538952 | tf_op jit(solution)/shard_map/ppermute | solution.py:628
  384.5 3.2 convolution_convert_fusion.3.refs_2_
  389.9 15.2 %convolution_convert_fusion.2.refs_1_ = bf16[1152,2304]{1,0:T(8,128)(2,1)} fusion(bf16[2048,1152]{1,0:T(8,128)(2,1)S(1)} %bitcast.143, bf16[2304,2048]{1,0:T(8,128)(2,1)} %after.38.refs_0_), kind=kOutput, calls=%fused_computation.7 | convolution fusion | flops 10874290176 | bytes 19464192 | tf_op jit(solution)/shard_map/td,ct->dc/dot_general | solution.py:37
  409.7 6.3 %pad_maximum_fusion.refs_1_ = bf16[1152,4608]{1,0:T(8,128)(2,1)} fusion(bf16[1152,1152]{1,0:T(8,128)(2,1)} %after.39, bf16[1152,2304]{1,0:T(8,128)(2,1)S(1)} %copy-done.1, bf16[1152,1152]{1,0:T(8,128)(2,1)S(1)} %copy-done.6), kind=kLoop, calls=%fused_computation.8 | loop fusion | flops 31850496 | bytes 21233664 | tf_op jit(solution)/shard_map/concatenate | solution.py:639
  427.3 7.7 %add_convert_fusion.2.refs_1_ = bf16[512,1152]{1,0:T(8,128)(2,1)S(1)} fusion(bf16[512,1152]{1,0:T(8,128)(2,1)} %collective-permute-done.13.refs_3_, bf16[1152,3456]{1,0:T(8,128)(2,1)} %all-gather.7.cloned.1.call-done, bf16[2304,2048]{1,0:T(8,128)(2,1)} %after.41.refs_0_, pred[]{:T(512)S(6)} %lt.81), kind=kOutput, calls=%fused_computation.87 | convolution fusion | flops 2721447936 | bytes 10027009 | tf_op jit(solution)/shard_map/ct,dc->td/dot_general | solution.py:37
  437.5 4.1 collective-permute-done.16.refs_2_.refs_4_
  443.8 3.6 fusion.73
  447.4 7.9 %fusion.22.refs_1_ = f32[512,1152]{1,0:T(8,128)} fusion(f32[512,1152]{1,0:T(8,128)S(1)} %fusion.73, bf16[1152,3456]{1,0:T(8,128)(2,1)} %all-gather.7.cloned.1.call-done, bf16[2304,2048]{1,0:T(8,128)(2,1)} %after.43.refs_0_), kind=kOutput, calls=%fused_computation.41 | convolution fusion | flops 2718498816 | bytes 12386304 | tf_op jit(solution)/shard_map/ct,dc->td/dot_general | solution.py:37
  456.6 8.3 %add_convert_fusion.1 = (bf16[512,1152]{1,0:T(8,128)(2,1)}, bf16[512,1152]{1,0:T(8,128)(2,1)}) fusion(bf16[512,1152]{1,0:T(8,128)(2,1)S(1)} %copy-done.42, bf16[1152,3456]{1,0:T(8,128)(2,1)} %all-gather.7.cloned.1.call-done, bf16[2304,2048]{1,0:T(8,128)(2,1)} %after.45, pred[]{:T(512)S(6)} %ge.50), kind=kOutput, calls=%fused_computation.86 | convolution fusion | flops 2721447936 | bytes 11206657 | tf_op jit(solution)/shard_map/ct,dc->td/dot_general | solution.py:37
  470.8 7.0 %collective-permute-start.17 = (bf16[144,1076]{1,0:T(8,128)(2,1)}, bf16[144,1076]{1,0:T(8,128)(2,1)}, u32[]{:S(2)}, u32[]{:S(2)}) collective-permute-start(bf16[144,1076]{1,0:T(8,128)(2,1)} %get-tuple-element.52), channel_id=1, source_target_pairs={{0,1},{1,2},{2,3},{3,0},{4,5},{5,6},{6,7},{7,4},{8,9},{9,10},{10,1... | collective-permute-start | bytes 929672 | tf_op jit(solution)/shard_map/ppermute | solution.py:643
  478.1 3.3 convert_reduce_fusion
  481.4 18.1 %collective-permute-done.19 = bf16[512,1152]{1,0:T(8,128)(2,1)} collective-permute-done((bf16[512,1152]{1,0:T(8,128)(2,1)}, bf16[512,1152]{1,0:T(8,128)(2,1)}, u32[]{:S(2)}, u32[]{:S(2)}) %collective-permute-start.19) | collective-permute-done | bytes 1179680 | tf_op jit(solution)/shard_map/ppermute | solution.py:664
  499.6 4.7 fusion.63
  505.0 4.3 collective-permute-done.17.refs_5_
  519.2 4.2 collective-permute-done.21
  526.9 3.9 fusion.62
  532.5 11.6 %fusion.54 = bf16[1,512,1152]{2,1,0:T(8,128)(2,1)} fusion(f32[512,1152]{1,0:T(8,128)S(1)} %copy-done.15, bf16[512,4304]{1,0:T(8,128)(2,1)} %after.47, bf16[1152,4304]{1,0:T(8,128)(2,1)} %all-gather.11.cloned.1.call-done, f32[1152]{0:T(1024)S(1)} %copy-done.67, f32[512]{0:T(512)S(1)} %copy-done.63), kind=kOutput, calls=%fused_computation.63 | convolution fusion | flops 5079564288 | bytes 17869312 | tf_op jit(solution)/shard_map/tf,df->td/dot_general | solution.py:37
  546.8 3.8 reduce-scatter.11.cloned.1.call-done
  (382 shorter events, 147.1 us)
Async XLA Ops:
  7.2 44.1 %copy-start.19 = (bf16[1,512,1152]{2,1,0:T(8,128)(2,1)S(1)}, bf16[1,512,1152]{2,1,0:T(8,128)(2,1)}, u32[]{:S(2)}) copy-start(bf16[1,512,1152]{2,1,0:T(8,128)(2,1)} %param.22) | copy-start | bytes 3538948
  7.2 52.8 %all-gather.13.cloned.1.call-start = ((), (), s32[]{:S(2)}) async-start(), calls=%async_computation.11 | async-start | bytes 1361920 | tf_op jit(solution)/shard_map/all_gather | solution.py:363
  7.2 46.7 %collective-permute-start.1 = (bf16[512,1152]{1,0:T(8,128)(2,1)}, bf16[512,1152]{1,0:T(8,128)(2,1)S(1)}, u32[]{:S(2)}, u32[]{:S(2)}) collective-permute-start(bf16[512,1152]{1,0:T(8,128)(2,1)} %bitcast.146), channel_id=1, source_target_pairs={{0,1},{1,2},{2,3},{4,5},{5,6},{6,7},{8,9},{9,10},{10,11},{12,13},{... | collective-permute-start | bytes 3538952 | tf_op jit(solution)/shard_map/ppermute | solution.py:421
  12.4 46.8 %collective-permute-start = (bf16[512,1152]{1,0:T(8,128)(2,1)}, bf16[512,1152]{1,0:T(8,128)(2,1)S(1)}, u32[]{:S(2)}, u32[]{:S(2)}) collective-permute-start(bf16[512,1152]{1,0:T(8,128)(2,1)} %bitcast.147), channel_id=1, source_target_pairs={{1,0},{2,1},{3,2},{5,4},{6,5},{7,6},{9,8},{10,9},{11,10},{13,12},{... | collective-permute-start | bytes 3538952 | tf_op jit(solution)/shard_map/ppermute | solution.py:420
  18.6 131.5 %all-gather.7.cloned.1.call-start = ((), (), s32[]{:S(2)}) async-start(), calls=%async_computation.4 | async-start | bytes 8957952 | tf_op jit(solution)/shard_map/all_gather | solution.py:480
  29.3 30.9 %copy-start.50 = (f32[3,512]{1,0:T(4,128)}, f32[3,512]{1,0:T(4,128)S(1)}, u32[]{:S(2)}) copy-start(f32[3,512]{1,0:T(4,128)S(1)} %get-tuple-element.104) | copy-start | bytes 18436
  64.1 161.0 %all-gather.9.cloned.1.call-start = ((), (), s32[]{:S(2)}) async-start(), calls=%async_computation.5 | async-start | bytes 14266368 | tf_op jit(solution)/shard_map/all_gather | solution.py:485
  64.2 46.6 %copy-start.71 = (pred[4]{0:T(512)(128)(4,1)}, pred[4]{0:T(512)(128)(4,1)S(1)}, u32[]{:S(2)}) copy-start(pred[4]{0:T(512)(128)(4,1)S(1)} %compare_and_fusion) | copy-start | bytes 16
  64.2 18.2 %copy-start.70 = (s32[1024]{0:T(1024)}, s32[1024]{0:T(1024)S(1)}, u32[]{:S(2)}) copy-start(s32[1024]{0:T(1024)S(1)} %pad_clamp_fusion.1) | copy-start | bytes 12292
  70.9 11.4 %collective-permute-start.4 = (bf16[144,1364]{1,0:T(8,128)(2,1)}, bf16[144,1364]{1,0:T(8,128)(2,1)S(1)}, u32[]{:S(2)}, u32[]{:S(2)}) collective-permute-start(bf16[144,1364]{1,0:T(8,128)(2,1)} %copy_after.2), channel_id=1, source_target_pairs={{0,3},{1,0},{2,1},{3,2},{4,7},{5,4},{6,5},{7,6},{8,11},{9,8},{10,9... | collective-permute-start | bytes 1178504 | tf_op jit(solution)/shard_map/ppermute | solution.py:80
  73.2 36.3 %collective-permute-start.3 = (bf16[144,1364]{1,0:T(8,128)(2,1)}, bf16[144,1364]{1,0:T(8,128)(2,1)S(1)}, u32[]{:S(2)}, u32[]{:S(2)}) collective-permute-start(bf16[144,1364]{1,0:T(8,128)(2,1)} %copy_after.2), channel_id=1, source_target_pairs={{0,2},{1,3},{2,0},{3,1},{4,6},{5,7},{6,4},{7,5},{8,10},{9,11},{10,... | collective-permute-start | bytes 1178504 | tf_op jit(solution)/shard_map/ppermute | solution.py:80
  75.2 34.3 %collective-permute-start.2 = (bf16[144,1364]{1,0:T(8,128)(2,1)}, bf16[144,1364]{1,0:T(8,128)(2,1)S(1)}, u32[]{:S(2)}, u32[]{:S(2)}) collective-permute-start(bf16[144,1364]{1,0:T(8,128)(2,1)} %copy_after.2), channel_id=1, source_target_pairs={{0,1},{1,2},{2,3},{3,0},{4,5},{5,6},{6,7},{7,4},{8,9},{9,10},{10,1... | collective-permute-start | bytes 1178504 | tf_op jit(solution)/shard_map/ppermute | solution.py:80
  82.3 28.6 %copy-start.24 = (bf16[144,1364]{1,0:T(8,128)(2,1)}, bf16[144,1364]{1,0:T(8,128)(2,1)S(1)}, u32[]{:S(2)}) copy-start(bf16[144,1364]{1,0:T(8,128)(2,1)S(1)} %collective-permute-done.4.refs_3_) | copy-start | bytes 1178500
  114.2 140.6 %all-gather.11.cloned.1.call-start = ((), (), s32[]{:S(2)}) async-start(), calls=%async_computation.6 | async-start | bytes 11280384 | tf_op jit(solution)/shard_map/all_gather | solution.py:510
  114.3 29.2 %collective-permute-start.5 = (bf16[512,1152]{1,0:T(8,128)(2,1)}, bf16[512,1152]{1,0:T(8,128)(2,1)S(1)}, u32[]{:S(2)}, u32[]{:S(2)}) collective-permute-start(bf16[512,1152]{1,0:T(8,128)(2,1)} %after.26.x_ref), channel_id=1, source_target_pairs={{1,0},{2,1},{3,2},{5,4},{6,5},{7,6},{9,8},{10,9},{11,10},{13,12},{... | collective-permute-start | bytes 3538952 | tf_op jit(solution)/shard_map/ppermute | solution.py:452
  115.6 29.2 %collective-permute-start.6 = (bf16[512,1152]{1,0:T(8,128)(2,1)}, bf16[512,1152]{1,0:T(8,128)(2,1)S(1)}, u32[]{:S(2)}, u32[]{:S(2)}) collective-permute-start(bf16[512,1152]{1,0:T(8,128)(2,1)} %after.27.x_ref), channel_id=1, source_target_pairs={{0,1},{1,2},{2,3},{4,5},{5,6},{6,7},{8,9},{9,10},{10,11},{12,13},{... | collective-permute-start | bytes 3538952 | tf_op jit(solution)/shard_map/ppermute | solution.py:453
  156.8 27.5 %collective-permute-start.9 = (bf16[144,1076]{1,0:T(8,128)(2,1)}, bf16[144,1076]{1,0:T(8,128)(2,1)S(1)}, u32[]{:S(2)}, u32[]{:S(2)}) collective-permute-start(bf16[144,1076]{1,0:T(8,128)(2,1)} %copy_after.3), channel_id=1, source_target_pairs={{0,3},{1,0},{2,1},{3,2},{4,7},{5,4},{6,5},{7,6},{8,11},{9,8},{10,9... | collective-permute-start | bytes 929672 | tf_op jit(solution)/shard_map/ppermute | solution.py:80
  160.5 27.5 %collective-permute-start.8 = (bf16[144,1076]{1,0:T(8,128)(2,1)}, bf16[144,1076]{1,0:T(8,128)(2,1)S(1)}, u32[]{:S(2)}, u32[]{:S(2)}) collective-permute-start(bf16[144,1076]{1,0:T(8,128)(2,1)} %copy_after.3), channel_id=1, source_target_pairs={{0,2},{1,3},{2,0},{3,1},{4,6},{5,7},{6,4},{7,5},{8,10},{9,11},{10,... | collective-permute-start | bytes 929672 | tf_op jit(solution)/shard_map/ppermute | solution.py:80
  160.7 28.2 %collective-permute-start.7 = (bf16[144,1076]{1,0:T(8,128)(2,1)}, bf16[144,1076]{1,0:T(8,128)(2,1)S(1)}, u32[]{:S(2)}, u32[]{:S(2)}) collective-permute-start(bf16[144,1076]{1,0:T(8,128)(2,1)} %copy_after.3), channel_id=1, source_target_pairs={{0,1},{1,2},{2,3},{3,0},{4,5},{5,6},{6,7},{7,4},{8,9},{9,10},{10,1... | collective-permute-start | bytes 929672 | tf_op jit(solution)/shard_map/ppermute | solution.py:80
  193.4 144.1 %reduce-scatter.5.cloned.1.call-start = ((), (), s32[]{:S(2)}) async-start(), calls=%async_computation.7 | async-start | bytes 11280384 | tf_op jit(solution)/shard_map/reduce_scatter | solution.py:536
  195.2 29.9 %copy-start.4 = (bf16[1,512,1152]{2,1,0:T(8,128)(2,1)S(1)}, bf16[1,512,1152]{2,1,0:T(8,128)(2,1)}, u32[]{:S(2)}) copy-start(bf16[1,512,1152]{2,1,0:T(8,128)(2,1)} %param.20) | copy-start | bytes 3538948
  251.3 169.3 %reduce-scatter.9.cloned.1.call-start = ((), (), s32[]{:S(2)}) async-start(), calls=%async_computation.9 | async-start | bytes 11280384 | tf_op jit(solution)/shard_map/reduce_scatter | solution.py:549
  254.8 16.0 %copy-start.13 = (f32[512,1152]{1,0:T(8,128)S(1)}, f32[512,1152]{1,0:T(8,128)}, u32[]{:S(2)}) copy-start(f32[512,1152]{1,0:T(8,128)} %copy-done.12) | copy-start | bytes 7077892
  279.5 229.7 %reduce-scatter.7.cloned.1.call-start = ((), (), s32[]{:S(2)}) async-start(), calls=%async_computation.8 | async-start | bytes 11943936 | tf_op jit(solution)/shard_map/reduce_scatter | solution.py:640
  337.5 47.0 %slice-start = ((s8[4718592]{0:T(1024)(128)(4,1)}), s8[4194304]{0:T(1024)(128)(4,1)S(1)}, s32[]{:S(2)}) async-start(s8[4718592]{0:T(1024)(128)(4,1)} %bitcast.142), calls=%async_computation.12 | async-start | bytes 8388608
  339.3 48.4 %collective-permute-start.12 = (bf16[144,1076]{1,0:T(8,128)(2,1)S(1)}, bf16[144,1076]{1,0:T(8,128)(2,1)S(1)}, u32[]{:S(2)}, u32[]{:S(2)}) collective-permute-start(bf16[144,1076]{1,0:T(8,128)(2,1)S(1)} %get-tuple-element.55), channel_id=1, source_target_pairs={{0,1},{1,2},{2,3},{3,0},{4,5},{5,6},{6,7},{7,4},{8,9},{9,10},{10,1... | collective-permute-start | bytes 929672 | tf_op jit(solution)/shard_map/ppermute | solution.py:593
  340.8 47.6 %collective-permute-start.11 = (bf16[144,1076]{1,0:T(8,128)(2,1)S(1)}, bf16[144,1076]{1,0:T(8,128)(2,1)S(1)}, u32[]{:S(2)}, u32[]{:S(2)}) collective-permute-start(bf16[144,1076]{1,0:T(8,128)(2,1)S(1)} %get-tuple-element.56), channel_id=1, source_target_pairs={{0,2},{1,3},{2,0},{3,1},{4,6},{5,7},{6,4},{7,5},{8,10},{9,11},{10,... | collective-permute-start | bytes 929672 | tf_op jit(solution)/shard_map/ppermute | solution.py:593
  343.2 46.0 %collective-permute-start.10 = (bf16[144,1076]{1,0:T(8,128)(2,1)S(1)}, bf16[144,1076]{1,0:T(8,128)(2,1)S(1)}, u32[]{:S(2)}, u32[]{:S(2)}) collective-permute-start(bf16[144,1076]{1,0:T(8,128)(2,1)S(1)} %get-tuple-element.57), channel_id=1, source_target_pairs={{0,3},{1,0},{2,1},{3,2},{4,7},{5,4},{6,5},{7,6},{8,11},{9,8},{10,9... | collective-permute-start | bytes 929672 | tf_op jit(solution)/shard_map/ppermute | solution.py:593
  344.7 39.8 %slice-start.1 = ((s8[4718592]{0:T(1024)(128)(4,1)}), s8[524288]{0:T(1024)(128)(4,1)S(1)}, s32[]{:S(2)}) async-start(s8[4718592]{0:T(1024)(128)(4,1)} %bitcast.142), calls=%async_computation.13 | async-start | bytes 1048576
  377.6 28.4 %collective-permute-start.14 = (bf16[512,1152]{1,0:T(8,128)(2,1)S(1)}, bf16[512,1152]{1,0:T(8,128)(2,1)S(1)}, u32[]{:S(2)}, u32[]{:S(2)}) collective-permute-start(bf16[512,1152]{1,0:T(8,128)(2,1)S(1)} %get-tuple-element.58.refs_2_), channel_id=1, source_target_pairs={{1,0},{2,1},{3,2},{5,4},{6,5},{7,6},{9,8},{10,9},{11,10},{13,12},{... | collective-permute-start | bytes 3538952 | tf_op jit(solution)/shard_map/ppermute | solution.py:629
  378.9 28.3 %collective-permute-start.13 = (bf16[512,1152]{1,0:T(8,128)(2,1)S(1)}, bf16[512,1152]{1,0:T(8,128)(2,1)}, u32[]{:S(2)}, u32[]{:S(2)}) collective-permute-start(bf16[512,1152]{1,0:T(8,128)(2,1)S(1)} %get-tuple-element.59.refs_1_), channel_id=1, source_target_pairs={{0,1},{1,2},{2,3},{4,5},{5,6},{6,7},{8,9},{9,10},{10,11},{12,13},{... | collective-permute-start | bytes 3538952 | tf_op jit(solution)/shard_map/ppermute | solution.py:628
  416.0 134.6 %reduce-scatter.11.cloned.1.call-start = ((), (), s32[]{:S(2)}) async-start(), calls=%async_computation.10 | async-start | bytes 1658880 | tf_op jit(solution)/shard_map/reduce_scatter | solution.py:705
  423.0 18.6 %collective-permute-start.16 = (bf16[144,1076]{1,0:T(8,128)(2,1)S(1)}, bf16[144,1076]{1,0:T(8,128)(2,1)S(1)}, u32[]{:S(2)}, u32[]{:S(2)}) collective-permute-start(bf16[144,1076]{1,0:T(8,128)(2,1)S(1)} %get-tuple-element.53), channel_id=1, source_target_pairs={{0,2},{1,3},{2,0},{3,1},{4,6},{5,7},{6,4},{7,5},{8,10},{9,11},{10,... | collective-permute-start | bytes 929672 | tf_op jit(solution)/shard_map/ppermute | solution.py:643
  425.4 17.0 %collective-permute-start.15 = (bf16[144,1076]{1,0:T(8,128)(2,1)S(1)}, bf16[144,1076]{1,0:T(8,128)(2,1)S(1)}, u32[]{:S(2)}, u32[]{:S(2)}) collective-permute-start(bf16[144,1076]{1,0:T(8,128)(2,1)S(1)} %get-tuple-element.54), channel_id=1, source_target_pairs={{0,3},{1,0},{2,1},{3,2},{4,7},{5,4},{6,5},{7,6},{8,11},{9,8},{10,9... | collective-permute-start | bytes 929672 | tf_op jit(solution)/shard_map/ppermute | solution.py:643
  435.0 42.9 %collective-permute-start.18 = (bf16[512,1152]{1,0:T(8,128)(2,1)S(1)}, bf16[512,1152]{1,0:T(8,128)(2,1)}, u32[]{:S(2)}, u32[]{:S(2)}) collective-permute-start(bf16[512,1152]{1,0:T(8,128)(2,1)S(1)} %add_convert_fusion.2.refs_1_), channel_id=1, source_target_pairs={{0,1},{1,2},{2,3},{4,5},{5,6},{6,7},{8,9},{9,10},{10,11},{12,13},{... | collective-permute-start | bytes 3538952 | tf_op jit(solution)/shard_map/ppermute | solution.py:658
  464.9 34.6 %collective-permute-start.19 = (bf16[512,1152]{1,0:T(8,128)(2,1)}, bf16[512,1152]{1,0:T(8,128)(2,1)}, u32[]{:S(2)}, u32[]{:S(2)}) collective-permute-start(bf16[512,1152]{1,0:T(8,128)(2,1)} %get-tuple-element.111), channel_id=1, source_target_pairs={{1,0},{2,1},{3,2},{5,4},{6,5},{7,6},{9,8},{10,9},{11,10},{13,12},{... | collective-permute-start | bytes 3538952 | tf_op jit(solution)/shard_map/ppermute | solution.py:664
  470.8 38.4 %collective-permute-start.17 = (bf16[144,1076]{1,0:T(8,128)(2,1)}, bf16[144,1076]{1,0:T(8,128)(2,1)}, u32[]{:S(2)}, u32[]{:S(2)}) collective-permute-start(bf16[144,1076]{1,0:T(8,128)(2,1)} %get-tuple-element.52), channel_id=1, source_target_pairs={{0,1},{1,2},{2,3},{3,0},{4,5},{5,6},{6,7},{7,4},{8,9},{9,10},{10,1... | collective-permute-start | bytes 929672 | tf_op jit(solution)/shard_map/ppermute | solution.py:643
  478.1 21.5 %copy-start.7 = (f32[512,1152]{1,0:T(8,128)S(1)}, f32[512,1152]{1,0:T(8,128)}, u32[]{:S(2)}) copy-start(f32[512,1152]{1,0:T(8,128)} %fusion.22.refs_1_) | copy-start | bytes 7077892
  478.1 21.4 %copy-start.53 = (f32[1152]{0:T(1024)S(1)}, f32[1152]{0:T(1024)}, u32[]{:S(2)}) copy-start(f32[1152]{0:T(1024)} %get-tuple-element.38) | copy-start | bytes 13828
  478.1 21.4 %copy-start.59 = (f32[512]{0:T(512)S(1)}, f32[512]{0:T(512)}, u32[]{:S(2)}) copy-start(f32[512]{0:T(512)} %copy-done.58) | copy-start | bytes 6148
  478.1 21.4 %copy-start.64 = (f32[512]{0:T(512)S(1)}, f32[512]{0:T(512)}, u32[]{:S(2)}) copy-start(f32[512]{0:T(512)} %add_rsqrt_fusion) | copy-start | bytes 6148
  512.1 14.9 %copy-start.60 = (f32[512]{0:T(512)S(1)}, f32[512]{0:T(512)}, u32[]{:S(2)}) copy-start(f32[512]{0:T(512)} %copy-done.58) | copy-start | bytes 6148
  512.1 14.9 %copy-start.65 = (f32[512]{0:T(512)S(1)}, f32[512]{0:T(512)}, u32[]{:S(2)}) copy-start(f32[512]{0:T(512)} %add_rsqrt_fusion) | copy-start | bytes 6148
  512.1 4.4 collective-permute-start.20
  518.0 5.4 collective-permute-start.21
  524.3 1.3 collective-permute-start.22
  525.6 5.2 collective-permute-start.23
  530.8 13.3 %collective-permute-start.24 = (f32[13520]{0:T(1024)S(1)}, f32[13520]{0:T(1024)S(1)}, u32[]{:S(2)}, u32[]{:S(2)}) collective-permute-start(f32[13520]{0:T(1024)S(1)} %add.323), channel_id=1, source_target_pairs={{0,16},{4,20},{8,24},{12,28},{16,0},{20,4},{24,8},{28,12},{1,17},{... | collective-permute-start | bytes 162248 | tf_op jit(solution)/shard_map/ppermute | solution.py:693
  (66 other events, 316.7 us)
Sparse Core Ops, SparseCore 0:
  18.7 41.3 all-gather.12
  64.2 52.4 all-gather.6
  119.1 72.5 all-gather.8
  193.6 61.1 all-gather.10
  258.3 79.2 reduce-scatter.4
  341.4 79.1 reduce-scatter.8
  424.1 82.2 reduce-scatter.6
  519.4 31.1 reduce-scatter.10

commit v6 on v5

--- a/solution.py
+++ b/solution.py
@@ -496,7 +496,7 @@
         (product("td,dc->ct", normed, query_full) + query_shift[:, None])
         * (scale * math.log2(math.e))
     ).astype(BF)
-    first_down = copy_after(down_weight[0], later[-1], prior[-1], queries)
+    first_down = copy_after(down_weight[0], later[-1], prior[-1])
     q_rest = jnp.zeros((AUG - (pics + 1), here), F32)
     q_aug = widen(queries, jnp.concatenate([q_mask, q_rest], axis=0))
 

time: 569 us -> 568 us (level)
    unnamed x163 -> x179, local copies, waits for them, and re-layouts: 22.2 us -> 24.7 us
  transfers between devices with their start and end apart: 33 -> 33, of which waited for: 19 -> 18; matrix products, arithmetic and copies ran while one was open for 44% -> 45% of each run, Pallas kernels for 18% -> 18%
where the time goes in v6:
time: 568 us; the launch traced here: 560 us
  matrix products  151 us (27%)
  Pallas kernels  104 us (18%)
  waiting for transfers between devices  95.9 us (17%)
  other arithmetic  67.1 us (12%)
  local copies, waits for them, and re-layouts  64.3 us (11%)
  starting transfers between devices  51.4 us (9%)
  between operations  17.1 us (3%)
  blocking collectives  9.37 us (2%)
    dot_general x19, matrix products, product(): return jnp.einsum(form, left, right, preferred_element_type=F32)  151 us
    pallas_call x2, Pallas kernels, attend_back(): pl.pallas_call(functools.partial(attend_back_kernel, q_block=q_block, k_b...  52 us
    ppermute x6, waiting for transfers between devices, slots_along_tp(): lax.ppermute(piece, 'tp', [(i, (i + distance) % count) for i in range(cou...  32.1 us
    pallas_call x1, Pallas kernels, attend(): pl.pallas_call(functools.partial(attend_kernel, q_block=q_block, k_block=...  30 us
    unnamed x179, local copies, waits for them, and re-layouts  24.7 us
    ppermute x1, waiting for transfers between devices, local(): moving_left = lax.ppermute(joined(moving_left, to_prior[1]), 'tp', to_left)  18.1 us
    pallas_call x4, Pallas kernels, norm_slot(): pl.pallas_call(norm_kernel, grid=(steps,), in_specs=[pl.BlockSpec((block,...  16 us
  transfers between devices with their start and end apart: 33, of which 18 were waited for; matrix products, arithmetic and copies ran while one was open for 45% of the time, Pallas kernels for 18%

profile of v6, /device:TPU:0, one launch (start us, length us, event | category | flops | bytes accessed | tf_op | source)
XLA Modules:
  0.0 560.0 jit_solution(11512828708010529993)
XLA Ops:
  7.2 5.1 collective-permute-start.1
  37.7 9.4 %all-gather.1 = f32[8,144,6]{1,2,0:T(8,128)S(1)} all-gather(f32[1,144,6]{1,2,0:T(8,128)} %bitcast.172), channel_id=1, replica_groups=mesh['fsdp'=8,'tp'=4] {'fsdp'}, dimensions={0}, use_global_device_ids=true | all-gather | bytes 31104 | tf_op jit(solution)/shard_map/all_gather | solution.py:365
  54.0 5.2 collective-permute-done.refs_8_.refs_0_
  77.4 5.0 collective-permute-done.4.refs_3_
  82.4 27.1 %collective-permute-done.3.refs_2_ = bf16[144,1364]{1,0:T(8,128)(2,1)S(1)} collective-permute-done((bf16[144,1364]{1,0:T(8,128)(2,1)}, bf16[144,1364]{1,0:T(8,128)(2,1)S(1)}, u32[]{:S(2)}, u32[]{:S(2)}) %collective-permute-start.3) | collective-permute-done | bytes 392864 | tf_op jit(solution)/shard_map/ppermute | solution.py:80
  111.0 3.2 concatenate.145
  115.6 4.6 collective-permute-start.6
  121.5 3.9 norm_slot.4.rest_0_
  125.4 4.0 norm_slot.5.rest_0_
  129.5 4.0 norm_slot.6.rest_0_
  133.4 10.1 %collective-permute-done.5.refs_0_ = bf16[512,1152]{1,0:T(8,128)(2,1)S(1)} collective-permute-done((bf16[512,1152]{1,0:T(8,128)(2,1)}, bf16[512,1152]{1,0:T(8,128)(2,1)S(1)}, u32[]{:S(2)}, u32[]{:S(2)}) %collective-permute-start.5) | collective-permute-done | bytes 1179680 | tf_op jit(solution)/shard_map/ppermute | solution.py:452
  147.6 3.7 collective-permute-start.9
  155.1 4.1 norm_slot.7
  159.2 9.2 %add_convert_fusion = bf16[1152,2048]{1,0:T(8,128)(2,1)S(1)} fusion(bf16[2048,1152]{1,0:T(8,128)(2,1)} %norm_slot.7, f32[1152]{0:T(1024)S(1)} %copy-done.53, bf16[1152,3456]{1,0:T(8,128)(2,1)} %all-gather.7.cloned.1.call-done), kind=kOutput, calls=%fused_computation.10 | convolution fusion | flops 5440536576 | bytes 12096000 | tf_op jit(solution)/shard_map/td,dc->ct/dot_general | solution.py:37
  172.9 8.5 %convolution_convert_fusion.5 = bf16[1152,2048]{1,0:T(8,128)(2,1)S(1)} fusion(bf16[2048,1152]{1,0:T(8,128)(2,1)S(1)} %bitcast.143, bf16[1152,3456]{1,0:T(8,128)(2,1)} %all-gather.7.cloned.1.call-done), kind=kOutput, calls=%fused_computation.27 | convolution fusion | flops 5438177280 | bytes 12091392 | tf_op jit(solution)/shard_map/td,dc->ct/dot_general | solution.py:37
  187.0 3.2 concatenate.144.rest_0_
  190.6 3.8 fusion.29
  195.8 30.0 %attend.1 = (bf16[16,72,512]{2,1,0:T(8,128)(2,1)}, f32[16,1,512]{2,1,0:T(1,128)}) custom-call(s32[1]{0:T(128)S(6)} %neg.49.refs_2_.count_ref, s32[8]{0:T(128)} %select_reduce_fusion.refs_3_.index_ref, bf16[16,80,512]{2,1,0:T(8,128)(2,1)} %pad_maximum_fusion.3.q_ref, bf16[16,80,2048]{2,1,0:T(8,128)(2,1)} %after.28.refs_1_.k_ref, ...), custom_call_target="tpu_custom_call" | custom-call | flops 5368709120 | bytes 13107200 | tf_op jit(solution)/shard_map/attend/pallas_call | solution.py:191
  225.9 4.2 fusion.104
  232.6 9.1 %multiply_convert_fusion = (bf16[512,4304]{1,0:T(8,128)(2,1)S(1)}, f32[512,4304]{1,0:T(8,128)}) fusion(f32[4304]{0:T(1024)S(1)} %copy-done.45, bf16[1152,5456]{1,0:T(8,128)(2,1)S(1)} %copy-done.83, f32[512,1152]{1,0:T(8,128)S(1)} %get-tuple-element.107, f32[1152]{0:T(1024)S(1)} %copy-done.71, f32[1152]{0:T(1024)S(1)} %get-tuple-element.41, ...), kind=kOutput, calls=%fused_computation.19 | convolution fusion | flops 5102190592 | bytes 25649152 | tf_op jit(solution)/shard_map/td,df->tf/dot_general | solution.py:37
  243.8 8.3 %convolution_convert_fusion.1.refs_1_ = bf16[1152,4304]{1,0:T(8,128)(2,1)} fusion(bf16[512,1152]{1,0:T(8,128)(2,1)S(1)} %copy-done.9, bf16[512,4304]{1,0:T(8,128)(2,1)S(1)} %get-tuple-element.108.refs_0_), kind=kOutput, calls=%fused_computation.4 | convolution fusion | flops 5082163200 | bytes 15503360 | tf_op jit(solution)/shard_map/td,tf->df/dot_general | solution.py:37
  254.9 14.1 %convert_reduce_fusion.1 = (f32[4304]{0:T(1024)}, bf16[512,4304]{1,0:T(8,128)(2,1)S(1)}) fusion(f32[512,4304]{1,0:T(8,128)} %get-tuple-element.109, bf16[512,1152]{1,0:T(8,128)(2,1)} %after.33, bf16[1152,4304]{1,0:T(8,128)(2,1)} %all-gather.11.cloned.1.call-done), kind=kOutput, calls=%fused_computation.18 | convolution fusion | flops 5125681152 | bytes 24335168 | tf_op jit(solution)/shard_map/td,df->tf/dot_general | solution.py:37
  271.5 8.7 %convolution_convert_fusion.rest_0_ = bf16[1152,4304]{1,0:T(8,128)(2,1)} fusion(bf16[512,4304]{1,0:T(8,128)(2,1)S(1)} %get-tuple-element.46, f32[512,1152]{1,0:T(8,128)S(1)} %get-tuple-element.107, f32[1152]{0:T(1024)S(1)} %copy-done.72, f32[1152]{0:T(1024)S(1)} %get-tuple-element.41, f32[512]{0:T(512)S(1)} %copy-done.74, f32[512]{0:T(512)S(1)} %broadcast_multiply_fusion.5), kind=kOutput, calls=%fused_computation.3 | convolution fusion | flops 5085112320 | bytes 16696320 | tf_op jit(solution)/shard_map/td,tf->df/dot_general | solution.py:37
  283.4 13.0 %multiply_reduce_fusion = (f32[1152]{0:T(1024)}, f32[512]{0:T(512)S(1)}, f32[512]{0:T(512)S(1)}, f32[1152]{0:T(1024)}, f32[512,1152]{1,0:T(8,128)S(1)}) fusion(f32[512,1152]{1,0:T(8,128)S(1)} %get-tuple-element.107, f32[512]{0:T(512)} %copy-done.73, f32[512]{0:T(512)S(1)} %copy-done.61, f32[1152]{0:T(1024)S(1)} %get-tuple-element.41, ...), kind=kOutput, calls=%fused_computation.82 | convolution fusion | flops 5082510336 | bytes 19224064 | tf_op jit(solution)/shard_map/tf,df->td/dot_general | solution.py:37
  298.7 4.4 fusion.39
  304.9 3.3 convolution_convert_fusion.4.rest_1_.refs_0_
  308.2 25.7 %attend_back.2 = (bf16[16,72,512]{2,1,0:T(8,128)(2,1)}, bf16[2,16,72,2048]{3,2,1,0:T(8,128)(2,1)}) custom-call(s32[1]{0:T(128)S(6)} %neg.49.refs_2_.count_ref, s32[8]{0:T(128)} %select_reduce_fusion.refs_3_.index_ref, bf16[16,80,512]{2,1,0:T(8,128)(2,1)} %maximum_maximum_fusion.q_ref, bf16[16,80,2048]{2,1,0:T(8,128)(2,1)} %after.28.refs_1_.k_ref, ...), custom_call_target="tpu_custom_call" | custom-call | flops 13421772800 | bytes 26214400 | tf_op jit(solution)/shard_map/attend_back/pallas_call | solution.py:287
  333.9 3.7 reduce-scatter.5.cloned.1.call-done.refs_0_
  344.8 26.3 %attend_back.3 = (bf16[16,72,512]{2,1,0:T(8,128)(2,1)}, bf16[2,16,72,2048]{3,2,1,0:T(8,128)(2,1)}) custom-call(s32[1]{0:T(128)S(6)} %neg.49.refs_2_.count_ref, s32[8]{0:T(128)} %select_reduce_fusion.refs_3_.index_ref, bf16[16,80,512]{2,1,0:T(8,128)(2,1)} %maximum_maximum_fusion.q_ref, ...), custom_call_target="tpu_custom_call", output_to_operand_aliasing={{0}: (6, {}), {1}: (7, {})} | custom-call | flops 13421772800 | bytes 26214400 | tf_op jit(solution)/shard_map/attend_back/pallas_call | solution.py:287
  371.1 6.6 %broadcast_select_fusion = (bf16[512,1152]{1,0:T(8,128)(2,1)S(1)}, bf16[512,1152]{1,0:T(8,128)(2,1)S(1)}) fusion(pred[]{:T(512)S(6)} %ge.49, pred[]{:T(512)S(6)} %lt.90, bf16[1152,3456]{1,0:T(8,128)(2,1)} %all-gather.7.cloned.1.call-done, bf16[2304,2048]{1,0:T(8,128)(2,1)} %bitcast.140), kind=kOutput, calls=%fused_computation.104 | convolution fusion | flops 2719678464 | bytes 10027010 | tf_op jit(solution)/shard_map/ct,dc->td/dot_general | solution.py:37
  379.0 5.6 %collective-permute-start.13 = (bf16[512,1152]{1,0:T(8,128)(2,1)S(1)}, bf16[512,1152]{1,0:T(8,128)(2,1)}, u32[]{:S(2)}, u32[]{:S(2)}) collective-permute-start(bf16[512,1152]{1,0:T(8,128)(2,1)S(1)} %get-tuple-element.59.refs_1_), channel_id=1, source_target_pairs={{0,1},{1,2},{2,3},{4,5},{5,6},{6,7},{8,9},{9,10},{10,11},{12,13},{... | collective-permute-start | bytes 3538952 | tf_op jit(solution)/shard_map/ppermute | solution.py:628
  384.6 3.2 convolution_convert_fusion.3.refs_2_
  390.1 15.1 %convolution_convert_fusion.2.refs_1_ = bf16[1152,2304]{1,0:T(8,128)(2,1)} fusion(bf16[2048,1152]{1,0:T(8,128)(2,1)S(1)} %bitcast.145, bf16[2304,2048]{1,0:T(8,128)(2,1)} %after.38.refs_0_), kind=kOutput, calls=%fused_computation.7 | convolution fusion | flops 10874290176 | bytes 19464192 | tf_op jit(solution)/shard_map/td,ct->dc/dot_general | solution.py:37
  409.8 6.3 %pad_maximum_fusion.refs_1_ = bf16[1152,4608]{1,0:T(8,128)(2,1)} fusion(bf16[1152,1152]{1,0:T(8,128)(2,1)} %after.39, bf16[1152,2304]{1,0:T(8,128)(2,1)S(1)} %copy-done, bf16[1152,1152]{1,0:T(8,128)(2,1)S(1)} %copy-done.5), kind=kLoop, calls=%fused_computation.8 | loop fusion | flops 31850496 | bytes 21233664 | tf_op jit(solution)/shard_map/concatenate | solution.py:639
  427.3 7.7 %add_convert_fusion.2.refs_1_ = bf16[512,1152]{1,0:T(8,128)(2,1)S(1)} fusion(bf16[512,1152]{1,0:T(8,128)(2,1)} %collective-permute-done.13.refs_3_, bf16[1152,3456]{1,0:T(8,128)(2,1)} %all-gather.7.cloned.1.call-done, bf16[2304,2048]{1,0:T(8,128)(2,1)} %after.41.refs_0_, pred[]{:T(512)S(6)} %lt.81), kind=kOutput, calls=%fused_computation.87 | convolution fusion | flops 2721447936 | bytes 10027009 | tf_op jit(solution)/shard_map/ct,dc->td/dot_general | solution.py:37
  437.6 4.1 collective-permute-done.16.refs_2_.refs_4_
  443.8 3.6 fusion.73
  447.5 7.9 %fusion.22.refs_1_ = f32[512,1152]{1,0:T(8,128)} fusion(f32[512,1152]{1,0:T(8,128)S(1)} %fusion.73, bf16[1152,3456]{1,0:T(8,128)(2,1)} %all-gather.7.cloned.1.call-done, bf16[2304,2048]{1,0:T(8,128)(2,1)} %after.43.refs_0_), kind=kOutput, calls=%fused_computation.41 | convolution fusion | flops 2718498816 | bytes 12386304 | tf_op jit(solution)/shard_map/ct,dc->td/dot_general | solution.py:37
  456.7 8.3 %add_convert_fusion.1 = (bf16[512,1152]{1,0:T(8,128)(2,1)}, bf16[512,1152]{1,0:T(8,128)(2,1)}) fusion(bf16[512,1152]{1,0:T(8,128)(2,1)S(1)} %copy-done.40, bf16[1152,3456]{1,0:T(8,128)(2,1)} %all-gather.7.cloned.1.call-done, bf16[2304,2048]{1,0:T(8,128)(2,1)} %after.45, pred[]{:T(512)S(6)} %ge.50), kind=kOutput, calls=%fused_computation.86 | convolution fusion | flops 2721447936 | bytes 11206657 | tf_op jit(solution)/shard_map/ct,dc->td/dot_general | solution.py:37
  470.8 7.0 %collective-permute-start.17 = (bf16[144,1076]{1,0:T(8,128)(2,1)}, bf16[144,1076]{1,0:T(8,128)(2,1)}, u32[]{:S(2)}, u32[]{:S(2)}) collective-permute-start(bf16[144,1076]{1,0:T(8,128)(2,1)} %get-tuple-element.52), channel_id=1, source_target_pairs={{0,1},{1,2},{2,3},{3,0},{4,5},{5,6},{6,7},{7,4},{8,9},{9,10},{10,1... | collective-permute-start | bytes 929672 | tf_op jit(solution)/shard_map/ppermute | solution.py:643
  478.2 3.3 convert_reduce_fusion
  481.4 18.1 %collective-permute-done.19 = bf16[512,1152]{1,0:T(8,128)(2,1)} collective-permute-done((bf16[512,1152]{1,0:T(8,128)(2,1)}, bf16[512,1152]{1,0:T(8,128)(2,1)}, u32[]{:S(2)}, u32[]{:S(2)}) %collective-permute-start.19) | collective-permute-done | bytes 1179680 | tf_op jit(solution)/shard_map/ppermute | solution.py:664
  499.6 4.7 fusion.63
  505.0 4.3 collective-permute-done.17.refs_5_
  519.2 4.2 collective-permute-done.21
  527.0 3.9 fusion.62
  532.5 11.6 %fusion.54 = bf16[1,512,1152]{2,1,0:T(8,128)(2,1)} fusion(f32[512,1152]{1,0:T(8,128)S(1)} %copy-done.11, bf16[512,4304]{1,0:T(8,128)(2,1)} %after.47, bf16[1152,4304]{1,0:T(8,128)(2,1)} %all-gather.11.cloned.1.call-done, f32[1152]{0:T(1024)S(1)} %copy-done.68, f32[512]{0:T(512)S(1)} %copy-done.64), kind=kOutput, calls=%fused_computation.63 | convolution fusion | flops 5079564288 | bytes 17869312 | tf_op jit(solution)/shard_map/tf,df->td/dot_general | solution.py:37
  546.8 3.8 reduce-scatter.11.cloned.1.call-done
  (399 shorter events, 149.0 us)
Async XLA Ops:
  7.2 44.1 %copy-start.17 = (bf16[1,512,1152]{2,1,0:T(8,128)(2,1)S(1)}, bf16[1,512,1152]{2,1,0:T(8,128)(2,1)}, u32[]{:S(2)}) copy-start(bf16[1,512,1152]{2,1,0:T(8,128)(2,1)} %param.22) | copy-start | bytes 3538948
  7.2 52.8 %all-gather.13.cloned.1.call-start = ((), (), s32[]{:S(2)}) async-start(), calls=%async_computation.11 | async-start | bytes 1361920 | tf_op jit(solution)/shard_map/all_gather | solution.py:363
  7.2 46.7 %collective-permute-start.1 = (bf16[512,1152]{1,0:T(8,128)(2,1)}, bf16[512,1152]{1,0:T(8,128)(2,1)S(1)}, u32[]{:S(2)}, u32[]{:S(2)}) collective-permute-start(bf16[512,1152]{1,0:T(8,128)(2,1)} %bitcast.148), channel_id=1, source_target_pairs={{0,1},{1,2},{2,3},{4,5},{5,6},{6,7},{8,9},{9,10},{10,11},{12,13},{... | collective-permute-start | bytes 3538952 | tf_op jit(solution)/shard_map/ppermute | solution.py:421
  12.4 46.8 %collective-permute-start = (bf16[512,1152]{1,0:T(8,128)(2,1)}, bf16[512,1152]{1,0:T(8,128)(2,1)S(1)}, u32[]{:S(2)}, u32[]{:S(2)}) collective-permute-start(bf16[512,1152]{1,0:T(8,128)(2,1)} %bitcast.149), channel_id=1, source_target_pairs={{1,0},{2,1},{3,2},{5,4},{6,5},{7,6},{9,8},{10,9},{11,10},{13,12},{... | collective-permute-start | bytes 3538952 | tf_op jit(solution)/shard_map/ppermute | solution.py:420
  18.6 140.6 %all-gather.7.cloned.1.call-start = ((), (), s32[]{:S(2)}) async-start(), calls=%async_computation.4 | async-start | bytes 8957952 | tf_op jit(solution)/shard_map/all_gather | solution.py:480
  29.3 31.0 %copy-start.48 = (f32[3,512]{1,0:T(4,128)}, f32[3,512]{1,0:T(4,128)S(1)}, u32[]{:S(2)}) copy-start(f32[3,512]{1,0:T(4,128)S(1)} %get-tuple-element.104) | copy-start | bytes 18436
  64.2 161.7 %all-gather.9.cloned.1.call-start = ((), (), s32[]{:S(2)}) async-start(), calls=%async_computation.5 | async-start | bytes 14266368 | tf_op jit(solution)/shard_map/all_gather | solution.py:485
  64.3 46.5 %copy-start.77 = (pred[4]{0:T(512)(128)(4,1)}, pred[4]{0:T(512)(128)(4,1)S(1)}, u32[]{:S(2)}) copy-start(pred[4]{0:T(512)(128)(4,1)S(1)} %compare_and_fusion) | copy-start | bytes 16
  64.3 18.0 %copy-start.76 = (s32[1024]{0:T(1024)}, s32[1024]{0:T(1024)S(1)}, u32[]{:S(2)}) copy-start(s32[1024]{0:T(1024)S(1)} %pad_clamp_fusion.1) | copy-start | bytes 12292
  71.1 11.3 %collective-permute-start.4 = (bf16[144,1364]{1,0:T(8,128)(2,1)}, bf16[144,1364]{1,0:T(8,128)(2,1)S(1)}, u32[]{:S(2)}, u32[]{:S(2)}) collective-permute-start(bf16[144,1364]{1,0:T(8,128)(2,1)} %copy_after.2), channel_id=1, source_target_pairs={{0,3},{1,0},{2,1},{3,2},{4,7},{5,4},{6,5},{7,6},{8,11},{9,8},{10,9... | collective-permute-start | bytes 1178504 | tf_op jit(solution)/shard_map/ppermute | solution.py:80
  73.2 36.3 %collective-permute-start.3 = (bf16[144,1364]{1,0:T(8,128)(2,1)}, bf16[144,1364]{1,0:T(8,128)(2,1)S(1)}, u32[]{:S(2)}, u32[]{:S(2)}) collective-permute-start(bf16[144,1364]{1,0:T(8,128)(2,1)} %copy_after.2), channel_id=1, source_target_pairs={{0,2},{1,3},{2,0},{3,1},{4,6},{5,7},{6,4},{7,5},{8,10},{9,11},{10,... | collective-permute-start | bytes 1178504 | tf_op jit(solution)/shard_map/ppermute | solution.py:80
  75.2 34.3 %collective-permute-start.2 = (bf16[144,1364]{1,0:T(8,128)(2,1)}, bf16[144,1364]{1,0:T(8,128)(2,1)S(1)}, u32[]{:S(2)}, u32[]{:S(2)}) collective-permute-start(bf16[144,1364]{1,0:T(8,128)(2,1)} %copy_after.2), channel_id=1, source_target_pairs={{0,1},{1,2},{2,3},{3,0},{4,5},{5,6},{6,7},{7,4},{8,9},{9,10},{10,1... | collective-permute-start | bytes 1178504 | tf_op jit(solution)/shard_map/ppermute | solution.py:80
  82.3 28.6 %copy-start.22 = (bf16[144,1364]{1,0:T(8,128)(2,1)}, bf16[144,1364]{1,0:T(8,128)(2,1)S(1)}, u32[]{:S(2)}) copy-start(bf16[144,1364]{1,0:T(8,128)(2,1)S(1)} %collective-permute-done.4.refs_3_) | copy-start | bytes 1178500
  114.2 140.7 %all-gather.11.cloned.1.call-start = ((), (), s32[]{:S(2)}) async-start(), calls=%async_computation.6 | async-start | bytes 11280384 | tf_op jit(solution)/shard_map/all_gather | solution.py:510
  114.3 29.2 %collective-permute-start.5 = (bf16[512,1152]{1,0:T(8,128)(2,1)}, bf16[512,1152]{1,0:T(8,128)(2,1)S(1)}, u32[]{:S(2)}, u32[]{:S(2)}) collective-permute-start(bf16[512,1152]{1,0:T(8,128)(2,1)} %after.26.x_ref), channel_id=1, source_target_pairs={{1,0},{2,1},{3,2},{5,4},{6,5},{7,6},{9,8},{10,9},{11,10},{13,12},{... | collective-permute-start | bytes 3538952 | tf_op jit(solution)/shard_map/ppermute | solution.py:452
  115.6 29.2 %collective-permute-start.6 = (bf16[512,1152]{1,0:T(8,128)(2,1)}, bf16[512,1152]{1,0:T(8,128)(2,1)S(1)}, u32[]{:S(2)}, u32[]{:S(2)}) collective-permute-start(bf16[512,1152]{1,0:T(8,128)(2,1)} %after.27.x_ref), channel_id=1, source_target_pairs={{0,1},{1,2},{2,3},{4,5},{5,6},{6,7},{8,9},{9,10},{10,11},{12,13},{... | collective-permute-start | bytes 3538952 | tf_op jit(solution)/shard_map/ppermute | solution.py:453
  121.5 161.9 %copy-start.55 = (f32[1152]{0:T(1024)}, f32[1152]{0:T(1024)S(1)}, u32[]{:S(2)}) copy-start(f32[1152]{0:T(1024)S(1)} %get-tuple-element.41) | copy-start | bytes 13828
  147.6 36.7 %collective-permute-start.9 = (bf16[144,1076]{1,0:T(8,128)(2,1)}, bf16[144,1076]{1,0:T(8,128)(2,1)S(1)}, u32[]{:S(2)}, u32[]{:S(2)}) collective-permute-start(bf16[144,1076]{1,0:T(8,128)(2,1)} %copy_after.3), channel_id=1, source_target_pairs={{0,3},{1,0},{2,1},{3,2},{4,7},{5,4},{6,5},{7,6},{8,11},{9,8},{10,9... | collective-permute-start | bytes 929672 | tf_op jit(solution)/shard_map/ppermute | solution.py:80
  151.3 33.7 %collective-permute-start.8 = (bf16[144,1076]{1,0:T(8,128)(2,1)}, bf16[144,1076]{1,0:T(8,128)(2,1)S(1)}, u32[]{:S(2)}, u32[]{:S(2)}) collective-permute-start(bf16[144,1076]{1,0:T(8,128)(2,1)} %copy_after.3), channel_id=1, source_target_pairs={{0,2},{1,3},{2,0},{3,1},{4,6},{5,7},{6,4},{7,5},{8,10},{9,11},{10,... | collective-permute-start | bytes 929672 | tf_op jit(solution)/shard_map/ppermute | solution.py:80
  151.4 34.3 %collective-permute-start.7 = (bf16[144,1076]{1,0:T(8,128)(2,1)}, bf16[144,1076]{1,0:T(8,128)(2,1)S(1)}, u32[]{:S(2)}, u32[]{:S(2)}) collective-permute-start(bf16[144,1076]{1,0:T(8,128)(2,1)} %copy_after.3), channel_id=1, source_target_pairs={{0,1},{1,2},{2,3},{3,0},{4,5},{5,6},{6,7},{7,4},{8,9},{9,10},{10,1... | collective-permute-start | bytes 929672 | tf_op jit(solution)/shard_map/ppermute | solution.py:80
  190.3 147.3 %reduce-scatter.5.cloned.1.call-start = ((), (), s32[]{:S(2)}) async-start(), calls=%async_computation.7 | async-start | bytes 11280384 | tf_op jit(solution)/shard_map/reduce_scatter | solution.py:536
  195.8 30.1 %copy-start.3 = (bf16[1,512,1152]{2,1,0:T(8,128)(2,1)S(1)}, bf16[1,512,1152]{2,1,0:T(8,128)(2,1)}, u32[]{:S(2)}) copy-start(bf16[1,512,1152]{2,1,0:T(8,128)(2,1)} %param.20) | copy-start | bytes 3538948
  230.1 66.3 %copy-start.10 = (f32[512,1152]{1,0:T(8,128)}, f32[512,1152]{1,0:T(8,128)S(1)}, u32[]{:S(2)}) copy-start(f32[512,1152]{1,0:T(8,128)S(1)} %get-tuple-element.107) | copy-start | bytes 7077892
  230.2 38.8 %copy-start.60 = (f32[512]{0:T(512)}, f32[512]{0:T(512)S(1)}, u32[]{:S(2)}) copy-start(f32[512]{0:T(512)S(1)} %broadcast_multiply_fusion.5) | copy-start | bytes 6148
  252.1 168.6 %reduce-scatter.9.cloned.1.call-start = ((), (), s32[]{:S(2)}) async-start(), calls=%async_computation.9 | async-start | bytes 11280384 | tf_op jit(solution)/shard_map/reduce_scatter | solution.py:549
  280.2 229.0 %reduce-scatter.7.cloned.1.call-start = ((), (), s32[]{:S(2)}) async-start(), calls=%async_computation.8 | async-start | bytes 11943936 | tf_op jit(solution)/shard_map/reduce_scatter | solution.py:640
  337.6 47.0 %slice-start.2 = ((s8[4718592]{0:T(1024)(128)(4,1)}), s8[4194304]{0:T(1024)(128)(4,1)S(1)}, s32[]{:S(2)}) async-start(s8[4718592]{0:T(1024)(128)(4,1)} %bitcast.144), calls=%async_computation.14 | async-start | bytes 8388608
  339.4 48.5 %collective-permute-start.12 = (bf16[144,1076]{1,0:T(8,128)(2,1)S(1)}, bf16[144,1076]{1,0:T(8,128)(2,1)S(1)}, u32[]{:S(2)}, u32[]{:S(2)}) collective-permute-start(bf16[144,1076]{1,0:T(8,128)(2,1)S(1)} %get-tuple-element.55), channel_id=1, source_target_pairs={{0,1},{1,2},{2,3},{3,0},{4,5},{5,6},{6,7},{7,4},{8,9},{9,10},{10,1... | collective-permute-start | bytes 929672 | tf_op jit(solution)/shard_map/ppermute | solution.py:593
  340.9 47.7 %collective-permute-start.11 = (bf16[144,1076]{1,0:T(8,128)(2,1)S(1)}, bf16[144,1076]{1,0:T(8,128)(2,1)S(1)}, u32[]{:S(2)}, u32[]{:S(2)}) collective-permute-start(bf16[144,1076]{1,0:T(8,128)(2,1)S(1)} %get-tuple-element.56), channel_id=1, source_target_pairs={{0,2},{1,3},{2,0},{3,1},{4,6},{5,7},{6,4},{7,5},{8,10},{9,11},{10,... | collective-permute-start | bytes 929672 | tf_op jit(solution)/shard_map/ppermute | solution.py:593
  343.3 46.0 %collective-permute-start.10 = (bf16[144,1076]{1,0:T(8,128)(2,1)S(1)}, bf16[144,1076]{1,0:T(8,128)(2,1)S(1)}, u32[]{:S(2)}, u32[]{:S(2)}) collective-permute-start(bf16[144,1076]{1,0:T(8,128)(2,1)S(1)} %get-tuple-element.57), channel_id=1, source_target_pairs={{0,3},{1,0},{2,1},{3,2},{4,7},{5,4},{6,5},{7,6},{8,11},{9,8},{10,9... | collective-permute-start | bytes 929672 | tf_op jit(solution)/shard_map/ppermute | solution.py:593
  344.8 39.8 %slice-start.3 = ((s8[4718592]{0:T(1024)(128)(4,1)}), s8[524288]{0:T(1024)(128)(4,1)S(1)}, s32[]{:S(2)}) async-start(s8[4718592]{0:T(1024)(128)(4,1)} %bitcast.144), calls=%async_computation.15 | async-start | bytes 1048576
  377.7 28.4 %collective-permute-start.14 = (bf16[512,1152]{1,0:T(8,128)(2,1)S(1)}, bf16[512,1152]{1,0:T(8,128)(2,1)S(1)}, u32[]{:S(2)}, u32[]{:S(2)}) collective-permute-start(bf16[512,1152]{1,0:T(8,128)(2,1)S(1)} %get-tuple-element.58.refs_2_), channel_id=1, source_target_pairs={{1,0},{2,1},{3,2},{5,4},{6,5},{7,6},{9,8},{10,9},{11,10},{13,12},{... | collective-permute-start | bytes 3538952 | tf_op jit(solution)/shard_map/ppermute | solution.py:629
  379.0 28.3 %collective-permute-start.13 = (bf16[512,1152]{1,0:T(8,128)(2,1)S(1)}, bf16[512,1152]{1,0:T(8,128)(2,1)}, u32[]{:S(2)}, u32[]{:S(2)}) collective-permute-start(bf16[512,1152]{1,0:T(8,128)(2,1)S(1)} %get-tuple-element.59.refs_1_), channel_id=1, source_target_pairs={{0,1},{1,2},{2,3},{4,5},{5,6},{6,7},{8,9},{9,10},{10,11},{12,13},{... | collective-permute-start | bytes 3538952 | tf_op jit(solution)/shard_map/ppermute | solution.py:628
  416.1 134.5 %reduce-scatter.11.cloned.1.call-start = ((), (), s32[]{:S(2)}) async-start(), calls=%async_computation.10 | async-start | bytes 1658880 | tf_op jit(solution)/shard_map/reduce_scatter | solution.py:705
  423.0 18.6 %collective-permute-start.16 = (bf16[144,1076]{1,0:T(8,128)(2,1)S(1)}, bf16[144,1076]{1,0:T(8,128)(2,1)S(1)}, u32[]{:S(2)}, u32[]{:S(2)}) collective-permute-start(bf16[144,1076]{1,0:T(8,128)(2,1)S(1)} %get-tuple-element.53), channel_id=1, source_target_pairs={{0,2},{1,3},{2,0},{3,1},{4,6},{5,7},{6,4},{7,5},{8,10},{9,11},{10,... | collective-permute-start | bytes 929672 | tf_op jit(solution)/shard_map/ppermute | solution.py:643
  425.4 17.0 %collective-permute-start.15 = (bf16[144,1076]{1,0:T(8,128)(2,1)S(1)}, bf16[144,1076]{1,0:T(8,128)(2,1)S(1)}, u32[]{:S(2)}, u32[]{:S(2)}) collective-permute-start(bf16[144,1076]{1,0:T(8,128)(2,1)S(1)} %get-tuple-element.54), channel_id=1, source_target_pairs={{0,3},{1,0},{2,1},{3,2},{4,7},{5,4},{6,5},{7,6},{8,11},{9,8},{10,9... | collective-permute-start | bytes 929672 | tf_op jit(solution)/shard_map/ppermute | solution.py:643
  435.0 42.9 %collective-permute-start.18 = (bf16[512,1152]{1,0:T(8,128)(2,1)S(1)}, bf16[512,1152]{1,0:T(8,128)(2,1)}, u32[]{:S(2)}, u32[]{:S(2)}) collective-permute-start(bf16[512,1152]{1,0:T(8,128)(2,1)S(1)} %add_convert_fusion.2.refs_1_), channel_id=1, source_target_pairs={{0,1},{1,2},{2,3},{4,5},{5,6},{6,7},{8,9},{9,10},{10,11},{12,13},{... | collective-permute-start | bytes 3538952 | tf_op jit(solution)/shard_map/ppermute | solution.py:658
  465.0 34.6 %collective-permute-start.19 = (bf16[512,1152]{1,0:T(8,128)(2,1)}, bf16[512,1152]{1,0:T(8,128)(2,1)}, u32[]{:S(2)}, u32[]{:S(2)}) collective-permute-start(bf16[512,1152]{1,0:T(8,128)(2,1)} %get-tuple-element.111), channel_id=1, source_target_pairs={{1,0},{2,1},{3,2},{5,4},{6,5},{7,6},{9,8},{10,9},{11,10},{13,12},{... | collective-permute-start | bytes 3538952 | tf_op jit(solution)/shard_map/ppermute | solution.py:664
  470.8 38.4 %collective-permute-start.17 = (bf16[144,1076]{1,0:T(8,128)(2,1)}, bf16[144,1076]{1,0:T(8,128)(2,1)}, u32[]{:S(2)}, u32[]{:S(2)}) collective-permute-start(bf16[144,1076]{1,0:T(8,128)(2,1)} %get-tuple-element.52), channel_id=1, source_target_pairs={{0,1},{1,2},{2,3},{3,0},{4,5},{5,6},{6,7},{7,4},{8,9},{9,10},{10,1... | collective-permute-start | bytes 929672 | tf_op jit(solution)/shard_map/ppermute | solution.py:643
  478.1 21.4 %copy-start.6 = (f32[512,1152]{1,0:T(8,128)S(1)}, f32[512,1152]{1,0:T(8,128)}, u32[]{:S(2)}) copy-start(f32[512,1152]{1,0:T(8,128)} %fusion.22.refs_1_) | copy-start | bytes 7077892
  478.1 21.4 %copy-start.51 = (f32[1152]{0:T(1024)S(1)}, f32[1152]{0:T(1024)}, u32[]{:S(2)}) copy-start(f32[1152]{0:T(1024)} %get-tuple-element.38) | copy-start | bytes 13828
  478.1 21.4 %copy-start.57 = (f32[512]{0:T(512)S(1)}, f32[512]{0:T(512)}, u32[]{:S(2)}) copy-start(f32[512]{0:T(512)} %copy-done.56) | copy-start | bytes 6148
  478.1 21.4 %copy-start.65 = (f32[512]{0:T(512)S(1)}, f32[512]{0:T(512)}, u32[]{:S(2)}) copy-start(f32[512]{0:T(512)} %add_rsqrt_fusion) | copy-start | bytes 6148
  512.1 4.4 collective-permute-start.20
  518.0 5.4 collective-permute-start.21
  524.3 1.3 collective-permute-start.22
  525.6 5.3 collective-permute-start.23
  530.9 13.3 %collective-permute-start.24 = (f32[13520]{0:T(1024)S(1)}, f32[13520]{0:T(1024)S(1)}, u32[]{:S(2)}, u32[]{:S(2)}) collective-permute-start(f32[13520]{0:T(1024)S(1)} %add.323), channel_id=1, source_target_pairs={{0,16},{4,20},{8,24},{12,28},{16,0},{20,4},{24,8},{28,12},{1,17},{... | collective-permute-start | bytes 162248 | tf_op jit(solution)/shard_map/ppermute | solution.py:693
  (74 other events, 354.4 us)
Sparse Core Ops, SparseCore 0:
  18.7 41.3 all-gather.12
  64.3 52.2 all-gather.6
  119.2 72.5 all-gather.8
  193.5 61.3 all-gather.10
  258.4 79.2 reduce-scatter.4
  341.5 79.1 reduce-scatter.8
  424.2 82.2 reduce-scatter.6
  519.4 31.1 reduce-scatter.10
